TPU v7x, 512 devices: a whole 4x4x16 slice. The times are simulated.
512 devices in a mesh: row: 16 (over z), col: 32 (over x, y, core).
Axes of the slice: x: 4, y: 4, z: 16, core: 2. Of those that a mesh axis runs over, the one named last changes fastest.
Arguments:
- tokens: bfloat16 [2048, 7168], P(('row', 'col')), may hold values from -6 to 6
- gate_up: bfloat16 [32, 2, 1536, 7168], P('col', None, 'row'), may hold values from -0.0625 to 0.0625
- down: bfloat16 [32, 1536, 7168], P('col', None, 'row'), may hold values from -0.15625 to 0.15625
- expert_ids: int32 [2048, 8], replicated, may hold values from 0 to 31, all different within a row; in each aligned block of 128 rows (0 to 127, 128 to 255, ...) at most 48 rows name the same one
- gate_weights: float32 [2048, 8], replicated, may hold values from 0.05 to 1
- capacity: int32 [32], replicated, may hold values from 24 to 48
Outputs:
- routed_out: bfloat16 [2048, 7168], P(('row', 'col'))
Inputs may be any that keep to these rules, and one draw needn't show every extreme that they name: `expert_ids`: each row names 8 different experts; within each aligned group of 128 rows no expert is named by more than 48 rows.
All inputs are finite; a program needn't handle non-finite values.
Results may differ from a plain program's by a relative error of at most 0.0063.
Values may be sent and summed in bfloat16 or wider, within the bound.
No kernel may reach another device: no remote copies, remote signals or barrier semaphores. Data moves between devices by JAX's collectives and lax.ppermute only.
A program may use at most 64 MiB of HBM per device.

v0:
```python
import jax
import jax.numpy as jnp
from jax import lax
from jax.sharding import PartitionSpec as P

TOP = 8


def expert_slots(expert_ids, gate_weights, capacity, expert, block_rows, slot_cap):
    total_rows = expert_ids.shape[0]
    member = expert_ids == expert
    hit_count = jnp.sum(member.astype(jnp.int32), axis=1)
    grouped = hit_count.reshape(total_rows // block_rows, block_rows)
    rank_in = (jnp.cumsum(grouped, axis=1) - grouped).reshape(total_rows)
    cap_here = lax.dynamic_index_in_dim(capacity, expert, 0, keepdims=False)
    usable = (hit_count > 0) & (rank_in < cap_here)
    weights = jnp.sum(jnp.where(member, gate_weights, 0.0), axis=1)
    groups = jnp.arange(total_rows, dtype=jnp.int32) // block_rows
    slot_ids = jnp.where(usable, groups * slot_cap + rank_in, -1)
    return (slot_ids, weights)


def local(tokens, gate_up, down, expert_ids, gate_weights, capacity):
    col_count = lax.axis_size("col")
    row_count = lax.axis_size("row")
    col_index = lax.axis_index("col")
    row_index = lax.axis_index("row")
    tok_dev = tokens.shape[0]
    block_rows = col_count * tok_dev
    slot_cap = min(3 * tok_dev * TOP // 2, block_rows)
    slot_count = row_count * slot_cap
    total_rows = expert_ids.shape[0]
    slot_ids, weights = expert_slots(
        expert_ids, gate_weights, capacity, col_index, block_rows, slot_cap
    )
    group_tokens = lax.all_gather(tokens, "col", axis=0, tiled=True)
    local_slots = (
        lax.dynamic_slice_in_dim(slot_ids, row_index * block_rows, block_rows)
        - row_index * slot_cap
    )
    cap_index = jnp.arange(slot_cap, dtype=jnp.int32)
    select = (cap_index[:, None] == local_slots[None, :]).astype(jnp.bfloat16)
    picked = jnp.dot(select, group_tokens, preferred_element_type=jnp.float32).astype(jnp.bfloat16)
    w_gate = gate_up[0, 0]
    w_up = gate_up[0, 1]
    contract = (((1,), (1,)), ((), ()))
    piece = lax.all_gather(picked, "row", axis=0, tiled=True)
    gate_part = lax.dot_general(piece, w_gate, contract, preferred_element_type=jnp.float32)
    up_part = lax.dot_general(piece, w_up, contract, preferred_element_type=jnp.float32)
    hidden = (jax.nn.silu(gate_part) * up_part).astype(jnp.bfloat16)
    w_down = down[0]
    outputs = jnp.dot(
        lax.all_gather(hidden, "row", axis=1, tiled=True),
        w_down,
        preferred_element_type=jnp.float32,
    ).astype(jnp.bfloat16)

    def by_column(values):
        return values.reshape(row_count, col_count, tok_dev).transpose(1, 0, 2).reshape(total_rows)

    column_slots = by_column(slot_ids)
    column_weights = by_column(weights)
    slot_index = jnp.arange(slot_count, dtype=jnp.int32)
    combine = jnp.where(
        column_slots[:, None] == slot_index[None, :], column_weights[:, None], 0.0
    ).astype(jnp.bfloat16)
    summed = lax.psum_scatter(
        jnp.dot(combine, outputs, preferred_element_type=jnp.float32),
        "col",
        scatter_dimension=0,
        tiled=True,
    )
    own_rows = lax.all_to_all(
        summed.astype(jnp.bfloat16), "row", split_axis=0, concat_axis=1, tiled=True
    ).astype(summed.dtype)
    return own_rows.astype(jnp.bfloat16)


def solution(mesh):
    in_specs = (
        P(("row", "col"), None),
        P("col", None, "row", None),
        P("col", None, "row"),
        P(),
        P(),
        P(),
    )
    out_specs = P(("row", "col"), None)
    return jax.shard_map(local, mesh=mesh, in_specs=in_specs, out_specs=out_specs, check_vma=False)
```

profile of v0, /device:TPU:1, one launch (start us, length us, event | category | flops | bytes accessed | tf_op | source)
XLA Modules:
  0.0 435.4 jit_solution(15671758591187416242)
XLA Ops:
  6.5 0.7 all-gather.9.cloned.1.call-update
  7.3 0.9 convert_reduce_fusion
  8.2 0.3 reduce_window_sum.15
  8.5 1.2 dynamic_slice.7
  9.7 0.7 fusion.31
  10.4 64.7 %all-gather.9.cloned.1.call-done = bf16[32,4,7168]{2,1,0:T(4,128)(2,1)} async-done(((bf16[1,4,7168]{2,1,0:T(4,128)(2,1)}), bf16[32,4,7168]{2,1,0:T(4,128)(2,1)}) %all-gather.9.cloned.1.call-update) | async-done | bytes 1835024 | tf_op jit(solution)/shard_map/all_gather | solution.py:36
  75.1 2.9 reshape.27
  78.0 1.2 convolution_convert_fusion
  79.4 131.3 %all-gather.5.cloned.1.call-done = bf16[768,7168]{1,0:T(8,128)(2,1)} async-done(((bf16[48,7168]{1,0:T(8,128)(2,1)}), bf16[768,7168]{1,0:T(8,128)(2,1)}) %all-gather.5.cloned.1.call-update) | async-done | bytes 11010064 | tf_op jit(solution)/shard_map/all_gather | solution.py:47
  210.7 8.1 %fusion.8 = f32[768,96]{0,1:T(8,128)S(1)} fusion(bf16[768,7168]{1,0:T(8,128)(2,1)} %all-gather.5.cloned.1.call-done, bf16[1,2,96,7168]{3,2,1,0:T(8,128)(2,1)} %param.7), kind=kOutput, calls=%fused_computation.11 | convolution fusion | flops 1056964608 | bytes 12681216 | tf_op jit(solution)/shard_map/dot_general | solution.py:48
  218.9 5.6 %fusion.18 = bf16[768,96]{0,1:T(8,128)(2,1)} fusion(bf16[768,7168]{1,0:T(8,128)(2,1)S(1)} %copy-done.2, bf16[1,2,96,7168]{3,2,1,0:T(8,128)(2,1)} %param.7, f32[768,96]{0,1:T(8,128)S(1)} %fusion.8), kind=kOutput, calls=%fused_computation.17 | convolution fusion | flops 1057406976 | bytes 12828672 | tf_op jit(solution)/shard_map/dot_general | solution.py:49
  224.6 0.3 reduce_sum.21
  224.9 0.3 reshape.25
  225.3 0.2 broadcast_in_dim.24
  225.5 0.3 copy.14
  225.8 0.9 fusion.27
  226.7 0.2 copy.15
  226.8 0.2 eq.36
  227.0 60.6 %all-gather.7.cloned.1.call-done = bf16[768,1536]{0,1:T(8,128)(2,1)} async-done(((bf16[768,96]{0,1:T(8,128)(2,1)}), bf16[768,1536]{0,1:T(8,128)(2,1)}) %all-gather.7.cloned.1.call-update) | async-done | bytes 2359312 | tf_op jit(solution)/shard_map/all_gather | solution.py:53
  287.6 6.7 %fusion = f32[2048,448]{1,0:T(8,128)} fusion(bf16[2048]{0:T(1024)(128)(2,1)S(1)} %broadcast_in_dim.24, s32[2048]{0:T(1024)S(1)} %eq.36, bf16[768,1536]{0,1:T(8,128)(2,1)} %all-gather.7.cloned.1.call-done, bf16[1,1536,448]{1,2,0:T(8,128)(2,1)S(1)} %copy-done), kind=kOutput, calls=%fused_computation.3 | convolution fusion | flops 2469740544 | bytes 7417856 | tf_op jit(solution)/shard_map/dot_general | solution.py:68
  294.3 109.4 %reduce-scatter.2.cloned.1.call-done = f32[64,448]{1,0:T(8,128)} async-done(((f32[2048,448]{1,0:T(8,128)}), f32[64,448]{1,0:T(8,128)}) %reduce-scatter.2.cloned.1.call-update) | async-done | bytes 114704 | tf_op jit(solution)/shard_map/reduce_scatter | solution.py:67
  403.7 0.9 convert_element_type.26
  404.7 23.4 %all_to_all.19 = bf16[16,4,448]{2,1,0:T(4,128)(2,1)S(1)} all-to-all(bf16[16,4,448]{2,1,0:T(4,128)(2,1)S(1)} %all_to_all.14), channel_id=1, replica_groups=mesh['row'=16,'col'=32] {'row'}, dimensions={0} | all-to-all | bytes 114688 | tf_op jit(solution)/shard_map/all_to_all | solution.py:73
  428.1 0.8 all_to_all.17
  (19 shorter events, 0.4 us)
Async XLA Ops:
  6.5 281.1 %copy-start = (bf16[1,1536,448]{1,2,0:T(8,128)(2,1)S(1)}, bf16[1,1536,448]{1,2,0:T(8,128)(2,1)}, u32[]{:S(2)}) copy-start(bf16[1,1536,448]{1,2,0:T(8,128)(2,1)} %param.8) | copy-start | bytes 4128772
  6.5 68.6 %all-gather.9.cloned.1.call-start = ((), (), s32[]{:S(2)}) async-start(), calls=%async_computation.5 | async-start | bytes 1892352 | tf_op jit(solution)/shard_map/all_gather | solution.py:36
  7.3 203.4 %all-gather.5.cloned.1.call-start = ((), (), s32[]{:S(2)}) async-start(), calls=%async_computation.2 | async-start | bytes 11698176 | tf_op jit(solution)/shard_map/all_gather | solution.py:47
  79.3 208.3 %all-gather.7.cloned.1.call-start = ((), (), s32[]{:S(2)}) async-start(), calls=%async_computation.3 | async-start | bytes 2506752 | tf_op jit(solution)/shard_map/all_gather | solution.py:53
  210.7 8.1 %copy-start.2 = (bf16[768,7168]{1,0:T(8,128)(2,1)S(1)}, bf16[768,7168]{1,0:T(8,128)(2,1)}, u32[]{:S(2)}) copy-start(bf16[768,7168]{1,0:T(8,128)(2,1)} %all-gather.5.cloned.1.call-done) | copy-start | bytes 33030148
  218.8 6.0 %copy-start.1 = (f32[2048,8]{0,1:T(8,128)S(1)}, f32[2048,8]{0,1:T(8,128)}, u32[]{:S(2)}) copy-start(f32[2048,8]{0,1:T(8,128)} %param.10) | copy-start | bytes 196612
  224.5 179.3 %reduce-scatter.2.cloned.1.call-start = ((), (), s32[]{:S(2)}) async-start(), calls=%async_computation.4 | async-start | bytes 4325376 | tf_op jit(solution)/shard_map/reduce_scatter | solution.py:67
Sparse Core Ops, SparseCore 0:
  10.5 64.5 all-gather.8
  79.4 131.2 all-gather.4
  224.6 62.9 all-gather.6
  294.5 109.2 reduce-scatter.1
where the time goes:
time: 438 us; the launch traced here: 435 us
  waiting for transfers between devices  367 us (84%)
  blocking collectives  23.4 us (5%)
  matrix products  21.7 us (5%)
  between operations  13.2 us (3%)
  local copies, waits for them, and re-layouts  6.54 us (1%)
    all_gather x1, waiting for transfers between devices, local(): piece = lax.all_gather(picked, 'row', axis=0, tiled=True)  131 us
    reduce_scatter x1, waiting for transfers between devices, local(): lax.psum_scatter(jnp.dot(combine, outputs, preferred_element_type=jnp.flo...  109 us
    all_gather x1, waiting for transfers between devices, local(): group_tokens = lax.all_gather(tokens, 'col', axis=0, tiled=True)  64.7 us
    all_gather x1, waiting for transfers between devices, local(): lax.all_gather(hidden, 'row', axis=1, tiled=True)  60.6 us
    all_to_all x1, blocking collectives, local(): lax.all_to_all(summed.astype(jnp.bfloat16), 'row', split_axis=0, concat_a...  23.4 us
  transfers between devices with their start and end apart: 4, of which 4 were waited for; matrix products, arithmetic and copies ran while one was open for 1% of the time, Pallas kernels for 0%

commit v1 on v0

v1 whole, which is shorter than its diff:
```python
import jax
import jax.numpy as jnp
from jax import lax
from jax.sharding import Mesh, PartitionSpec as P

PARTS = (6, 5, 5)
SLOTS = 48
PLANE = ("x", "y")
PAIR = [(0, 1), (1, 0)]


def routing(expert_ids, gate_weights, capacity, expert, groups, group_rows):
    member = expert_ids == expert
    hits = jnp.sum(member.astype(jnp.int32), axis=1).reshape(groups, group_rows)
    rank = jnp.cumsum(hits, axis=1) - hits
    cap = lax.dynamic_index_in_dim(capacity, expert, 0, keepdims=False)
    weights = jnp.sum(jnp.where(member, gate_weights, 0.0), axis=1)
    slots = jnp.where((hits > 0) & (rank < cap), rank, -1)
    return slots, weights.reshape(groups, group_rows)


def local(tokens, gate_up, down, expert_ids, gate_weights, capacity):
    core = lax.axis_index("c")
    plane_index = lax.axis_index(PLANE)
    chips = lax.axis_size("x") * lax.axis_size("y")
    groups = lax.axis_size("z")
    own, width = tokens.shape
    half = width // 2
    pair = 2 * own
    group_rows = chips * pair
    mine, other = core * half, (1 - core) * half

    def half_of(array, start):
        return lax.dynamic_slice_in_dim(array, start, half, axis=array.ndim - 1)

    kept = half_of(tokens, mine)
    got = lax.ppermute(half_of(tokens, other), "c", PAIR)
    first = core == 0
    pair_tokens = jnp.concatenate(
        [jnp.where(first, kept, got), jnp.where(first, got, kept)], axis=0
    )
    line = lax.all_gather(pair_tokens, "z", axis=0, tiled=False)

    units = 2 * gate_up.shape[2]
    weights_all = gate_up[0].reshape(units, width)
    w_mine = half_of(weights_all, mine)
    w_other = lax.ppermute(half_of(weights_all, other), "c", PAIR)
    w_down = down[0]

    slots, route = routing(
        expert_ids, gate_weights, capacity, plane_index * 2 + core, groups, group_rows
    )

    gathered = []
    start = 0
    for count in PARTS:
        piece = line[start : start + count].reshape(count * pair, half)
        gathered.append(lax.all_gather(piece, PLANE, axis=0, tiled=True))
        start += count

    rows_out = []
    start = 0
    contract = (((1,), (1,)), ((), ()))
    for count, part in zip(PARTS, gathered):
        ours = lax.dot_general(part, w_mine, contract, preferred_element_type=jnp.float32)
        theirs = lax.dot_general(part, w_other, contract, preferred_element_type=jnp.float32)
        both = ours + lax.ppermute(theirs, "c", PAIR)
        hidden = (jax.nn.silu(both[:, : units // 2]) * both[:, units // 2 :]).astype(jnp.bfloat16)
        rows = count * group_rows
        n_slots = count * SLOTS
        offset = jnp.arange(count, dtype=jnp.int32)[:, None] * SLOTS
        slot_of = slots[start : start + count]
        slot_of = jnp.where(slot_of >= 0, slot_of + offset, -1).reshape(count, chips, pair)
        route_of = route[start : start + count].reshape(count, chips, pair)
        by_row = slot_of.transpose(1, 0, 2).reshape(rows)
        slot_index = jnp.arange(n_slots, dtype=jnp.int32)
        select = (by_row[:, None] == slot_index[None, :]).astype(jnp.bfloat16)
        picked = lax.dot_general(
            hidden, select, (((0,), (0,)), ((), ())), preferred_element_type=jnp.float32
        ).astype(jnp.bfloat16)
        all_hidden = lax.all_gather(picked, "z", axis=0, tiled=True)
        outputs = lax.dot_general(
            all_hidden, w_down, (((0,), (0,)), ((), ())), preferred_element_type=jnp.float32
        ).astype(jnp.bfloat16)

        def by_target(values):
            return values.reshape(count, chips, 2, own).transpose(2, 1, 0, 3).reshape(rows)

        to_slot, to_weight = by_target(slot_of), by_target(route_of)
        combine = jnp.where(
            to_slot[:, None] == slot_index[None, :], to_weight[:, None], 0.0
        ).astype(jnp.bfloat16)
        summed = jnp.dot(combine, outputs, preferred_element_type=jnp.float32)
        summed = summed.reshape(2, rows // 2, summed.shape[1])
        keep = lax.dynamic_index_in_dim(summed, core, 0, keepdims=False)
        give = lax.dynamic_index_in_dim(summed, 1 - core, 0, keepdims=False)
        chip_sum = (keep + lax.ppermute(give, "c", PAIR)).astype(jnp.bfloat16)
        arrived = lax.all_to_all(chip_sum, PLANE, split_axis=0, concat_axis=0, tiled=True)
        arrived = arrived.reshape(chips, count, own, arrived.shape[1]).astype(jnp.float32)
        rows_out.append(jnp.sum(arrived, axis=0).astype(jnp.bfloat16))
        start += count

    own_rows = jnp.concatenate(rows_out, axis=0)
    own_rows = lax.all_to_all(own_rows, "z", split_axis=0, concat_axis=0, tiled=True)
    return own_rows.transpose(1, 0, 2).reshape(own, width)


def solution(mesh):
    rows, cols = mesh.devices.shape
    side = 4
    fine = Mesh(mesh.devices.reshape(rows, side, cols // (2 * side), 2), ("z", "x", "y", "c"))
    col = ("x", "y", "c")
    in_specs = (
        P(("z",) + col, None),
        P(col, None, "z", None),
        P(col, None, "z"),
        P(),
        P(),
        P(),
    )
    out_specs = P(("z",) + col, None)
    return jax.shard_map(local, mesh=fine, in_specs=in_specs, out_specs=out_specs, check_vma=False)
```

time: 438 us -> 419 us (0.957)
  waiting for transfers between devices: 367 us -> 132 us
  blocking collectives: 23.4 us -> 135 us
  starting transfers between devices: 0.13 us -> 60.8 us
  local copies, waits for them, and re-layouts: 6.54 us -> 29.3 us
  matrix products: 21.7 us -> 33.9 us
  other arithmetic: 3.7 us -> 10 us
    all_gather x3, waiting for transfers between devices: 257 us -> 116 us  [local(): gathered.append(lax.all_gather(piece, PLANE, axis=0, tiled=True))]
    all_gather x0 -> x4, blocking collectives: none -> 116 us  [the longest x3 87 us: local(): all_hidden = lax.all_gather(picked, 'z', axis=0, tiled=True)]
    reduce_scatter x1 -> x0, waiting for transfers between devices: 109 us -> none  [local(): lax.psum_scatter(jnp.dot(combine, outputs, preferred_element_type=jnp.flo...]
    ppermute x0 -> x8, starting transfers between devices: none -> 48.5 us  [the longest x3 19.3 us: local(): chip_sum = (keep + lax.ppermute(give, 'c', PAIR)).astype(jnp.bfloat16)]
    all_to_all x0 -> x3, waiting for transfers between devices: none -> 14.4 us  [local(): lax.all_to_all(chip_sum, PLANE, split_axis=0, concat_axis=0, tiled=True)]
    dot_general x4 -> x12, matrix products: 21.7 us -> 33.9 us  [the longest x3 15.4 us: local(): lax.dot_general(part, w_other, contract, preferred_element_type=jnp.float32)]
    all_to_all x0 -> x3, starting transfers between devices: none -> 12.2 us  [local(): lax.all_to_all(chip_sum, PLANE, split_axis=0, concat_axis=0, tiled=True)]
    dynamic_slice x1 -> x5, local copies, waits for them, and re-layouts: 1.24 us -> 8.87 us  [the longest x2 6.2 us: local(): keep = lax.dynamic_index_in_dim(summed, core, 0, keepdims=False)]
  transfers between devices with their start and end apart: 4 -> 14, of which waited for: 4 -> 6; matrix products, arithmetic and copies ran while one was open for 1% -> 16% of each run, Pallas kernels for 0% -> 0%
where the time goes in v1:
time: 419 us; the launch traced here: 414 us
  blocking collectives  135 us (32%)
  waiting for transfers between devices  132 us (32%)
  starting transfers between devices  60.8 us (15%)
  matrix products  33.9 us (8%)
  local copies, waits for them, and re-layouts  29.3 us (7%)
  between operations  13.7 us (3%)
  other arithmetic  10 us (2%)
    all_gather x3, waiting for transfers between devices, local(): gathered.append(lax.all_gather(piece, PLANE, axis=0, tiled=True))  116 us
    all_gather x3, blocking collectives, local(): all_hidden = lax.all_gather(picked, 'z', axis=0, tiled=True)  87 us
    all_gather x1, blocking collectives, local(): line = lax.all_gather(pair_tokens, 'z', axis=0, tiled=False)  28.8 us
    ppermute x3, starting transfers between devices, local(): chip_sum = (keep + lax.ppermute(give, 'c', PAIR)).astype(jnp.bfloat16)  19.3 us
    all_to_all x1, blocking collectives, local(): lax.all_to_all(own_rows, 'z', split_axis=0, concat_axis=0, tiled=True)  19 us
    dot_general x3, matrix products, local(): lax.dot_general(part, w_other, contract, preferred_element_type=jnp.float32)  15.4 us
    all_to_all x3, waiting for transfers between devices, local(): lax.all_to_all(chip_sum, PLANE, split_axis=0, concat_axis=0, tiled=True)  14.4 us
    all_to_all x3, starting transfers between devices, local(): lax.all_to_all(chip_sum, PLANE, split_axis=0, concat_axis=0, tiled=True)  12.2 us
  transfers between devices with their start and end apart: 14, of which 6 were waited for; matrix products, arithmetic and copies ran while one was open for 16% of the time, Pallas kernels for 0%

profile of v1, /device:TPU:1, one launch (start us, length us, event | category | flops | bytes accessed | tf_op | source)
XLA Modules:
  0.0 414.5 jit_solution(13217734029825779971)
XLA Ops:
  7.5 8.8 %collective-permute-start = (bf16[4,3584]{1,0:T(4,128)(2,1)S(1)}, bf16[4,3584]{1,0:T(4,128)(2,1)S(1)}, u32[]{:S(2)}, u32[]{:S(2)}) collective-permute-start(bf16[4,3584]{1,0:T(4,128)(2,1)S(1)} %constant_dynamic-slice_fusion.3), channel_id=1, source_target_pairs={{0,1},{1,0},{2,3},{3,2},{4,5},{5,4},{6,7},{7,6},{8,9},{9,8},{10,11... | collective-permute-start | bytes 86024 | tf_op jit(solution)/shard_map/ppermute | solution.py:37
  17.9 28.8 %all-gather = bf16[128,3584]{1,0:T(8,128)(2,1)S(1)} all-gather(bf16[8,3584]{1,0:T(8,128)(2,1)S(1)} %pad_maximum_fusion.1), channel_id=2, replica_groups=mesh['z'=16,'x'=4,'y'=4,'c'=2] {'z'}, dimensions={0}, use_global_device_ids=true | all-gather | bytes 974848 | tf_op jit(solution)/shard_map/all_gather | solution.py:42
  52.3 8.7 %collective-permute-start.1 = (bf16[192,3584]{1,0:T(8,128)(2,1)}, bf16[192,3584]{1,0:T(8,128)(2,1)}, u32[]{:S(2)}, u32[]{:S(2)}) collective-permute-start(bf16[192,3584]{1,0:T(8,128)(2,1)} %constant_dynamic-slice_fusion.2), channel_id=1, source_target_pairs={{0,1},{1,0},{2,3},{3,2},{4,5},{5,4},{6,7},{7,6},{8,9},{9,8},{10,11... | collective-permute-start | bytes 4128776 | tf_op jit(solution)/shard_map/ppermute | solution.py:47
  67.7 52.1 %all-gather.9.cloned.1.call-done = bf16[640,3584]{1,0:T(8,128)(2,1)} async-done(((bf16[40,3584]{1,0:T(8,128)(2,1)}), bf16[640,3584]{1,0:T(8,128)(2,1)}) %all-gather.9.cloned.1.call-update) | async-done | bytes 4587536 | tf_op jit(solution)/shard_map/all_gather | solution.py:58
  119.8 5.1 %fusion.66 = f32[640,192]{0,1:T(8,128)} fusion(bf16[640,3584]{1,0:T(8,128)(2,1)} %all-gather.9.cloned.1.call-done, bf16[192,3584]{1,0:T(8,128)(2,1)} %collective-permute-done.1), kind=kOutput, calls=%fused_computation.88 | convolution fusion | flops 880803840 | bytes 6455296 | tf_op jit(solution)/shard_map/dot_general | solution.py:66
  127.5 63.9 %all-gather.7.cloned.1.call-done = bf16[640,3584]{1,0:T(8,128)(2,1)} async-done(((bf16[40,3584]{1,0:T(8,128)(2,1)}), bf16[640,3584]{1,0:T(8,128)(2,1)}) %all-gather.7.cloned.1.call-update) | async-done | bytes 4587536 | tf_op jit(solution)/shard_map/all_gather | solution.py:58
  191.4 5.3 %fusion.65 = f32[640,192]{0,1:T(8,128)} fusion(bf16[640,3584]{1,0:T(8,128)(2,1)} %all-gather.7.cloned.1.call-done, bf16[192,3584]{1,0:T(8,128)(2,1)} %collective-permute-done.1), kind=kOutput, calls=%fused_computation.87 | convolution fusion | flops 880803840 | bytes 6455296 | tf_op jit(solution)/shard_map/dot_general | solution.py:66
  204.1 29.1 %all_gather.31 = bf16[1536,240]{1,0:T(8,128)(2,1)S(1)} all-gather(bf16[96,240]{1,0:T(8,128)(2,1)S(1)} %convolution_convert_fusion), channel_id=1, replica_groups=mesh['z'=16,'x'=4,'y'=4,'c'=2] {'z'}, dimensions={0}, use_global_device_ids=true | all-gather | bytes 783360 | tf_op jit(solution)/shard_map/all_gather | solution.py:81
  233.2 3.5 fusion.23
  238.8 8.0 %collective-permute-start.7 = (f32[320,448]{1,0:T(8,128)}, f32[320,448]{1,0:T(8,128)}, u32[]{:S(2)}, u32[]{:S(2)}) collective-permute-start(f32[320,448]{1,0:T(8,128)} %dynamic-slice_bitcast_fusion), channel_id=1, source_target_pairs={{0,1},{1,0},{2,3},{3,2},{4,5},{5,4},{6,7},{7,6},{8,9},{9,8},{10,11... | collective-permute-start | bytes 1720328 | tf_op jit(solution)/shard_map/ppermute | solution.py:97
  248.2 26.9 %all_gather.29 = bf16[1536,240]{1,0:T(8,128)(2,1)S(1)} all-gather(bf16[96,240]{1,0:T(8,128)(2,1)S(1)} %convolution_convert_fusion.1), channel_id=1, replica_groups=mesh['z'=16,'x'=4,'y'=4,'c'=2] {'z'}, dimensions={0}, use_global_device_ids=true | all-gather | bytes 783360 | tf_op jit(solution)/shard_map/all_gather | solution.py:81
  275.2 3.5 fusion.20
  278.7 5.0 %fusion.64 = f32[768,192]{0,1:T(8,128)S(1)} fusion(bf16[768,3584]{1,0:T(8,128)(2,1)} %all-gather.5.cloned.1.call-done, bf16[192,3584]{1,0:T(8,128)(2,1)} %collective-permute-done.1), kind=kOutput, calls=%fused_computation.86 | convolution fusion | flops 1056964608 | bytes 7471104 | tf_op jit(solution)/shard_map/dot_general | solution.py:66
  283.7 6.3 %collective-permute-start.2 = (f32[768,192]{0,1:T(8,128)S(1)}, f32[768,192]{0,1:T(8,128)S(1)}, u32[]{:S(2)}, u32[]{:S(2)}) collective-permute-start(f32[768,192]{0,1:T(8,128)S(1)} %fusion.64), channel_id=1, source_target_pairs={{0,1},{1,0},{2,3},{3,2},{4,5},{5,4},{6,7},{7,6},{8,9},{9,8},{10,11... | collective-permute-start | bytes 1769480 | tf_op jit(solution)/shard_map/ppermute | solution.py:67
  295.9 30.9 %all_gather.27 = bf16[1536,288]{1,0:T(8,128)(2,1)} all-gather(bf16[96,288]{1,0:T(8,128)(2,1)S(1)} %fusion.25), channel_id=1, replica_groups=mesh['z'=16,'x'=4,'y'=4,'c'=2] {'z'}, dimensions={0}, use_global_device_ids=true | all-gather | bytes 940032 | tf_op jit(solution)/shard_map/all_gather | solution.py:81
  326.8 4.3 %fusion.17 = f32[768,448]{0,1:T(8,128)} fusion(bf16[1536,288]{1,0:T(8,128)(2,1)} %all_gather.27, bf16[1,1536,448]{1,2,0:T(8,128)(2,1)} %param.8, bf16[768]{0:T(1024)(128)(2,1)S(1)} %copy-done.10, s32[768]{0:T(1024)S(1)} %copy-done.8), kind=kOutput, calls=%fused_computation.13 | convolution fusion | flops 595113984 | bytes 3641856 | tf_op jit(solution)/shard_map/dot_general | solution.py:93
  334.0 4.0 constant_dynamic-slice_fusion.1
  339.0 9.5 %collective-permute-start.3 = (f32[384,448]{0,1:T(8,128)}, f32[384,448]{0,1:T(8,128)}, u32[]{:S(2)}, u32[]{:S(2)}) collective-permute-start(f32[384,448]{0,1:T(8,128)} %bitcast.68), channel_id=1, source_target_pairs={{0,1},{1,0},{2,3},{3,2},{4,5},{5,4},{6,7},{7,6},{8,9},{9,8},{10,11... | collective-permute-start | bytes 2064392 | tf_op jit(solution)/shard_map/ppermute | solution.py:97
  350.5 4.4 %all-to-all-start.2 = ((bf16[16,20,448]{2,1,0:T(8,128)(2,1)}), bf16[16,20,448]{2,1,0:T(8,128)(2,1)}, u32[]{:S(2)}, u32[]{:S(2)}) async-start(bf16[16,20,448]{2,1,0:T(8,128)(2,1)} %all_to_all.25), calls=%async_computation.2 | async-start | bytes 786432 | tf_op jit(solution)/shard_map/all_to_all | solution.py:98
  364.1 4.2 %all-to-all-start.1 = ((bf16[16,20,448]{2,1,0:T(8,128)(2,1)}), bf16[16,20,448]{2,1,0:T(8,128)(2,1)}, u32[]{:S(2)}, u32[]{:S(2)}) async-start(bf16[16,20,448]{2,1,0:T(8,128)(2,1)} %all_to_all.23), calls=%async_computation.1 | async-start | bytes 786432 | tf_op jit(solution)/shard_map/all_to_all | solution.py:98
  370.3 6.1 %all-to-all-done.1 = bf16[16,20,448]{2,1,0:T(8,128)(2,1)} async-done(((bf16[16,20,448]{2,1,0:T(8,128)(2,1)}), bf16[16,20,448]{2,1,0:T(8,128)(2,1)}, u32[]{:S(2)}, u32[]{:S(2)}) %all-to-all-start.1) | async-done | bytes 286752 | tf_op jit(solution)/shard_map/all_to_all | solution.py:98
  376.4 3.6 all-to-all-start
  382.2 5.8 %all-to-all-done = bf16[16,24,448]{2,1,0:T(8,128)(2,1)S(1)} async-done(((bf16[16,24,448]{2,1,0:T(8,128)(2,1)}), bf16[16,24,448]{2,1,0:T(8,128)(2,1)S(1)}, u32[]{:S(2)}, u32[]{:S(2)}) %all-to-all-start) | async-done | bytes 344096 | tf_op jit(solution)/shard_map/all_to_all | solution.py:98
  388.1 19.0 %all_to_all.32 = bf16[16,4,448]{2,1,0:T(4,128)(2,1)S(1)} all-to-all(bf16[16,4,448]{2,1,0:T(4,128)(2,1)S(1)} %pad_maximum_fusion), channel_id=1, replica_groups=mesh['z'=16,'x'=4,'y'=4,'c'=2] {'z'}, dimensions={0} | all-to-all | bytes 114688 | tf_op jit(solution)/shard_map/all_to_all | solution.py:104
  (122 shorter events, 53.9 us)
Async XLA Ops:
  6.5 44.6 %copy-start = (bf16[1,2,96,7168]{3,2,1,0:T(8,128)(2,1)S(1)}, bf16[1,2,96,7168]{3,2,1,0:T(8,128)(2,1)}, u32[]{:S(2)}) copy-start(bf16[1,2,96,7168]{3,2,1,0:T(8,128)(2,1)} %param.7) | copy-start | bytes 8257540
  6.5 113.3 %all-gather.9.cloned.1.call-start = ((), (), s32[]{:S(2)}) async-start(), calls=%async_computation.6 | async-start | bytes 4874240 | tf_op jit(solution)/shard_map/all_gather | solution.py:58
  7.5 9.6 %collective-permute-start = (bf16[4,3584]{1,0:T(4,128)(2,1)S(1)}, bf16[4,3584]{1,0:T(4,128)(2,1)S(1)}, u32[]{:S(2)}, u32[]{:S(2)}) collective-permute-start(bf16[4,3584]{1,0:T(4,128)(2,1)S(1)} %constant_dynamic-slice_fusion.3), channel_id=1, source_target_pairs={{0,1},{1,0},{2,3},{3,2},{4,5},{5,4},{6,7},{7,6},{8,9},{9,8},{10,11... | collective-permute-start | bytes 86024 | tf_op jit(solution)/shard_map/ppermute | solution.py:37
  48.5 142.9 %all-gather.7.cloned.1.call-start = ((), (), s32[]{:S(2)}) async-start(), calls=%async_computation.5 | async-start | bytes 4874240 | tf_op jit(solution)/shard_map/all_gather | solution.py:58
  49.3 229.4 %all-gather.5.cloned.1.call-start = ((), (), s32[]{:S(2)}) async-start(), calls=%async_computation.4 | async-start | bytes 5849088 | tf_op jit(solution)/shard_map/all_gather | solution.py:58
  51.1 10.0 %copy-start.5 = (f32[2048,8]{0,1:T(8,128)S(1)}, f32[2048,8]{0,1:T(8,128)}, u32[]{:S(2)}) copy-start(f32[2048,8]{0,1:T(8,128)} %param.10) | copy-start | bytes 196612
  51.1 10.3 %copy-start.14 = (s32[32]{0:T(128)S(1)}, s32[32]{0:T(128)}, u32[]{:S(2)}) copy-start(s32[32]{0:T(128)} %param.11) | copy-start | bytes 388
  52.3 15.4 %collective-permute-start.1 = (bf16[192,3584]{1,0:T(8,128)(2,1)}, bf16[192,3584]{1,0:T(8,128)(2,1)}, u32[]{:S(2)}, u32[]{:S(2)}) collective-permute-start(bf16[192,3584]{1,0:T(8,128)(2,1)} %constant_dynamic-slice_fusion.2), channel_id=1, source_target_pairs={{0,1},{1,0},{2,3},{3,2},{4,5},{5,4},{6,7},{7,6},{8,9},{9,8},{10,11... | collective-permute-start | bytes 4128776 | tf_op jit(solution)/shard_map/ppermute | solution.py:47
  124.9 78.7 %collective-permute-start.6 = (f32[640,192]{0,1:T(8,128)}, f32[640,192]{0,1:T(8,128)S(1)}, u32[]{:S(2)}, u32[]{:S(2)}) collective-permute-start(f32[640,192]{0,1:T(8,128)} %fusion.66), channel_id=1, source_target_pairs={{0,1},{1,0},{2,3},{3,2},{4,5},{5,4},{6,7},{7,6},{8,9},{9,8},{10,11... | collective-permute-start | bytes 1474568 | tf_op jit(solution)/shard_map/ppermute | solution.py:67
  196.7 50.1 %collective-permute-start.4 = (f32[640,192]{0,1:T(8,128)}, f32[640,192]{0,1:T(8,128)}, u32[]{:S(2)}, u32[]{:S(2)}) collective-permute-start(f32[640,192]{0,1:T(8,128)} %fusion.65), channel_id=1, source_target_pairs={{0,1},{1,0},{2,3},{3,2},{4,5},{5,4},{6,7},{7,6},{8,9},{9,8},{10,11... | collective-permute-start | bytes 1474568 | tf_op jit(solution)/shard_map/ppermute | solution.py:67
  236.7 10.1 %copy-start.4 = (f32[640,192]{0,1:T(8,128)S(1)}, f32[640,192]{0,1:T(8,128)}, u32[]{:S(2)}) copy-start(f32[640,192]{0,1:T(8,128)} %fusion.28) | copy-start | bytes 1474564
  236.7 11.1 %copy-start.9 = (s32[640]{0:T(1024)S(1)}, s32[640]{0:T(1024)}, u32[]{:S(2)}) copy-start(s32[640]{0:T(1024)} %eq.114) | copy-start | bytes 7684
  238.8 109.6 %collective-permute-start.7 = (f32[320,448]{1,0:T(8,128)}, f32[320,448]{1,0:T(8,128)}, u32[]{:S(2)}, u32[]{:S(2)}) collective-permute-start(f32[320,448]{1,0:T(8,128)} %dynamic-slice_bitcast_fusion), channel_id=1, source_target_pairs={{0,1},{1,0},{2,3},{3,2},{4,5},{5,4},{6,7},{7,6},{8,9},{9,8},{10,11... | collective-permute-start | bytes 1720328 | tf_op jit(solution)/shard_map/ppermute | solution.py:97
  278.7 11.3 %copy-start.2 = (f32[640,448]{1,0:T(8,128)S(1)}, f32[640,448]{1,0:T(8,128)}, u32[]{:S(2)}) copy-start(f32[640,448]{1,0:T(8,128)} %fusion.20) | copy-start | bytes 3440644
  278.7 14.1 %copy-start.11 = (bf16[768,3584]{1,0:T(8,128)(2,1)S(1)}, bf16[768,3584]{1,0:T(8,128)(2,1)}, u32[]{:S(2)}) copy-start(bf16[768,3584]{1,0:T(8,128)(2,1)} %all-gather.5.cloned.1.call-done) | copy-start | bytes 16515076
  283.7 11.0 %collective-permute-start.2 = (f32[768,192]{0,1:T(8,128)S(1)}, f32[768,192]{0,1:T(8,128)S(1)}, u32[]{:S(2)}, u32[]{:S(2)}) collective-permute-start(f32[768,192]{0,1:T(8,128)S(1)} %fusion.64), channel_id=1, source_target_pairs={{0,1},{1,0},{2,3},{3,2},{4,5},{5,4},{6,7},{7,6},{8,9},{9,8},{10,11... | collective-permute-start | bytes 1769480 | tf_op jit(solution)/shard_map/ppermute | solution.py:67
  290.9 64.0 %collective-permute-start.5 = (f32[320,448]{1,0:T(8,128)}, f32[320,448]{1,0:T(8,128)}, u32[]{:S(2)}, u32[]{:S(2)}) collective-permute-start(f32[320,448]{1,0:T(8,128)} %dynamic-slice_bitcast_fusion.1), channel_id=1, source_target_pairs={{0,1},{1,0},{2,3},{3,2},{4,5},{5,4},{6,7},{7,6},{8,9},{9,8},{10,11... | collective-permute-start | bytes 1720328 | tf_op jit(solution)/shard_map/ppermute | solution.py:97
  295.4 31.3 %copy-start.8 = (s32[768]{0:T(1024)S(1)}, s32[768]{0:T(1024)}, u32[]{:S(2)}) copy-start(s32[768]{0:T(1024)} %eq.101) | copy-start | bytes 9220
  295.4 31.3 %copy-start.10 = (bf16[768]{0:T(1024)(128)(2,1)S(1)}, bf16[768]{0:T(1024)(128)(2,1)}, u32[]{:S(2)}) copy-start(bf16[768]{0:T(1024)(128)(2,1)} %broadcast_in_dim.65) | copy-start | bytes 4612
  338.1 10.4 %copy-start.1 = (f32[640,448]{1,0:T(8,128)S(1)}, f32[640,448]{1,0:T(8,128)}, u32[]{:S(2)}) copy-start(f32[640,448]{1,0:T(8,128)} %fusion.23) | copy-start | bytes 3440644
  339.0 20.3 %collective-permute-start.3 = (f32[384,448]{0,1:T(8,128)}, f32[384,448]{0,1:T(8,128)}, u32[]{:S(2)}, u32[]{:S(2)}) collective-permute-start(f32[384,448]{0,1:T(8,128)} %bitcast.68), channel_id=1, source_target_pairs={{0,1},{1,0},{2,3},{3,2},{4,5},{5,4},{6,7},{7,6},{8,9},{9,8},{10,11... | collective-permute-start | bytes 2064392 | tf_op jit(solution)/shard_map/ppermute | solution.py:97
  350.5 13.6 %all-to-all-start.2 = ((bf16[16,20,448]{2,1,0:T(8,128)(2,1)}), bf16[16,20,448]{2,1,0:T(8,128)(2,1)}, u32[]{:S(2)}, u32[]{:S(2)}) async-start(bf16[16,20,448]{2,1,0:T(8,128)(2,1)} %all_to_all.25), calls=%async_computation.2 | async-start | bytes 786432 | tf_op jit(solution)/shard_map/all_to_all | solution.py:98
  364.1 12.4 %all-to-all-start.1 = ((bf16[16,20,448]{2,1,0:T(8,128)(2,1)}), bf16[16,20,448]{2,1,0:T(8,128)(2,1)}, u32[]{:S(2)}, u32[]{:S(2)}) async-start(bf16[16,20,448]{2,1,0:T(8,128)(2,1)} %all_to_all.23), calls=%async_computation.1 | async-start | bytes 786432 | tf_op jit(solution)/shard_map/all_to_all | solution.py:98
  376.4 11.6 %all-to-all-start = ((bf16[16,24,448]{2,1,0:T(8,128)(2,1)}), bf16[16,24,448]{2,1,0:T(8,128)(2,1)S(1)}, u32[]{:S(2)}, u32[]{:S(2)}) async-start(bf16[16,24,448]{2,1,0:T(8,128)(2,1)} %bitcast.77), calls=%async_computation | async-start | bytes 786432 | tf_op jit(solution)/shard_map/all_to_all | solution.py:98
  (5 other events, 24.2 us)
Sparse Core Ops, SparseCore 0:
  48.7 71.0 all-gather.8
  122.9 68.5 all-gather.6
  194.5 72.7 all-gather.4

commit v2 on v1

v2 whole, which is shorter than its diff:
```python
import jax
import jax.numpy as jnp
from jax import lax
from jax.sharding import Mesh, PartitionSpec as P

SLOTS = 48
LINE = ("zh", "zl")
PLANE = ("x", "y")
PAIR = [(0, 1), (1, 0)]


def routing(expert_ids, gate_weights, capacity, expert, groups, group_rows):
    member = expert_ids == expert
    hits = jnp.sum(member.astype(jnp.int32), axis=1).reshape(groups, group_rows)
    rank = jnp.cumsum(hits, axis=1) - hits
    cap = lax.dynamic_index_in_dim(capacity, expert, 0, keepdims=False)
    weights = jnp.sum(jnp.where(member, gate_weights, 0.0), axis=1)
    slots = jnp.where((hits > 0) & (rank < cap), rank, -1)
    return slots, weights.reshape(groups, group_rows)


def gather_near(block, near):
    size = lax.axis_size(near)
    from_left, from_right = [], []
    left, right = block, block
    for step in range(1, size):
        left = lax.ppermute(left, near, [(i, i + 1) for i in range(step - 1, size - 1)])
        right = lax.ppermute(right, near, [(i + 1, i) for i in range(0, size - step)])
        from_left.append(left)
        from_right.append(right)
    around = jnp.stack(from_left[::-1] + [block] + from_right)
    return lax.dynamic_slice_in_dim(around, size - 1 - lax.axis_index(near), size, axis=0)


def local(tokens, gate_up, down, expert_ids, gate_weights, capacity):
    core = lax.axis_index("c")
    plane_index = lax.axis_index(PLANE)
    near = lax.axis_index("zl")
    chips = lax.axis_size("x") * lax.axis_size("y")
    far_size, near_size = lax.axis_size("zh"), lax.axis_size("zl")
    groups = far_size * near_size
    own, width = tokens.shape
    half = width // 2
    pair = 2 * own
    group_rows = chips * pair
    class_rows = far_size * group_rows
    class_slots = far_size * SLOTS
    mine, other = core * half, (1 - core) * half

    def half_of(array, start):
        return lax.dynamic_slice_in_dim(array, start, half, axis=array.ndim - 1)

    kept = half_of(tokens, mine)
    got = lax.ppermute(half_of(tokens, other), "c", PAIR)
    first = core == 0
    pair_tokens = jnp.concatenate(
        [jnp.where(first, kept, got), jnp.where(first, got, kept)], axis=0
    )
    line = lax.all_gather(pair_tokens, LINE, axis=0, tiled=True)
    every = lax.all_gather(line, PLANE, axis=0, tiled=True)

    units = 2 * gate_up.shape[2]
    weights_all = gate_up[0].reshape(units, width)
    w_both = jnp.concatenate(
        [half_of(weights_all, mine), lax.ppermute(half_of(weights_all, other), "c", PAIR)], axis=0
    )
    w_down = gather_near(down[0], "zl")

    slots, route = routing(
        expert_ids, gate_weights, capacity, plane_index * 2 + core, groups, group_rows
    )

    both = lax.dot_general(
        every, w_both, (((1,), (1,)), ((), ())), preferred_element_type=jnp.float32
    )
    both = both[:, :units] + lax.ppermute(both[:, units:], "c", PAIR)
    hidden = (jax.nn.silu(both[:, : units // 2]) * both[:, units // 2 :]).astype(jnp.bfloat16)

    offset = jnp.arange(far_size, dtype=jnp.int32)[:, None, None] * SLOTS
    slots = slots.reshape(far_size, near_size, group_rows)
    slots = jnp.where(slots >= 0, slots + offset, -1)
    slot_index = jnp.arange(class_slots, dtype=jnp.int32)
    by_row = slots.reshape(far_size, near_size, chips, pair).transpose(1, 2, 0, 3)
    by_row = by_row.reshape(near_size, class_rows)
    select = (by_row[:, :, None] == slot_index).astype(jnp.bfloat16)
    hidden = hidden.reshape(chips, far_size, near_size, pair, units // 2)
    hidden = hidden.transpose(2, 0, 1, 3, 4).reshape(near_size, class_rows, units // 2)
    picked = lax.dot_general(
        hidden, select, (((1,), (1,)), ((0,), (0,))), preferred_element_type=jnp.float32
    ).astype(jnp.bfloat16)
    to_all = jnp.broadcast_to(picked, (far_size,) + picked.shape)
    to_all = to_all.reshape(groups * picked.shape[1], class_slots)
    all_hidden = lax.all_to_all(to_all, LINE, split_axis=0, concat_axis=0, tiled=True)
    outputs = jnp.concatenate(
        [
            lax.dot_general(
                all_hidden, w_down[i], (((0,), (0,)), ((), ())), preferred_element_type=jnp.float32
            ).astype(jnp.bfloat16)
            for i in range(near_size)
        ],
        axis=1,
    )

    def by_target(values):
        mine = lax.dynamic_index_in_dim(values, near, 1, keepdims=False)
        mine = mine.reshape(far_size, chips, 2, own).transpose(2, 1, 0, 3)
        return mine.reshape(class_rows)

    to_slot = by_target(slots)
    to_weight = by_target(route.reshape(slots.shape))
    combine = jnp.where(
        to_slot[:, None] == slot_index[None, :], to_weight[:, None], 0.0
    ).astype(jnp.bfloat16)
    combine = combine.reshape(2, class_rows // 2, class_slots)
    give = jnp.dot(
        lax.dynamic_index_in_dim(combine, 1 - core, 0, keepdims=False),
        outputs,
        preferred_element_type=jnp.float32,
    ).astype(jnp.bfloat16)
    got = lax.ppermute(give, "c", PAIR)
    keep = jnp.dot(
        lax.dynamic_index_in_dim(combine, core, 0, keepdims=False),
        outputs,
        preferred_element_type=jnp.float32,
    )
    chip_sum = (keep + got).astype(jnp.bfloat16)
    arrived = lax.all_to_all(chip_sum, PLANE, split_axis=0, concat_axis=0, tiled=True)
    arrived = arrived.reshape(chips, far_size * own, arrived.shape[1]).astype(jnp.float32)
    own_rows = jnp.sum(arrived, axis=0).astype(jnp.bfloat16)
    own_rows = lax.all_to_all(own_rows, "zh", split_axis=0, concat_axis=0, tiled=True)
    own_rows = own_rows.reshape(far_size, own, own_rows.shape[1])
    return own_rows.transpose(1, 0, 2).reshape(own, width)


def solution(mesh):
    rows, cols = mesh.devices.shape
    near, side = 4, 4
    shape = (rows // near, near, side, cols // (2 * side), 2)
    fine = Mesh(mesh.devices.reshape(shape), ("zh", "zl", "x", "y", "c"))
    row, col = LINE, PLANE + ("c",)
    in_specs = (
        P(row + col, None),
        P(col, None, row, None),
        P(col, None, row),
        P(),
        P(),
        P(),
    )
    out_specs = P(row + col, None)
    return jax.shard_map(local, mesh=fine, in_specs=in_specs, out_specs=out_specs, check_vma=False)
```

time: 419 us -> 318 us (0.76)
  blocking collectives: 135 us -> 71.6 us
  matrix products: 33.9 us -> 20 us
  starting transfers between devices: 60.8 us -> 47.6 us
  other arithmetic: 10 us -> 4.74 us
  local copies, waits for them, and re-layouts: 29.3 us -> 24.2 us
    all_gather x4 -> x1, blocking collectives: 116 us -> 30.6 us  [local(): line = lax.all_gather(pair_tokens, LINE, axis=0, tiled=True)]
    ppermute x7 -> x9, waiting for transfers between devices: 0.02 us -> 44.5 us  [the longest x3 23.2 us: gather_near(): lax.ppermute(right, near, [(i + 1, i) for i in range(0, size - step)])]
    all_gather x3 -> x1, waiting for transfers between devices: 116 us -> 77.9 us  [local(): every = lax.all_gather(line, PLANE, axis=0, tiled=True)]
    all_to_all x1 -> x2, blocking collectives: 19 us -> 41 us  [the longest x1 22.1 us: local(): lax.all_to_all(own_rows, 'zh', split_axis=0, concat_axis=0, tiled=True)]
    ppermute x7 -> x9, starting transfers between devices: 39.7 us -> 24.7 us  [the longest x1 9.55 us: local(): lax.ppermute(half_of(weights_all, other), 'c', PAIR)]
    dot_general x12 -> x8, matrix products: 33.9 us -> 20 us  [the longest x1 9.91 us: local(): lax.dot_general(every, w_both, (((1,), (1,)), ((), ())), preferred_elemen...]
    unnamed x31 -> x19, local copies, waits for them, and re-layouts: 2.47 us -> 13.1 us
    dynamic_slice x2 -> x1, local copies, waits for them, and re-layouts: 6.2 us -> 0.02 us  [by_target(): mine = lax.dynamic_index_in_dim(values, near, 1, keepdims=False)]
  transfers between devices with their start and end apart: 14 -> 12, of which waited for: 6 -> 6; matrix products, arithmetic and copies ran while one was open for 16% -> 12% of each run, Pallas kernels for 0% -> 0%
where the time goes in v2:
time: 318 us; the launch traced here: 316 us
  waiting for transfers between devices  135 us (42%)
  blocking collectives  71.6 us (23%)
  starting transfers between devices  47.6 us (15%)
  local copies, waits for them, and re-layouts  24.2 us (8%)
  matrix products  20 us (6%)
  between operations  13.8 us (4%)
  other arithmetic  4.74 us (1%)
    all_gather x1, waiting for transfers between devices, local(): every = lax.all_gather(line, PLANE, axis=0, tiled=True)  77.9 us
    all_gather x1, blocking collectives, local(): line = lax.all_gather(pair_tokens, LINE, axis=0, tiled=True)  30.6 us
    ppermute x3, waiting for transfers between devices, gather_near(): lax.ppermute(right, near, [(i + 1, i) for i in range(0, size - step)])  23.2 us
    all_to_all x1, blocking collectives, local(): lax.all_to_all(own_rows, 'zh', split_axis=0, concat_axis=0, tiled=True)  22.1 us
    ppermute x3, waiting for transfers between devices, gather_near(): lax.ppermute(left, near, [(i, i + 1) for i in range(step - 1, size - 1)])  19.2 us
    all_to_all x1, blocking collectives, local(): lax.all_to_all(chip_sum, PLANE, split_axis=0, concat_axis=0, tiled=True)  18.9 us
    all_to_all x1, starting transfers between devices, local(): lax.all_to_all(to_all, LINE, split_axis=0, concat_axis=0, tiled=True)  14.1 us
    unnamed x19, local copies, waits for them, and re-layouts  13.1 us
  transfers between devices with their start and end apart: 12, of which 6 were waited for; matrix products, arithmetic and copies ran while one was open for 12% of the time, Pallas kernels for 0%

profile of v2, /device:TPU:1, one launch (start us, length us, event | category | flops | bytes accessed | tf_op | source)
XLA Modules:
  0.0 316.5 jit_solution(188111253558993494)
XLA Ops:
  7.3 8.8 %collective-permute-start = (bf16[4,3584]{1,0:T(4,128)(2,1)S(1)}, bf16[4,3584]{1,0:T(4,128)(2,1)S(1)}, u32[]{:S(2)}, u32[]{:S(2)}) collective-permute-start(bf16[4,3584]{1,0:T(4,128)(2,1)S(1)} %constant_dynamic-slice_fusion.4), channel_id=1, source_target_pairs={{0,1},{1,0},{2,3},{3,2},{4,5},{5,4},{6,7},{7,6},{8,9},{9,8},{10,11... | collective-permute-start | bytes 86024 | tf_op jit(solution)/shard_map/ppermute | solution.py:54
  17.7 30.6 %all_gather.6 = bf16[128,3584]{1,0:T(8,128)(2,1)} all-gather(bf16[8,3584]{1,0:T(8,128)(2,1)S(1)} %pad_maximum_fusion), channel_id=1, replica_groups=mesh['zh'=4,'zl'=4,'x'=4,'y'=4,'c'=2] {'zh','zl'}, dimensions={0}, use_global_device_ids=true | all-gather | bytes 974848 | tf_op jit(solution)/shard_map/all_gather | solution.py:59
  51.8 3.1 constant_dynamic-slice_fusion.3
  54.9 19.1 %collective-permute-done.3 = bf16[1536,448]{0,1:T(8,128)(2,1)S(1)} collective-permute-done((bf16[1536,448]{0,1:T(8,128)(2,1)}, bf16[1536,448]{0,1:T(8,128)(2,1)S(1)}, u32[]{:S(2)}, u32[]{:S(2)}) %collective-permute-start.3) | collective-permute-done | bytes 1376288 | tf_op jit(solution)/shard_map/ppermute | solution.py:27
  75.8 9.6 %collective-permute-start.1 = (bf16[192,3584]{1,0:T(8,128)(2,1)S(1)}, bf16[192,3584]{1,0:T(8,128)(2,1)}, u32[]{:S(2)}, u32[]{:S(2)}) collective-permute-start(bf16[192,3584]{1,0:T(8,128)(2,1)S(1)} %get-tuple-element.8), channel_id=1, source_target_pairs={{0,1},{1,0},{2,3},{3,2},{4,5},{5,4},{6,7},{7,6},{8,9},{9,8},{10,11... | collective-permute-start | bytes 4128776 | tf_op jit(solution)/shard_map/ppermute | solution.py:65
  89.6 77.9 %all-gather.2.cloned.1.call-done = bf16[2048,3584]{1,0:T(8,128)(2,1)} async-done(((bf16[128,3584]{1,0:T(8,128)(2,1)}), bf16[2048,3584]{1,0:T(8,128)(2,1)}) %all-gather.2.cloned.1.call-update) | async-done | bytes 14680080 | tf_op jit(solution)/shard_map/all_gather | solution.py:60
  167.5 9.9 %fusion = f32[2048,384]{0,1:T(8,128)S(1)} fusion(bf16[2048,3584]{1,0:T(8,128)(2,1)} %all-gather.2.cloned.1.call-done, bf16[192,3584]{1,0:T(8,128)(2,1)} %collective-permute-done.1, bf16[192,3584]{1,0:T(8,128)(2,1)} %get-tuple-element.7), kind=kOutput, calls=%fused_computation | convolution fusion | flops 5642649600 | bytes 20578304 | tf_op jit(solution)/shard_map/dot_general | solution.py:73
  178.7 2.6 collective-permute-start.2
  185.2 2.5 bitcast_dynamic-update-slice_fusion.5
  187.8 2.5 bitcast_dynamic-update-slice_fusion.4
  193.9 14.1 %all-to-all-start = ((bf16[16,96,192]{2,1,0:T(8,128)(2,1)}), bf16[16,96,192]{2,1,0:T(8,128)(2,1)}, u32[]{:S(2)}, u32[]{:S(2)}) async-start(bf16[16,96,192]{2,1,0:T(8,128)(2,1)} %bitcast.13), calls=%async_computation | async-start | bytes 1572864 | tf_op jit(solution)/shard_map/all_to_all | solution.py:93
  210.4 2.5 bitcast_dynamic-update-slice_fusion.2
  212.9 2.5 bitcast_dynamic-update-slice_fusion.1
  215.4 23.2 %collective-permute-done.8 = bf16[1536,448]{0,1:T(8,128)(2,1)} collective-permute-done((bf16[1536,448]{0,1:T(8,128)(2,1)}, bf16[1536,448]{0,1:T(8,128)(2,1)}, u32[]{:S(2)}, u32[]{:S(2)}) %collective-permute-start.8) | collective-permute-done | bytes 1376288 | tf_op jit(solution)/shard_map/ppermute | solution.py:28
  238.6 2.6 bitcast_dynamic-update-slice_fusion
  241.2 11.3 %all-to-all-done = bf16[16,96,192]{2,1,0:T(8,128)(2,1)} async-done(((bf16[16,96,192]{2,1,0:T(8,128)(2,1)}), bf16[16,96,192]{2,1,0:T(8,128)(2,1)}, u32[]{:S(2)}, u32[]{:S(2)}) %all-to-all-start) | async-done | bytes 589856 | tf_op jit(solution)/shard_map/all_to_all | solution.py:93
  252.5 2.2 fusion.10
  254.7 2.2 fusion.11
  257.0 2.2 fusion.12
  259.2 2.2 fusion.13
  262.3 3.1 collective-permute-start.9
  265.4 2.1 collective-permute-done.9
  267.9 18.9 %all_to_all.30 = bf16[16,16,1792]{2,1,0:T(8,128)(2,1)S(1)} all-to-all(bf16[16,16,1792]{2,1,0:T(8,128)(2,1)S(1)} %bitcast.69), channel_id=1, replica_groups=mesh['zh'=4,'zl'=4,'x'=4,'y'=4,'c'=2] {'x','y'}, dimensions={0} | all-to-all | bytes 1835008 | tf_op jit(solution)/shard_map/all_to_all | solution.py:127
  286.9 22.1 %all_to_all.31 = bf16[4,4,1792]{2,1,0:T(4,128)(2,1)S(1)} all-to-all(bf16[4,4,1792]{2,1,0:T(4,128)(2,1)S(1)} %all_to_all.25), channel_id=1, replica_groups=mesh['zh'=4,'zl'=4,'x'=4,'y'=4,'c'=2] {'zh'}, dimensions={0} | all-to-all | bytes 114688 | tf_op jit(solution)/shard_map/all_to_all | solution.py:130
  (64 shorter events, 24.8 us)
Async XLA Ops:
  6.5 161.0 %all-gather.2.cloned.1.call-start = ((), (), s32[]{:S(2)}) async-start(), calls=%async_computation.3 | async-start | bytes 15597568 | tf_op jit(solution)/shard_map/all_gather | solution.py:60
  7.3 9.6 %collective-permute-start = (bf16[4,3584]{1,0:T(4,128)(2,1)S(1)}, bf16[4,3584]{1,0:T(4,128)(2,1)S(1)}, u32[]{:S(2)}, u32[]{:S(2)}) collective-permute-start(bf16[4,3584]{1,0:T(4,128)(2,1)S(1)} %constant_dynamic-slice_fusion.4), channel_id=1, source_target_pairs={{0,1},{1,0},{2,3},{3,2},{4,5},{5,4},{6,7},{7,6},{8,9},{9,8},{10,11... | collective-permute-start | bytes 86024 | tf_op jit(solution)/shard_map/ppermute | solution.py:54
  48.4 25.6 %collective-permute-start.3 = (bf16[1536,448]{0,1:T(8,128)(2,1)}, bf16[1536,448]{0,1:T(8,128)(2,1)S(1)}, u32[]{:S(2)}, u32[]{:S(2)}) collective-permute-start(bf16[1536,448]{0,1:T(8,128)(2,1)} %bitcast.72), channel_id=1, source_target_pairs={{0,32},{32,64},{64,96},{1,33},{33,65},{65,97},{2,34},{34,66},{66,9... | collective-permute-start | bytes 4128776 | tf_op jit(solution)/shard_map/ppermute | solution.py:27
  50.5 36.1 %collective-permute-start.6 = (bf16[1536,448]{0,1:T(8,128)(2,1)}, bf16[1536,448]{0,1:T(8,128)(2,1)}, u32[]{:S(2)}, u32[]{:S(2)}) collective-permute-start(bf16[1536,448]{0,1:T(8,128)(2,1)} %bitcast.73), channel_id=1, source_target_pairs={{32,0},{64,32},{96,64},{33,1},{65,33},{97,65},{34,2},{66,34},{98,6... | collective-permute-start | bytes 4128776 | tf_op jit(solution)/shard_map/ppermute | solution.py:28
  51.8 33.6 %copy-start.3 = (f32[2048,8]{0,1:T(8,128)S(1)}, f32[2048,8]{0,1:T(8,128)}, u32[]{:S(2)}) copy-start(f32[2048,8]{0,1:T(8,128)} %param.10) | copy-start | bytes 196612
  51.8 33.6 %copy-start.4 = (s32[2048,8]{0,1:T(8,128)S(1)}, s32[2048,8]{0,1:T(8,128)}, u32[]{:S(2)}) copy-start(s32[2048,8]{0,1:T(8,128)} %param.9) | copy-start | bytes 196612
  51.8 34.2 %copy-start.5 = (s32[32]{0:T(128)S(1)}, s32[32]{0:T(128)}, u32[]{:S(2)}) copy-start(s32[32]{0:T(128)} %param.11) | copy-start | bytes 388
  74.0 93.5 %copy-start.1 = (bf16[1536,448]{0,1:T(8,128)(2,1)}, bf16[1536,448]{0,1:T(8,128)(2,1)S(1)}, u32[]{:S(2)}) copy-start(bf16[1536,448]{0,1:T(8,128)(2,1)S(1)} %collective-permute-done.3) | copy-start | bytes 4128772
  74.0 13.8 %collective-permute-start.4 = (bf16[1536,448]{0,1:T(8,128)(2,1)S(1)}, bf16[1536,448]{0,1:T(8,128)(2,1)}, u32[]{:S(2)}, u32[]{:S(2)}) collective-permute-start(bf16[1536,448]{0,1:T(8,128)(2,1)S(1)} %collective-permute-done.3), channel_id=1, source_target_pairs={{32,64},{64,96},{33,65},{65,97},{34,66},{66,98},{35,67},{67,99},{3... | collective-permute-start | bytes 4128776 | tf_op jit(solution)/shard_map/ppermute | solution.py:27
  75.8 13.8 %collective-permute-start.1 = (bf16[192,3584]{1,0:T(8,128)(2,1)S(1)}, bf16[192,3584]{1,0:T(8,128)(2,1)}, u32[]{:S(2)}, u32[]{:S(2)}) collective-permute-start(bf16[192,3584]{1,0:T(8,128)(2,1)S(1)} %get-tuple-element.8), channel_id=1, source_target_pairs={{0,1},{1,0},{2,3},{3,2},{4,5},{5,4},{6,7},{7,6},{8,9},{9,8},{10,11... | collective-permute-start | bytes 4128776 | tf_op jit(solution)/shard_map/ppermute | solution.py:65
  86.6 97.3 %collective-permute-start.7 = (bf16[1536,448]{0,1:T(8,128)(2,1)}, bf16[1536,448]{0,1:T(8,128)(2,1)}, u32[]{:S(2)}, u32[]{:S(2)}) collective-permute-start(bf16[1536,448]{0,1:T(8,128)(2,1)} %collective-permute-done.6), channel_id=1, source_target_pairs={{32,0},{64,32},{33,1},{65,33},{34,2},{66,34},{35,3},{67,35},{36,4}... | collective-permute-start | bytes 4128776 | tf_op jit(solution)/shard_map/ppermute | solution.py:28
  87.9 97.3 %collective-permute-start.5 = (bf16[1536,448]{0,1:T(8,128)(2,1)}, bf16[1536,448]{0,1:T(8,128)(2,1)}, u32[]{:S(2)}, u32[]{:S(2)}) collective-permute-start(bf16[1536,448]{0,1:T(8,128)(2,1)} %collective-permute-done.4), channel_id=1, source_target_pairs={{64,96},{65,97},{66,98},{67,99},{68,100},{69,101},{70,102},{71,103... | collective-permute-start | bytes 4128776 | tf_op jit(solution)/shard_map/ppermute | solution.py:27
  178.7 11.6 %collective-permute-start.2 = (f32[2048,192]{0,1:T(8,128)}, f32[2048,192]{0,1:T(8,128)}, u32[]{:S(2)}, u32[]{:S(2)}) collective-permute-start(f32[2048,192]{0,1:T(8,128)} %slice.33), channel_id=1, source_target_pairs={{0,1},{1,0},{2,3},{3,2},{4,5},{5,4},{6,7},{7,6},{8,9},{9,8},{10,11... | collective-permute-start | bytes 4718600 | tf_op jit(solution)/shard_map/ppermute | solution.py:76
  183.9 54.8 %collective-permute-start.8 = (bf16[1536,448]{0,1:T(8,128)(2,1)}, bf16[1536,448]{0,1:T(8,128)(2,1)}, u32[]{:S(2)}, u32[]{:S(2)}) collective-permute-start(bf16[1536,448]{0,1:T(8,128)(2,1)} %collective-permute-done.7), channel_id=1, source_target_pairs={{32,0},{33,1},{34,2},{35,3},{36,4},{37,5},{38,6},{39,7},{40,8},{41... | collective-permute-start | bytes 4128776 | tf_op jit(solution)/shard_map/ppermute | solution.py:28
  192.1 15.9 %copy-start.2 = (bf16[1536,448]{0,1:T(8,128)(2,1)S(1)}, bf16[1536,448]{0,1:T(8,128)(2,1)}, u32[]{:S(2)}) copy-start(bf16[1536,448]{0,1:T(8,128)(2,1)} %copy-done.1) | copy-start | bytes 4128772
  192.9 16.2 %copy-start = (bf16[1,1536,448]{1,2,0:T(8,128)(2,1)S(1)}, bf16[1,1536,448]{1,2,0:T(8,128)(2,1)}, u32[]{:S(2)}) copy-start(bf16[1,1536,448]{1,2,0:T(8,128)(2,1)} %param.8) | copy-start | bytes 4128772
  193.9 58.6 %all-to-all-start = ((bf16[16,96,192]{2,1,0:T(8,128)(2,1)}), bf16[16,96,192]{2,1,0:T(8,128)(2,1)}, u32[]{:S(2)}, u32[]{:S(2)}) async-start(bf16[16,96,192]{2,1,0:T(8,128)(2,1)} %bitcast.13), calls=%async_computation | async-start | bytes 1572864 | tf_op jit(solution)/shard_map/all_to_all | solution.py:93
  262.3 5.2 %collective-permute-start.9 = (bf16[256,1792]{1,0:T(8,128)(2,1)S(1)}, bf16[256,1792]{1,0:T(8,128)(2,1)S(1)}, u32[]{:S(2)}, u32[]{:S(2)}) collective-permute-start(bf16[256,1792]{1,0:T(8,128)(2,1)S(1)} %convolution_convert_fusion), channel_id=1, source_target_pairs={{0,1},{1,0},{2,3},{3,2},{4,5},{5,4},{6,7},{7,6},{8,9},{9,8},{10,11... | collective-permute-start | bytes 2752520 | tf_op jit(solution)/shard_map/ppermute | solution.py:120
Sparse Core Ops, SparseCore 0:
  48.5 118.9 all-gather.1

commit v3 on v1

v3 whole, which is shorter than its diff:
```python
import jax
import jax.numpy as jnp
from jax import lax
from jax.sharding import Mesh, PartitionSpec as P

SLOTS = 48
LINE = ("zh", "k", "p")
PLANE = ("x", "y")
PAIR = [(0, 1), (1, 0)]


def routing(expert_ids, gate_weights, capacity, expert):
    member = expert_ids == expert
    hits = jnp.sum(member.astype(jnp.int32), axis=2)
    rank = jnp.cumsum(hits, axis=1) - hits
    cap = lax.dynamic_index_in_dim(capacity, expert, 0, keepdims=False)
    weights = jnp.sum(jnp.where(member, gate_weights, 0.0), axis=2)
    offset = jnp.arange(hits.shape[0], dtype=jnp.int32)[:, None] * SLOTS
    return jnp.where((hits > 0) & (rank < cap), rank + offset, -1), weights


def local(tokens, gate_up, down, expert_ids, gate_weights, capacity):
    core = lax.axis_index("c")
    k, p = lax.axis_index("k"), lax.axis_index("p")
    plane_index = lax.axis_index(PLANE)
    chips = lax.axis_size("x") * lax.axis_size("y")
    far = lax.axis_size("zh")
    own, width = tokens.shape
    group_rows = chips * 2 * own
    class_rows = far * group_rows
    class_slots = far * SLOTS

    def of_class(values, which):
        values = values.reshape((far, 2, 2) + values.shape[1:])
        return lax.dynamic_index_in_dim(
            lax.dynamic_index_in_dim(values, p, 2, keepdims=False), which, 1, keepdims=False
        )

    line = lax.all_gather(tokens, LINE, axis=0, tiled=False)
    mine = of_class(line, core)
    got = lax.ppermute(of_class(line, 1 - core), "c", PAIR)
    first = core == 0
    chip_rows = jnp.stack([jnp.where(first, mine, got), jnp.where(first, got, mine)])
    chip_rows = chip_rows.reshape(2 * far * own, width)
    every = lax.all_gather(chip_rows, PLANE, axis=0, tiled=True)

    units = gate_up.shape[2]
    w_own = gate_up[0].reshape(2 * units, width)
    w_pair = lax.ppermute(w_own, "p", PAIR)
    d_own = down[0]
    d_pair = lax.ppermute(d_own, "p", PAIR)
    w_all = jnp.concatenate(
        [w_own, lax.ppermute(w_own, "c", PAIR), w_pair, lax.ppermute(w_pair, "c", PAIR)], axis=0
    )
    d_all = [[d_own, d_pair], [lax.ppermute(d_own, "c", PAIR), lax.ppermute(d_pair, "c", PAIR)]]

    ids = of_class(expert_ids.reshape(far * 4, group_rows, -1), core)
    gates = of_class(gate_weights.reshape(far * 4, group_rows, -1), core)

    def by_row(values):
        values = values.reshape(far, chips, 2, own).transpose(1, 2, 0, 3)
        return values.reshape(class_rows)

    slot_index = jnp.arange(class_slots, dtype=jnp.int32)
    hits, combine = [], []
    for expert in (plane_index * 2 + core, plane_index * 2 + 1 - core):
        slots, weights = routing(ids, gates, capacity, expert)
        hit = by_row(slots)[:, None] == slot_index[None, :]
        hits.append(hit.astype(jnp.bfloat16))
        combine.append(jnp.where(hit, by_row(weights)[:, None], 0.0).astype(jnp.bfloat16))
    combine = jnp.concatenate(combine, axis=1)

    both = lax.dot_general(
        w_all, every, (((1,), (1,)), ((), ())), preferred_element_type=jnp.float32
    )
    both = both.reshape(2, 2, 2, units, class_rows)
    hidden = (jax.nn.silu(both[:, :, 0]) * both[:, :, 1]).astype(jnp.bfloat16)

    outputs = []
    for e in range(2):
        picked = lax.dot_general(
            hidden[:, e].reshape(2 * units, class_rows),
            hits[e],
            (((1,), (0,)), ((), ())),
            preferred_element_type=jnp.float32,
        ).astype(jnp.bfloat16)
        picked = picked.reshape(2, units, class_slots)
        picked = jnp.where(p == 0, picked, picked[::-1]).reshape(2 * units, class_slots)
        all_hidden = lax.all_gather(picked, ("zh", "k"), axis=0, tiled=True)
        outputs.append(
            jnp.concatenate(
                [
                    lax.dot_general(
                        all_hidden, d, (((0,), (0,)), ((), ())), preferred_element_type=jnp.float32
                    ).astype(jnp.bfloat16)
                    for d in d_all[e]
                ],
                axis=1,
            )
        )
    outputs = jnp.concatenate(outputs, axis=0)

    summed = jnp.dot(combine, outputs, preferred_element_type=jnp.float32).astype(jnp.bfloat16)
    arrived = lax.all_to_all(summed, PLANE, split_axis=0, concat_axis=0, tiled=True)
    arrived = arrived.reshape(chips, 2 * far * own, arrived.shape[1]).astype(jnp.float32)
    rows = jnp.sum(arrived, axis=0).astype(jnp.bfloat16)
    features = rows.shape[1]

    rows = rows.reshape(2, far, own, features).transpose(1, 0, 2, 3)[:, None]
    here = (jnp.arange(2) == core)[None, :, None, None, None]
    send = jnp.where(here, rows, jnp.zeros((), rows.dtype)).reshape(far * 4 * own, features)
    recv = lax.all_to_all(send, ("zh", "k", "c"), split_axis=0, concat_axis=0, tiled=True)
    recv = recv.reshape(far, 2, 2, own, features)
    recv = lax.dynamic_index_in_dim(recv, k, 2, keepdims=False)
    recv = recv.reshape(far, 2, own, 2, features // 2)
    recv = jnp.where(p == 0, recv, recv[:, :, :, ::-1])
    return recv.transpose(2, 0, 1, 3, 4).reshape(own, width)


def solution(mesh):
    rows, cols = mesh.devices.shape
    side = 4
    shape = (rows // 4, 2, 2, side, cols // (2 * side), 2)
    fine = Mesh(mesh.devices.reshape(shape), LINE + PLANE + ("c",))
    row, col = LINE, PLANE + ("c",)
    in_specs = (
        P(row + col, None),
        P(col, None, row, None),
        P(col, None, row),
        P(),
        P(),
        P(),
    )
    out_specs = P(row + col, None)
    return jax.shard_map(local, mesh=fine, in_specs=in_specs, out_specs=out_specs, check_vma=False)
```

time: 419 us -> 296 us (0.71)
  blocking collectives: 135 us -> 87.1 us
  local copies, waits for them, and re-layouts: 29.3 us -> 5.09 us
  waiting for transfers between devices: 132 us -> 110 us
  matrix products: 33.9 us -> 22.9 us
  starting transfers between devices: 60.8 us -> 51.8 us
  other arithmetic: 10 us -> 4.92 us
    all_gather x3 -> x1, waiting for transfers between devices: 116 us -> 0.02 us  [local(): every = lax.all_gather(chip_rows, PLANE, axis=0, tiled=True)]
    ppermute x8 -> x7, waiting for transfers between devices: 0.84 us -> 83.8 us  [the longest x1 58.9 us: local(): w_pair = lax.ppermute(w_own, 'p', PAIR)]
    all_gather x4 -> x3, blocking collectives: 116 us -> 87.1 us  [the longest x2 52.1 us: local(): all_hidden = lax.all_gather(picked, ('zh', 'k'), axis=0, tiled=True)]
    ppermute x8 -> x7, starting transfers between devices: 48.5 us -> 23.6 us  [the longest x1 9.51 us: local(): got = lax.ppermute(of_class(line, 1 - core), 'c', PAIR)]
    all_to_all x1 -> x0, blocking collectives: 19 us -> none  [local(): lax.all_to_all(own_rows, 'z', split_axis=0, concat_axis=0, tiled=True)]
    all_to_all x3 -> x2, starting transfers between devices: 12.2 us -> 28.1 us  [the longest x1 16.5 us: local(): lax.all_to_all(send, ('zh', 'k', 'c'), split_axis=0, concat_axis=0, tiled...]
    all_to_all x3 -> x2, waiting for transfers between devices: 14.4 us -> 25.8 us  [the longest x1 14.9 us: local(): lax.all_to_all(send, ('zh', 'k', 'c'), split_axis=0, concat_axis=0, tiled...]
    dot_general x12 -> x8, matrix products: 33.9 us -> 22.9 us  [the longest x1 14.1 us: local(): lax.dot_general(w_all, every, (((1,), (1,)), ((), ())), preferred_element...]
  transfers between devices with their start and end apart: 14 -> 10, of which waited for: 6 -> 5; matrix products, arithmetic and copies ran while one was open for 16% -> 9% of each run, Pallas kernels for 0% -> 0%
where the time goes in v3:
time: 296 us; the launch traced here: 295 us
  waiting for transfers between devices  110 us (37%)
  blocking collectives  87.1 us (29%)
  starting transfers between devices  51.8 us (18%)
  matrix products  22.9 us (8%)
  between operations  13.7 us (5%)
  local copies, waits for them, and re-layouts  5.09 us (2%)
  other arithmetic  4.92 us (2%)
    ppermute x1, waiting for transfers between devices, local(): w_pair = lax.ppermute(w_own, 'p', PAIR)  58.9 us
    all_gather x2, blocking collectives, local(): all_hidden = lax.all_gather(picked, ('zh', 'k'), axis=0, tiled=True)  52.1 us
    all_gather x1, blocking collectives, local(): line = lax.all_gather(tokens, LINE, axis=0, tiled=False)  35 us
    ppermute x1, waiting for transfers between devices, local(): d_pair = lax.ppermute(d_own, 'p', PAIR)  23.9 us
    all_to_all x1, starting transfers between devices, local(): lax.all_to_all(send, ('zh', 'k', 'c'), split_axis=0, concat_axis=0, tiled...  16.5 us
    all_to_all x1, waiting for transfers between devices, local(): lax.all_to_all(send, ('zh', 'k', 'c'), split_axis=0, concat_axis=0, tiled...  14.9 us
    dot_general x1, matrix products, local(): lax.dot_general(w_all, every, (((1,), (1,)), ((), ())), preferred_element...  14.1 us
    all_to_all x1, starting transfers between devices, local(): lax.all_to_all(summed, PLANE, split_axis=0, concat_axis=0, tiled=True)  11.6 us
  transfers between devices with their start and end apart: 10, of which 5 were waited for; matrix products, arithmetic and copies ran while one was open for 9% of the time, Pallas kernels for 0%

profile of v3, /device:TPU:1, one launch (start us, length us, event | category | flops | bytes accessed | tf_op | source)
XLA Modules:
  0.0 295.2 jit_solution(12810110194536229752)
XLA Ops:
  6.5 35.0 %all-gather.1 = bf16[16,4,7168]{2,1,0:T(4,128)(2,1)S(1)} all-gather(bf16[1,4,7168]{2,1,0:T(4,128)(2,1)} %bitcast.90), channel_id=2, replica_groups=mesh['zh'=4,'k'=2,'p'=2,'x'=4,'y'=4,'c'=2] {'zh','k','p'}, dimensions={0}, use_global_device_ids=true | all-gather | bytes 974848 | tf_op jit(solution)/shard_map/all_gather | solution.py:39
  41.6 9.5 %collective-permute-start.3 = (bf16[4,4,7168]{2,1,0:T(4,128)(2,1)S(1)}, bf16[4,4,7168]{2,1,0:T(4,128)(2,1)S(1)}, u32[]{:S(2)}, u32[]{:S(2)}) collective-permute-start(bf16[4,4,7168]{2,1,0:T(4,128)(2,1)S(1)} %dynamic-slice_bitcast_fusion), channel_id=1, source_target_pairs={{0,1},{1,0},{2,3},{3,2},{4,5},{5,4},{6,7},{7,6},{8,9},{9,8},{10,11... | collective-permute-start | bytes 688136 | tf_op jit(solution)/shard_map/ppermute | solution.py:41
  51.1 1.1 collective-permute-done.3
  52.7 0.9 reshape.115
  53.6 1.9 collective-permute-start.1
  55.6 2.3 collective-permute-start
  57.9 58.9 %collective-permute-done.1 = bf16[192,7168]{1,0:T(8,128)(2,1)} collective-permute-done((bf16[192,7168]{1,0:T(8,128)(2,1)}, bf16[192,7168]{1,0:T(8,128)(2,1)}, u32[]{:S(2)}, u32[]{:S(2)}) %collective-permute-start.1) | collective-permute-done | bytes 2752544 | tf_op jit(solution)/shard_map/ppermute | solution.py:49
  116.7 3.1 %collective-permute-start.2 = (bf16[192,7168]{1,0:T(8,128)(2,1)}, bf16[192,7168]{1,0:T(8,128)(2,1)}, u32[]{:S(2)}, u32[]{:S(2)}) collective-permute-start(bf16[192,7168]{1,0:T(8,128)(2,1)} %collective-permute-done.1), channel_id=1, source_target_pairs={{0,1},{1,0},{2,3},{3,2},{4,5},{5,4},{6,7},{7,6},{8,9},{9,8},{10,11... | collective-permute-start | bytes 8257544 | tf_op jit(solution)/shard_map/ppermute | solution.py:53
  119.9 1.9 collective-permute-start.4
  121.8 2.2 collective-permute-start.5
  126.6 1.3 select_bitcast_fusion.1
  129.8 23.9 %collective-permute-done.4 = bf16[1536,448]{0,1:T(8,128)(2,1)} collective-permute-done((bf16[1536,448]{0,1:T(8,128)(2,1)S(1)}, bf16[1536,448]{0,1:T(8,128)(2,1)}, u32[]{:S(2)}, u32[]{:S(2)}) %collective-permute-start.4) | collective-permute-done | bytes 1376288 | tf_op jit(solution)/shard_map/ppermute | solution.py:51
  153.7 2.7 collective-permute-start.6
  156.4 14.1 %fusion = f32[768,512]{1,0:T(8,128)S(1)} fusion(bf16[512,7168]{1,0:T(8,128)(2,1)} %all-gather.4.cloned.1.call-done, bf16[192,7168]{1,0:T(8,128)(2,1)} %collective-permute-done.2, bf16[192,7168]{1,0:T(8,128)(2,1)} %collective-permute-done.1, bf16[192,7168]{1,0:T(8,128)(2,1)} %collective-permute-done, bf16[192,7168]{1,0:T(8,128)(2,1)} %bitcast.95), kind=kOutput, calls=%fused_computation | convolution fusion | flops 5681184768 | bytes 19922944 | tf_op jit(solution)/shard_map/dot_general | solution.py:73
  171.6 26.5 %all_gather.19 = bf16[1536,192]{1,0:T(8,128)(2,1)S(1)} all-gather(bf16[192,192]{1,0:T(8,128)(2,1)S(1)} %bitcast.77), channel_id=1, replica_groups=mesh['zh'=4,'k'=2,'p'=2,'x'=4,'y'=4,'c'=2] {'zh','k'}, dimensions={0}, use_global_device_ids=true | all-gather | bytes 663552 | tf_op jit(solution)/shard_map/all_gather | solution.py:89
  198.1 25.5 %all_gather.18 = bf16[1536,192]{1,0:T(8,128)(2,1)S(1)} all-gather(bf16[192,192]{1,0:T(8,128)(2,1)S(1)} %bitcast.78), channel_id=1, replica_groups=mesh['zh'=4,'k'=2,'p'=2,'x'=4,'y'=4,'c'=2] {'zh','k'}, dimensions={0}, use_global_device_ids=true | all-gather | bytes 663552 | tf_op jit(solution)/shard_map/all_gather | solution.py:89
  224.3 2.0 convolution_convert_fusion.3
  226.2 2.0 convolution_convert_fusion.1
  228.2 2.0 convolution_convert_fusion.2
  230.2 1.7 convolution_convert_fusion
  231.9 11.6 %all-to-all-start = ((bf16[16,32,896]{2,1,0:T(8,128)(2,1)}), bf16[16,32,896]{2,1,0:T(8,128)(2,1)S(1)}, u32[]{:S(2)}, u32[]{:S(2)}) async-start(bf16[16,32,896]{2,1,0:T(8,128)(2,1)} %bitcast.27), calls=%async_computation | async-start | bytes 1835008 | tf_op jit(solution)/shard_map/all_to_all | solution.py:104
  243.7 10.9 %all-to-all-done = bf16[16,32,896]{2,1,0:T(8,128)(2,1)S(1)} async-done(((bf16[16,32,896]{2,1,0:T(8,128)(2,1)}), bf16[16,32,896]{2,1,0:T(8,128)(2,1)S(1)}, u32[]{:S(2)}, u32[]{:S(2)}) %all-to-all-start) | async-done | bytes 917536 | tf_op jit(solution)/shard_map/all_to_all | solution.py:104
  255.4 16.5 %all-to-all-start.1 = ((bf16[16,4,896]{2,1,0:T(4,128)(2,1)}), bf16[16,4,896]{2,1,0:T(4,128)(2,1)S(1)}, u32[]{:S(2)}, u32[]{:S(2)}) async-start(bf16[16,4,896]{2,1,0:T(4,128)(2,1)} %bitcast_select_fusion.2), calls=%async_computation.1 | async-start | bytes 229376 | tf_op jit(solution)/shard_map/all_to_all | solution.py:112
  272.0 14.9 %all-to-all-done.1 = bf16[16,4,896]{2,1,0:T(4,128)(2,1)S(1)} async-done(((bf16[16,4,896]{2,1,0:T(4,128)(2,1)}), bf16[16,4,896]{2,1,0:T(4,128)(2,1)S(1)}, u32[]{:S(2)}, u32[]{:S(2)}) %all-to-all-start.1) | async-done | bytes 114720 | tf_op jit(solution)/shard_map/all_to_all | solution.py:112
  (59 shorter events, 9.1 us)
Async XLA Ops:
  6.5 113.3 %copy-start = (bf16[1,1536,448]{1,2,0:T(8,128)(2,1)S(1)}, bf16[1,1536,448]{1,2,0:T(8,128)(2,1)}, u32[]{:S(2)}) copy-start(bf16[1,1536,448]{1,2,0:T(8,128)(2,1)} %param.8) | copy-start | bytes 4128772
  6.5 119.4 %copy-start.1 = (s32[32]{0:T(128)S(1)}, s32[32]{0:T(128)}, u32[]{:S(2)}) copy-start(s32[32]{0:T(128)} %param.11) | copy-start | bytes 388
  6.5 149.9 %all-gather.4.cloned.1.call-start = ((), (), s32[]{:S(2)}) async-start(), calls=%async_computation.2 | async-start | bytes 7798784 | tf_op jit(solution)/shard_map/all_gather | solution.py:45
  41.6 10.6 %collective-permute-start.3 = (bf16[4,4,7168]{2,1,0:T(4,128)(2,1)S(1)}, bf16[4,4,7168]{2,1,0:T(4,128)(2,1)S(1)}, u32[]{:S(2)}, u32[]{:S(2)}) collective-permute-start(bf16[4,4,7168]{2,1,0:T(4,128)(2,1)S(1)} %dynamic-slice_bitcast_fusion), channel_id=1, source_target_pairs={{0,1},{1,0},{2,3},{3,2},{4,5},{5,4},{6,7},{7,6},{8,9},{9,8},{10,11... | collective-permute-start | bytes 688136 | tf_op jit(solution)/shard_map/ppermute | solution.py:41
  53.6 63.1 %collective-permute-start.1 = (bf16[192,7168]{1,0:T(8,128)(2,1)}, bf16[192,7168]{1,0:T(8,128)(2,1)}, u32[]{:S(2)}, u32[]{:S(2)}) collective-permute-start(bf16[192,7168]{1,0:T(8,128)(2,1)} %bitcast.93), channel_id=1, source_target_pairs={{0,32},{32,0},{1,33},{33,1},{2,34},{34,2},{3,35},{35,3},{4,36},{36... | collective-permute-start | bytes 8257544 | tf_op jit(solution)/shard_map/ppermute | solution.py:49
  55.6 100.8 %collective-permute-start = (bf16[192,7168]{1,0:T(8,128)(2,1)}, bf16[192,7168]{1,0:T(8,128)(2,1)}, u32[]{:S(2)}, u32[]{:S(2)}) collective-permute-start(bf16[192,7168]{1,0:T(8,128)(2,1)} %bitcast.94), channel_id=1, source_target_pairs={{0,1},{1,0},{2,3},{3,2},{4,5},{5,4},{6,7},{7,6},{8,9},{9,8},{10,11... | collective-permute-start | bytes 8257544 | tf_op jit(solution)/shard_map/ppermute | solution.py:53
  116.7 39.6 %collective-permute-start.2 = (bf16[192,7168]{1,0:T(8,128)(2,1)}, bf16[192,7168]{1,0:T(8,128)(2,1)}, u32[]{:S(2)}, u32[]{:S(2)}) collective-permute-start(bf16[192,7168]{1,0:T(8,128)(2,1)} %collective-permute-done.1), channel_id=1, source_target_pairs={{0,1},{1,0},{2,3},{3,2},{4,5},{5,4},{6,7},{7,6},{8,9},{9,8},{10,11... | collective-permute-start | bytes 8257544 | tf_op jit(solution)/shard_map/ppermute | solution.py:53
  119.9 33.8 %collective-permute-start.4 = (bf16[1536,448]{0,1:T(8,128)(2,1)S(1)}, bf16[1536,448]{0,1:T(8,128)(2,1)}, u32[]{:S(2)}, u32[]{:S(2)}) collective-permute-start(bf16[1536,448]{0,1:T(8,128)(2,1)S(1)} %bitcast.75), channel_id=1, source_target_pairs={{0,32},{32,0},{1,33},{33,1},{2,34},{34,2},{3,35},{35,3},{4,36},{36... | collective-permute-start | bytes 4128776 | tf_op jit(solution)/shard_map/ppermute | solution.py:51
  121.8 106.4 %collective-permute-start.5 = (bf16[1536,448]{0,1:T(8,128)(2,1)S(1)}, bf16[1536,448]{0,1:T(8,128)(2,1)}, u32[]{:S(2)}, u32[]{:S(2)}) collective-permute-start(bf16[1536,448]{0,1:T(8,128)(2,1)S(1)} %bitcast.76), channel_id=1, source_target_pairs={{0,1},{1,0},{2,3},{3,2},{4,5},{5,4},{6,7},{7,6},{8,9},{9,8},{10,11... | collective-permute-start | bytes 4128776 | tf_op jit(solution)/shard_map/ppermute | solution.py:55
  153.7 72.6 %collective-permute-start.6 = (bf16[1536,448]{0,1:T(8,128)(2,1)}, bf16[1536,448]{0,1:T(8,128)(2,1)}, u32[]{:S(2)}, u32[]{:S(2)}) collective-permute-start(bf16[1536,448]{0,1:T(8,128)(2,1)} %collective-permute-done.4), channel_id=1, source_target_pairs={{0,1},{1,0},{2,3},{3,2},{4,5},{5,4},{6,7},{7,6},{8,9},{9,8},{10,11... | collective-permute-start | bytes 4128776 | tf_op jit(solution)/shard_map/ppermute | solution.py:55
  231.9 22.7 %all-to-all-start = ((bf16[16,32,896]{2,1,0:T(8,128)(2,1)}), bf16[16,32,896]{2,1,0:T(8,128)(2,1)S(1)}, u32[]{:S(2)}, u32[]{:S(2)}) async-start(bf16[16,32,896]{2,1,0:T(8,128)(2,1)} %bitcast.27), calls=%async_computation | async-start | bytes 1835008 | tf_op jit(solution)/shard_map/all_to_all | solution.py:104
  255.4 31.5 %all-to-all-start.1 = ((bf16[16,4,896]{2,1,0:T(4,128)(2,1)}), bf16[16,4,896]{2,1,0:T(4,128)(2,1)S(1)}, u32[]{:S(2)}, u32[]{:S(2)}) async-start(bf16[16,4,896]{2,1,0:T(4,128)(2,1)} %bitcast_select_fusion.2), calls=%async_computation.1 | async-start | bytes 229376 | tf_op jit(solution)/shard_map/all_to_all | solution.py:112
Sparse Core Ops, SparseCore 0:
  53.8 77.0 all-gather.3

commit v4 on v3

--- a/solution.py
+++ b/solution.py
@@ -6,7 +6,32 @@
 SLOTS = 48
 LINE = ("zh", "k", "p")
 PLANE = ("x", "y")
+CHIP = PLANE + ("c",)
 PAIR = [(0, 1), (1, 0)]
+
+
+def turned(block, phase, shift):
+    nx, ny = lax.axis_size("x"), lax.axis_size("y")
+    perm = []
+    for x in range(nx):
+        for y in range(ny):
+            for c in range(2):
+                along_x = c == phase
+                to_x = (x + shift) % nx if along_x else x
+                to_y = y if along_x else (y + shift) % ny
+                perm.append(((x * ny + y) * 2 + c, (to_x * ny + to_y) * 2 + c))
+    return lax.ppermute(block, CHIP, perm)
+
+
+def ring(block, phase, other=None):
+    half = block.shape[0] // 2
+    behind = turned(block, phase, 1)
+    ahead = turned(block, phase, -1)
+    if other is not None:
+        other, ahead, behind = lax.optimization_barrier((other, ahead, behind))
+    far_low = turned(behind[:half], phase, 1)
+    far_high = turned(ahead[half:], phase, -1)
+    return (block, ahead, jnp.concatenate([far_low, far_high], axis=0), behind), other
 
 
 def routing(expert_ids, gate_weights, capacity, expert):
@@ -42,17 +67,15 @@
     first = core == 0
     chip_rows = jnp.stack([jnp.where(first, mine, got), jnp.where(first, got, mine)])
     chip_rows = chip_rows.reshape(2 * far * own, width)
-    every = lax.all_gather(chip_rows, PLANE, axis=0, tiled=True)
+    w_mine = lax.all_gather(gate_up[0], "p", axis=0, tiled=False)
+    d_mine = lax.all_gather(down[0], "p", axis=0, tiled=False)
+    units = gate_up.shape[2]
+    w_mine = w_mine.reshape(4 * units, width)
 
-    units = gate_up.shape[2]
-    w_own = gate_up[0].reshape(2 * units, width)
-    w_pair = lax.ppermute(w_own, "p", PAIR)
-    d_own = down[0]
-    d_pair = lax.ppermute(d_own, "p", PAIR)
-    w_all = jnp.concatenate(
-        [w_own, lax.ppermute(w_own, "c", PAIR), w_pair, lax.ppermute(w_pair, "c", PAIR)], axis=0
-    )
-    d_all = [[d_own, d_pair], [lax.ppermute(d_own, "c", PAIR), lax.ppermute(d_pair, "c", PAIR)]]
+    around, unused = ring(chip_rows, 0)
+    row = jnp.concatenate(around, axis=0)
+    parts, w_late = ring(row, 1, w_mine)
+    w_theirs = lax.ppermute(w_late, "c", PAIR)
 
     ids = of_class(expert_ids.reshape(far * 4, group_rows, -1), core)
     gates = of_class(gate_weights.reshape(far * 4, group_rows, -1), core)
@@ -61,31 +84,43 @@
         values = values.reshape(far, chips, 2, own).transpose(1, 2, 0, 3)
         return values.reshape(class_rows)
 
+    def by_arrival(values):
+        values = values.reshape(far, lax.axis_size("x"), lax.axis_size("y"), 2, own)
+        values = jnp.roll(values, -lax.axis_index("x"), axis=1)
+        values = jnp.roll(values, -lax.axis_index("y"), axis=2)
+        x_first = values.transpose(2, 1, 3, 0, 4)
+        y_first = values.transpose(1, 2, 3, 0, 4)
+        return jnp.where(first, x_first, y_first).reshape(class_rows)
+
     slot_index = jnp.arange(class_slots, dtype=jnp.int32)
     hits, combine = [], []
     for expert in (plane_index * 2 + core, plane_index * 2 + 1 - core):
         slots, weights = routing(ids, gates, capacity, expert)
-        hit = by_row(slots)[:, None] == slot_index[None, :]
-        hits.append(hit.astype(jnp.bfloat16))
-        combine.append(jnp.where(hit, by_row(weights)[:, None], 0.0).astype(jnp.bfloat16))
+        hits.append((by_arrival(slots)[:, None] == slot_index[None, :]).astype(jnp.bfloat16))
+        target = by_row(slots)[:, None] == slot_index[None, :]
+        combine.append(jnp.where(target, by_row(weights)[:, None], 0.0).astype(jnp.bfloat16))
     combine = jnp.concatenate(combine, axis=1)
 
-    both = lax.dot_general(
-        w_all, every, (((1,), (1,)), ((), ())), preferred_element_type=jnp.float32
-    )
-    both = both.reshape(2, 2, 2, units, class_rows)
-    hidden = (jax.nn.silu(both[:, :, 0]) * both[:, :, 1]).astype(jnp.bfloat16)
+    contract = (((1,), (1,)), ((), ()))
+    both = [
+        jnp.concatenate(
+            [lax.dot_general(w, t, contract, preferred_element_type=jnp.float32) for t in parts],
+            axis=1,
+        ).reshape(2, 2, units, class_rows)
+        for w in (w_mine, w_theirs)
+    ]
+    hidden = [(jax.nn.silu(b[:, 0]) * b[:, 1]).astype(jnp.bfloat16) for b in both]
+    d_late, hidden = lax.optimization_barrier((d_mine, hidden))
+    d_theirs = lax.ppermute(d_late, "c", PAIR)
 
     outputs = []
     for e in range(2):
         picked = lax.dot_general(
-            hidden[:, e].reshape(2 * units, class_rows),
+            hidden[e].reshape(2 * units, class_rows),
             hits[e],
             (((1,), (0,)), ((), ())),
             preferred_element_type=jnp.float32,
         ).astype(jnp.bfloat16)
-        picked = picked.reshape(2, units, class_slots)
-        picked = jnp.where(p == 0, picked, picked[::-1]).reshape(2 * units, class_slots)
         all_hidden = lax.all_gather(picked, ("zh", "k"), axis=0, tiled=True)
         outputs.append(
             jnp.concatenate(
@@ -93,7 +128,7 @@
                     lax.dot_general(
                         all_hidden, d, (((0,), (0,)), ((), ())), preferred_element_type=jnp.float32
                     ).astype(jnp.bfloat16)
-                    for d in d_all[e]
+                    for d in (d_mine, d_theirs)[e]
                 ],
                 axis=1,
             )
@@ -112,9 +147,7 @@
     recv = lax.all_to_all(send, ("zh", "k", "c"), split_axis=0, concat_axis=0, tiled=True)
     recv = recv.reshape(far, 2, 2, own, features)
     recv = lax.dynamic_index_in_dim(recv, k, 2, keepdims=False)
-    recv = recv.reshape(far, 2, own, 2, features // 2)
-    recv = jnp.where(p == 0, recv, recv[:, :, :, ::-1])
-    return recv.transpose(2, 0, 1, 3, 4).reshape(own, width)
+    return recv.transpose(2, 0, 1, 3).reshape(own, width)
 
 
 def solution(mesh):

time: 296 us -> 314 us (1.061)
  waiting for transfers between devices: 110 us -> 91.9 us
  starting transfers between devices: 51.8 us -> 65.5 us
  matrix products: 22.9 us -> 36 us
  blocking collectives: 87.1 us -> 91.3 us
    ppermute x6 -> x10, waiting for transfers between devices: 82.8 us -> 37.8 us  [the longest x8 37.8 us: turned(): return lax.ppermute(block, CHIP, perm)]
    all_gather x1 -> x2, waiting for transfers between devices: 0.02 us -> 26.1 us  [the longest x1 21.1 us: local(): w_mine = lax.all_gather(gate_up[0], 'p', axis=0, tiled=False)]
    ppermute x6 -> x10, starting transfers between devices: 14.1 us -> 31.4 us  [the longest x8 26 us: turned(): return lax.ppermute(block, CHIP, perm)]
    dot_general x3 -> x10, matrix products: 14.8 us -> 29.2 us  [the longest x8 28.5 us: local(): lax.dot_general(w, t, contract, preferred_element_type=jnp.float32)]
    all_to_all x1, starting transfers between devices: 11.6 us -> 7.18 us  [local(): lax.all_to_all(summed, PLANE, split_axis=0, concat_axis=0, tiled=True)]
    all_gather x2, blocking collectives: 52.1 us -> 56.4 us  [local(): all_hidden = lax.all_gather(picked, ('zh', 'k'), axis=0, tiled=True)]
  transfers between devices with their start and end apart: 10 -> 15, of which waited for: 5 -> 12; matrix products, arithmetic and copies ran while one was open for 9% -> 14% of each run, Pallas kernels for 0% -> 0%
where the time goes in v4:
time: 314 us; the launch traced here: 313 us
  waiting for transfers between devices  91.9 us (29%)
  blocking collectives  91.3 us (29%)
  starting transfers between devices  65.5 us (21%)
  matrix products  36 us (11%)
  between operations  14.2 us (5%)
  other arithmetic  7.56 us (2%)
  local copies, waits for them, and re-layouts  6.58 us (2%)
    all_gather x2, blocking collectives, local(): all_hidden = lax.all_gather(picked, ('zh', 'k'), axis=0, tiled=True)  56.4 us
    ppermute x8, waiting for transfers between devices, turned(): return lax.ppermute(block, CHIP, perm)  37.8 us
    all_gather x1, blocking collectives, local(): line = lax.all_gather(tokens, LINE, axis=0, tiled=False)  34.8 us
    dot_general x8, matrix products, local(): lax.dot_general(w, t, contract, preferred_element_type=jnp.float32)  28.5 us
    ppermute x8, starting transfers between devices, turned(): return lax.ppermute(block, CHIP, perm)  26 us
    all_gather x1, waiting for transfers between devices, local(): w_mine = lax.all_gather(gate_up[0], 'p', axis=0, tiled=False)  21.1 us
    all_to_all x1, starting transfers between devices, local(): lax.all_to_all(send, ('zh', 'k', 'c'), split_axis=0, concat_axis=0, tiled...  17.4 us
    all_to_all x1, waiting for transfers between devices, local(): lax.all_to_all(send, ('zh', 'k', 'c'), split_axis=0, concat_axis=0, tiled...  16.1 us
  transfers between devices with their start and end apart: 15, of which 12 were waited for; matrix products, arithmetic and copies ran while one was open for 14% of the time, Pallas kernels for 0%

profile of v4, /device:TPU:1, one launch (start us, length us, event | category | flops | bytes accessed | tf_op | source)
XLA Modules:
  0.0 313.0 jit_solution(14333581164385653865)
XLA Ops:
  6.5 34.8 %all-gather.1 = bf16[16,4,7168]{2,1,0:T(4,128)(2,1)S(1)} all-gather(bf16[1,4,7168]{2,1,0:T(4,128)(2,1)} %bitcast.158), channel_id=2, replica_groups=mesh['zh'=4,'k'=2,'p'=2,'x'=4,'y'=4,'c'=2] {'zh','k','p'}, dimensions={0}, use_global_device_ids=true | all-gather | bytes 974848 | tf_op jit(solution)/shard_map/all_gather | solution.py:64
  41.5 9.5 %collective-permute-start = (bf16[4,4,7168]{2,1,0:T(4,128)(2,1)S(1)}, bf16[4,4,7168]{2,1,0:T(4,128)(2,1)S(1)}, u32[]{:S(2)}, u32[]{:S(2)}) collective-permute-start(bf16[4,4,7168]{2,1,0:T(4,128)(2,1)S(1)} %dynamic-slice_bitcast_fusion), channel_id=1, source_target_pairs={{0,1},{1,0},{2,3},{3,2},{4,5},{5,4},{6,7},{7,6},{8,9},{9,8},{10,11... | collective-permute-start | bytes 688136 | tf_op jit(solution)/shard_map/ppermute | solution.py:66
  52.7 4.6 %collective-permute-start.1 = (bf16[32,7168]{1,0:T(8,128)(2,1)S(1)}, bf16[32,7168]{1,0:T(8,128)(2,1)S(1)}, u32[]{:S(2)}, u32[]{:S(2)}) collective-permute-start(bf16[32,7168]{1,0:T(8,128)(2,1)S(1)} %reshape.135), channel_id=1, source_target_pairs={{0,24},{1,7},{2,26},{3,1},{4,28},{5,3},{6,30},{7,5},{8,0},{9,15},{... | collective-permute-start | bytes 1376264 | tf_op jit(solution)/shard_map/ppermute | solution.py:23
  59.3 8.8 %collective-permute-done.2 = bf16[32,7168]{1,0:T(8,128)(2,1)S(1)} collective-permute-done((bf16[32,7168]{1,0:T(8,128)(2,1)S(1)}, bf16[32,7168]{1,0:T(8,128)(2,1)S(1)}, u32[]{:S(2)}, u32[]{:S(2)}) %collective-permute-start.2) | collective-permute-done | bytes 458784 | tf_op jit(solution)/shard_map/ppermute | solution.py:23
  70.1 4.6 %collective-permute-start.4 = (bf16[16,7168]{1,0:T(8,128)(2,1)S(1)}, bf16[16,7168]{1,0:T(8,128)(2,1)S(1)}, u32[]{:S(2)}, u32[]{:S(2)}) collective-permute-start(bf16[16,7168]{1,0:T(8,128)(2,1)S(1)} %slice.33), channel_id=1, source_target_pairs={{0,24},{1,7},{2,26},{3,1},{4,28},{5,3},{6,30},{7,5},{8,0},{9,15},{... | collective-permute-start | bytes 688136 | tf_op jit(solution)/shard_map/ppermute | solution.py:23
  77.7 4.1 %collective-permute-start.5 = (bf16[128,7168]{1,0:T(8,128)(2,1)S(1)}, bf16[128,7168]{1,0:T(8,128)(2,1)S(1)}, u32[]{:S(2)}, u32[]{:S(2)}) collective-permute-start(bf16[128,7168]{1,0:T(8,128)(2,1)S(1)} %constant_dynamic-update-slice_fusion), channel_id=1, source_target_pairs={{0,6},{1,25},{2,0},{3,27},{4,2},{5,29},{6,4},{7,31},{8,14},{9,1},{... | collective-permute-start | bytes 5505032 | tf_op jit(solution)/shard_map/ppermute | solution.py:23
  83.7 18.3 %collective-permute-done.5 = bf16[128,7168]{1,0:T(8,128)(2,1)S(1)} collective-permute-done((bf16[128,7168]{1,0:T(8,128)(2,1)S(1)}, bf16[128,7168]{1,0:T(8,128)(2,1)S(1)}, u32[]{:S(2)}, u32[]{:S(2)}) %collective-permute-start.5) | collective-permute-done | bytes 1835040 | tf_op jit(solution)/shard_map/ppermute | solution.py:23
  102.0 5.3 %collective-permute-done.6 = bf16[128,7168]{1,0:T(8,128)(2,1)} collective-permute-done((bf16[128,7168]{1,0:T(8,128)(2,1)S(1)}, bf16[128,7168]{1,0:T(8,128)(2,1)}, u32[]{:S(2)}, u32[]{:S(2)}) %collective-permute-start.6) | collective-permute-done | bytes 1835040 | tf_op jit(solution)/shard_map/ppermute | solution.py:23
  107.3 21.1 %all-gather.7.cloned.1.call-done = bf16[2,2,96,7168]{3,2,1,0:T(8,128)(2,1)} async-done(((bf16[1,2,96,7168]{3,2,1,0:T(8,128)(2,1)}), bf16[2,2,96,7168]{3,2,1,0:T(8,128)(2,1)}) %all-gather.7.cloned.1.call-update) | async-done | bytes 5505040 | tf_op jit(solution)/shard_map/all_gather | solution.py:70
  137.5 3.1 collective-permute-start.7
  140.7 3.8 %collective-permute-start.8 = (bf16[64,7168]{1,0:T(8,128)(2,1)S(1)}, bf16[64,7168]{1,0:T(8,128)(2,1)S(1)}, u32[]{:S(2)}, u32[]{:S(2)}) collective-permute-start(bf16[64,7168]{1,0:T(8,128)(2,1)S(1)} %slice.27), channel_id=1, source_target_pairs={{0,6},{1,25},{2,0},{3,27},{4,2},{5,29},{6,4},{7,31},{8,14},{9,1},{... | collective-permute-start | bytes 2752520 | tf_op jit(solution)/shard_map/ppermute | solution.py:23
  144.5 4.9 %convolution_bitcast_fusion = f32[384,128]{0,1:T(8,128)S(1)} fusion(bf16[128,7168]{1,0:T(8,128)(2,1)} %collective-permute-done.6, bf16[384,7168]{1,0:T(8,128)(2,1)} %bitcast.137), kind=kOutput, calls=%fused_computation.13 | convolution fusion | flops 704643072 | bytes 7536640 | tf_op jit(solution)/shard_map/dot_general | solution.py:107
  157.7 4.9 %fusion.33 = f32[384,128]{0,1:T(8,128)S(1)} fusion(bf16[384,7168]{1,0:T(8,128)(2,1)} %collective-permute-done.9, bf16[128,7168]{1,0:T(8,128)(2,1)} %copy-done.3), kind=kOutput, calls=%fused_computation.93 | convolution fusion | flops 704643072 | bytes 7536640 | tf_op jit(solution)/shard_map/dot_general | solution.py:107
  162.5 4.4 %fusion.34 = f32[384,128]{0,1:T(8,128)S(1)} fusion(bf16[384,7168]{1,0:T(8,128)(2,1)} %collective-permute-done.9, bf16[128,7168]{1,0:T(8,128)(2,1)S(1)} %collective-permute-done.5), kind=kOutput, calls=%fused_computation.94 | convolution fusion | flops 704643072 | bytes 7536640 | tf_op jit(solution)/shard_map/dot_general | solution.py:107
  167.0 4.3 %fusion.35 = f32[384,128]{0,1:T(8,128)S(1)} fusion(bf16[384,7168]{1,0:T(8,128)(2,1)} %collective-permute-done.9, bf16[128,7168]{1,0:T(8,128)(2,1)S(1)} %copy-done.2), kind=kOutput, calls=%fused_computation.95 | convolution fusion | flops 704643072 | bytes 7536640 | tf_op jit(solution)/shard_map/dot_general | solution.py:107
  171.3 4.9 %fusion.36 = f32[384,128]{0,1:T(8,128)S(1)} fusion(bf16[384,7168]{1,0:T(8,128)(2,1)} %collective-permute-done.9, bf16[128,7168]{1,0:T(8,128)(2,1)} %collective-permute-done.6), kind=kOutput, calls=%fused_computation.96 | convolution fusion | flops 704643072 | bytes 7536640 | tf_op jit(solution)/shard_map/dot_general | solution.py:107
  176.8 5.1 %all-gather.5.cloned.1.call-done = bf16[2,1536,448]{1,2,0:T(8,128)(2,1)} async-done(((bf16[1,1536,448]{1,2,0:T(8,128)(2,1)}), bf16[2,1536,448]{1,2,0:T(8,128)(2,1)}) %all-gather.5.cloned.1.call-update) | async-done | bytes 2752528 | tf_op jit(solution)/shard_map/all_gather | solution.py:71
  181.9 2.8 collective-permute-start.10
  189.6 29.3 %all_gather.23 = bf16[1536,192]{1,0:T(8,128)(2,1)S(1)} all-gather(bf16[192,192]{1,0:T(8,128)(2,1)S(1)} %convolution_convert_fusion.1), channel_id=1, replica_groups=mesh['zh'=4,'k'=2,'p'=2,'x'=4,'y'=4,'c'=2] {'zh','k'}, dimensions={0}, use_global_device_ids=true | all-gather | bytes 663552 | tf_op jit(solution)/shard_map/all_gather | solution.py:124
  218.9 27.1 %all_gather.22 = bf16[1536,192]{1,0:T(8,128)(2,1)S(1)} all-gather(bf16[192,192]{1,0:T(8,128)(2,1)S(1)} %convolution_convert_fusion.2), channel_id=1, replica_groups=mesh['zh'=4,'k'=2,'p'=2,'x'=4,'y'=4,'c'=2] {'zh','k'}, dimensions={0}, use_global_device_ids=true | all-gather | bytes 663552 | tf_op jit(solution)/shard_map/all_gather | solution.py:124
  252.9 7.2 %all-to-all-start = ((bf16[16,32,896]{2,1,0:T(8,128)(2,1)}), bf16[16,32,896]{2,1,0:T(8,128)(2,1)S(1)}, u32[]{:S(2)}, u32[]{:S(2)}) async-start(bf16[16,32,896]{2,1,0:T(8,128)(2,1)} %bitcast.39), calls=%async_computation | async-start | bytes 1835008 | tf_op jit(solution)/shard_map/all_to_all | solution.py:139
  260.3 10.9 %all-to-all-done = bf16[16,32,896]{2,1,0:T(8,128)(2,1)S(1)} async-done(((bf16[16,32,896]{2,1,0:T(8,128)(2,1)}), bf16[16,32,896]{2,1,0:T(8,128)(2,1)S(1)}, u32[]{:S(2)}, u32[]{:S(2)}) %all-to-all-start) | async-done | bytes 917536 | tf_op jit(solution)/shard_map/all_to_all | solution.py:139
  272.0 17.4 %all-to-all-start.1 = ((bf16[16,4,896]{2,1,0:T(4,128)(2,1)}), bf16[16,4,896]{2,1,0:T(4,128)(2,1)S(1)}, u32[]{:S(2)}, u32[]{:S(2)}) async-start(bf16[16,4,896]{2,1,0:T(4,128)(2,1)} %bitcast_select_fusion.2), calls=%async_computation.1 | async-start | bytes 229376 | tf_op jit(solution)/shard_map/all_to_all | solution.py:147
  289.4 16.1 %all-to-all-done.1 = bf16[16,4,896]{2,1,0:T(4,128)(2,1)S(1)} async-done(((bf16[16,4,896]{2,1,0:T(4,128)(2,1)}), bf16[16,4,896]{2,1,0:T(4,128)(2,1)S(1)}, u32[]{:S(2)}, u32[]{:S(2)}) %all-to-all-start.1) | async-done | bytes 114720 | tf_op jit(solution)/shard_map/all_to_all | solution.py:147
  (122 shorter events, 41.6 us)
Async XLA Ops:
  6.5 121.9 %all-gather.7.cloned.1.call-start = ((), (), s32[]{:S(2)}) async-start(), calls=%async_computation.3 | async-start | bytes 8257536 | tf_op jit(solution)/shard_map/all_gather | solution.py:70
  41.5 10.6 %collective-permute-start = (bf16[4,4,7168]{2,1,0:T(4,128)(2,1)S(1)}, bf16[4,4,7168]{2,1,0:T(4,128)(2,1)S(1)}, u32[]{:S(2)}, u32[]{:S(2)}) collective-permute-start(bf16[4,4,7168]{2,1,0:T(4,128)(2,1)S(1)} %dynamic-slice_bitcast_fusion), channel_id=1, source_target_pairs={{0,1},{1,0},{2,3},{3,2},{4,5},{5,4},{6,7},{7,6},{8,9},{9,8},{10,11... | collective-permute-start | bytes 688136 | tf_op jit(solution)/shard_map/ppermute | solution.py:66
  51.0 130.9 %all-gather.5.cloned.1.call-start = ((), (), s32[]{:S(2)}) async-start(), calls=%async_computation.2 | async-start | bytes 4128768 | tf_op jit(solution)/shard_map/all_gather | solution.py:71
  52.7 17.3 %collective-permute-start.1 = (bf16[32,7168]{1,0:T(8,128)(2,1)S(1)}, bf16[32,7168]{1,0:T(8,128)(2,1)S(1)}, u32[]{:S(2)}, u32[]{:S(2)}) collective-permute-start(bf16[32,7168]{1,0:T(8,128)(2,1)S(1)} %reshape.135), channel_id=1, source_target_pairs={{0,24},{1,7},{2,26},{3,1},{4,28},{5,3},{6,30},{7,5},{8,0},{9,15},{... | collective-permute-start | bytes 1376264 | tf_op jit(solution)/shard_map/ppermute | solution.py:23
  57.4 10.7 %collective-permute-start.2 = (bf16[32,7168]{1,0:T(8,128)(2,1)S(1)}, bf16[32,7168]{1,0:T(8,128)(2,1)S(1)}, u32[]{:S(2)}, u32[]{:S(2)}) collective-permute-start(bf16[32,7168]{1,0:T(8,128)(2,1)S(1)} %reshape.135), channel_id=1, source_target_pairs={{0,8},{1,3},{2,10},{3,5},{4,12},{5,7},{6,14},{7,1},{8,16},{9,11},{... | collective-permute-start | bytes 1376264 | tf_op jit(solution)/shard_map/ppermute | solution.py:23
  68.1 8.3 %collective-permute-start.3 = (bf16[16,7168]{1,0:T(8,128)(2,1)S(1)}, bf16[16,7168]{1,0:T(8,128)(2,1)S(1)}, u32[]{:S(2)}, u32[]{:S(2)}) collective-permute-start(bf16[16,7168]{1,0:T(8,128)(2,1)S(1)} %slice.32), channel_id=1, source_target_pairs={{0,8},{1,3},{2,10},{3,5},{4,12},{5,7},{6,14},{7,1},{8,16},{9,11},{... | collective-permute-start | bytes 688136 | tf_op jit(solution)/shard_map/ppermute | solution.py:23
  70.1 7.5 %collective-permute-start.4 = (bf16[16,7168]{1,0:T(8,128)(2,1)S(1)}, bf16[16,7168]{1,0:T(8,128)(2,1)S(1)}, u32[]{:S(2)}, u32[]{:S(2)}) collective-permute-start(bf16[16,7168]{1,0:T(8,128)(2,1)S(1)} %slice.33), channel_id=1, source_target_pairs={{0,24},{1,7},{2,26},{3,1},{4,28},{5,3},{6,30},{7,5},{8,0},{9,15},{... | collective-permute-start | bytes 688136 | tf_op jit(solution)/shard_map/ppermute | solution.py:23
  74.7 58.9 %copy-start.14 = (s32[32]{0:T(128)S(1)}, s32[32]{0:T(128)}, u32[]{:S(2)}) copy-start(s32[32]{0:T(128)} %param.15) | copy-start | bytes 388
  77.7 24.4 %copy-start.3 = (bf16[128,7168]{1,0:T(8,128)(2,1)}, bf16[128,7168]{1,0:T(8,128)(2,1)S(1)}, u32[]{:S(2)}) copy-start(bf16[128,7168]{1,0:T(8,128)(2,1)S(1)} %constant_dynamic-update-slice_fusion) | copy-start | bytes 5505028
  77.7 24.4 %collective-permute-start.5 = (bf16[128,7168]{1,0:T(8,128)(2,1)S(1)}, bf16[128,7168]{1,0:T(8,128)(2,1)S(1)}, u32[]{:S(2)}, u32[]{:S(2)}) collective-permute-start(bf16[128,7168]{1,0:T(8,128)(2,1)S(1)} %constant_dynamic-update-slice_fusion), channel_id=1, source_target_pairs={{0,6},{1,25},{2,0},{3,27},{4,2},{5,29},{6,4},{7,31},{8,14},{9,1},{... | collective-permute-start | bytes 5505032 | tf_op jit(solution)/shard_map/ppermute | solution.py:23
  81.8 25.6 %collective-permute-start.6 = (bf16[128,7168]{1,0:T(8,128)(2,1)S(1)}, bf16[128,7168]{1,0:T(8,128)(2,1)}, u32[]{:S(2)}, u32[]{:S(2)}) collective-permute-start(bf16[128,7168]{1,0:T(8,128)(2,1)S(1)} %constant_dynamic-update-slice_fusion), channel_id=1, source_target_pairs={{0,2},{1,9},{2,4},{3,11},{4,6},{5,13},{6,0},{7,15},{8,10},{9,17},{... | collective-permute-start | bytes 5505032 | tf_op jit(solution)/shard_map/ppermute | solution.py:23
  128.4 29.2 %collective-permute-start.9 = (bf16[384,7168]{1,0:T(8,128)(2,1)}, bf16[384,7168]{1,0:T(8,128)(2,1)}, u32[]{:S(2)}, u32[]{:S(2)}) collective-permute-start(bf16[384,7168]{1,0:T(8,128)(2,1)} %bitcast.136), channel_id=1, source_target_pairs={{0,1},{1,0},{2,3},{3,2},{4,5},{5,4},{6,7},{7,6},{8,9},{9,8},{10,11... | collective-permute-start | bytes 16515080 | tf_op jit(solution)/shard_map/ppermute | solution.py:78
  137.5 15.6 %collective-permute-start.7 = (bf16[64,7168]{1,0:T(8,128)(2,1)S(1)}, bf16[64,7168]{1,0:T(8,128)(2,1)S(1)}, u32[]{:S(2)}, u32[]{:S(2)}) collective-permute-start(bf16[64,7168]{1,0:T(8,128)(2,1)S(1)} %slice.26), channel_id=1, source_target_pairs={{0,2},{1,9},{2,4},{3,11},{4,6},{5,13},{6,0},{7,15},{8,10},{9,17},{... | collective-permute-start | bytes 2752520 | tf_op jit(solution)/shard_map/ppermute | solution.py:23
  140.7 14.8 %collective-permute-start.8 = (bf16[64,7168]{1,0:T(8,128)(2,1)S(1)}, bf16[64,7168]{1,0:T(8,128)(2,1)S(1)}, u32[]{:S(2)}, u32[]{:S(2)}) collective-permute-start(bf16[64,7168]{1,0:T(8,128)(2,1)S(1)} %slice.27), channel_id=1, source_target_pairs={{0,6},{1,25},{2,0},{3,27},{4,2},{5,29},{6,4},{7,31},{8,14},{9,1},{... | collective-permute-start | bytes 2752520 | tf_op jit(solution)/shard_map/ppermute | solution.py:23
  176.2 9.0 %copy-start.7 = (s32[4,4,4,2,4]{0,4,3,2,1:T(4,128)S(1)}, s32[4,4,4,2,4]{0,4,3,2,1:T(4,128)}, u32[]{:S(2)}) copy-start(s32[4,4,4,2,4]{0,4,3,2,1:T(4,128)} %get-tuple-element.27) | copy-start | bytes 6148
  176.5 9.3 %copy-start.6 = (s32[4,128]{0,1:T(8,128)S(1)}, s32[4,128]{0,1:T(8,128)}, u32[]{:S(2)}) copy-start(s32[4,128]{0,1:T(8,128)} %copy-done.5) | copy-start | bytes 6148
  176.5 9.3 %copy-start.9 = (pred[4,128]{0,1:T(8,128)(4,1)S(1)}, pred[4,128]{0,1:T(8,128)(4,1)}, u32[]{:S(2)}) copy-start(pred[4,128]{0,1:T(8,128)(4,1)} %copy-done.8) | copy-start | bytes 1540
  176.5 9.3 %copy-start.13 = (s32[4]{0:T(128)S(1)}, s32[4]{0:T(128)}, u32[]{:S(2)}) copy-start(s32[4]{0:T(128)} %copy-done.12) | copy-start | bytes 52
  176.5 11.0 %copy-start.11 = (bf16[4,128]{1,0:T(4,128)(2,1)S(1)}, bf16[4,128]{1,0:T(4,128)(2,1)}, u32[]{:S(2)}) copy-start(bf16[4,128]{1,0:T(4,128)(2,1)} %get-tuple-element.20) | copy-start | bytes 3076
  176.5 11.7 %copy-start.10 = (bf16[4,128]{1,0:T(4,128)(2,1)S(1)}, bf16[4,128]{1,0:T(4,128)(2,1)}, u32[]{:S(2)}) copy-start(bf16[4,128]{1,0:T(4,128)(2,1)} %get-tuple-element.19) | copy-start | bytes 3076
  181.9 65.4 %collective-permute-start.10 = (bf16[2,1536,448]{1,2,0:T(8,128)(2,1)}, bf16[2,1536,448]{1,2,0:T(8,128)(2,1)}, u32[]{:S(2)}, u32[]{:S(2)}) collective-permute-start(bf16[2,1536,448]{1,2,0:T(8,128)(2,1)} %all-gather.5.cloned.1.call-done), channel_id=1, source_target_pairs={{0,1},{1,0},{2,3},{3,2},{4,5},{5,4},{6,7},{7,6},{8,9},{9,8},{10,11... | collective-permute-start | bytes 8257544 | tf_op jit(solution)/shard_map/ppermute | solution.py:114
  187.5 58.5 %copy-start.15 = (bf16[2,1536,448]{1,2,0:T(8,128)(2,1)S(1)}, bf16[2,1536,448]{1,2,0:T(8,128)(2,1)}, u32[]{:S(2)}) copy-start(bf16[2,1536,448]{1,2,0:T(8,128)(2,1)} %all-gather.5.cloned.1.call-done) | copy-start | bytes 8257540
  252.9 18.2 %all-to-all-start = ((bf16[16,32,896]{2,1,0:T(8,128)(2,1)}), bf16[16,32,896]{2,1,0:T(8,128)(2,1)S(1)}, u32[]{:S(2)}, u32[]{:S(2)}) async-start(bf16[16,32,896]{2,1,0:T(8,128)(2,1)} %bitcast.39), calls=%async_computation | async-start | bytes 1835008 | tf_op jit(solution)/shard_map/all_to_all | solution.py:139
  272.0 33.5 %all-to-all-start.1 = ((bf16[16,4,896]{2,1,0:T(4,128)(2,1)}), bf16[16,4,896]{2,1,0:T(4,128)(2,1)S(1)}, u32[]{:S(2)}, u32[]{:S(2)}) async-start(bf16[16,4,896]{2,1,0:T(4,128)(2,1)} %bitcast_select_fusion.2), calls=%async_computation.1 | async-start | bytes 229376 | tf_op jit(solution)/shard_map/all_to_all | solution.py:147
  (7 other events, 37.5 us)
Sparse Core Ops, SparseCore 0:
  51.1 77.2 all-gather.6
  131.1 50.6 all-gather.4

commit v5 on v3

--- a/solution.py
+++ b/solution.py
@@ -36,23 +36,37 @@
             lax.dynamic_index_in_dim(values, p, 2, keepdims=False), which, 1, keepdims=False
         )
 
+    units = gate_up.shape[2]
+    w_own = gate_up[0].reshape(2 * units, width)
+    gate_pair = lax.ppermute(w_own[:units], "p", PAIR)
     line = lax.all_gather(tokens, LINE, axis=0, tiled=False)
+    line, gate_pair = lax.optimization_barrier((line, gate_pair))
     mine = of_class(line, core)
     got = lax.ppermute(of_class(line, 1 - core), "c", PAIR)
     first = core == 0
+    up_pair = lax.ppermute(w_own[units:], "p", PAIR)
+
     chip_rows = jnp.stack([jnp.where(first, mine, got), jnp.where(first, got, mine)])
     chip_rows = chip_rows.reshape(2 * far * own, width)
     every = lax.all_gather(chip_rows, PLANE, axis=0, tiled=True)
 
-    units = gate_up.shape[2]
-    w_own = gate_up[0].reshape(2 * units, width)
-    w_pair = lax.ppermute(w_own, "p", PAIR)
+    w_all = lax.optimization_barrier(
+        jnp.concatenate(
+            [
+                w_own,
+                lax.ppermute(w_own, "c", PAIR),
+                gate_pair,
+                up_pair,
+                lax.ppermute(gate_pair, "c", PAIR),
+                lax.ppermute(up_pair, "c", PAIR),
+            ],
+            axis=0,
+        )
+    )
     d_own = down[0]
-    d_pair = lax.ppermute(d_own, "p", PAIR)
-    w_all = jnp.concatenate(
-        [w_own, lax.ppermute(w_own, "c", PAIR), w_pair, lax.ppermute(w_pair, "c", PAIR)], axis=0
-    )
-    d_all = [[d_own, d_pair], [lax.ppermute(d_own, "c", PAIR), lax.ppermute(d_pair, "c", PAIR)]]
+    d_own_other = lax.ppermute(d_own, "c", PAIR)
+    d_later, up_pair = lax.optimization_barrier((d_own, up_pair))
+    d_pair = lax.ppermute(d_later, "p", PAIR)
 
     ids = of_class(expert_ids.reshape(far * 4, group_rows, -1), core)
     gates = of_class(gate_weights.reshape(far * 4, group_rows, -1), core)
@@ -75,6 +89,8 @@
     )
     both = both.reshape(2, 2, 2, units, class_rows)
     hidden = (jax.nn.silu(both[:, :, 0]) * both[:, :, 1]).astype(jnp.bfloat16)
+    d_pair, hidden = lax.optimization_barrier((d_pair, hidden))
+    d_all = [[d_own, d_pair], [d_own_other, lax.ppermute(d_pair, "c", PAIR)]]
 
     outputs = []
     for e in range(2):

time: 296 us -> 306 us (1.034)
  waiting for transfers between devices: 110 us -> 74.9 us
  blocking collectives: 87.1 us -> 117 us
  local copies, waits for them, and re-layouts: 5.09 us -> 20.6 us
  matrix products: 22.9 us -> 19.6 us
    ppermute x5 -> x7, waiting for transfers between devices: 82.8 us -> 22.2 us  [the longest x1 22.2 us: local(): up_pair = lax.ppermute(w_own[units:], 'p', PAIR)]
    all_gather x1, blocking collectives: 35 us -> 59.6 us  [local(): line = lax.all_gather(tokens, LINE, axis=0, tiled=False)]
    all_gather x1, waiting for transfers between devices: 0.02 us -> 24.6 us  [local(): every = lax.all_gather(chip_rows, PLANE, axis=0, tiled=True)]
    unnamed x4 -> x17, local copies, waits for them, and re-layouts: 0.01 us -> 11.3 us
    ppermute x5 -> x7, starting transfers between devices: 11.8 us -> 18 us  [the longest x1 4.36 us: local(): gate_pair = lax.ppermute(w_own[:units], 'p', PAIR)]
    all_to_all x1, starting transfers between devices: 11.6 us -> 5.82 us  [local(): lax.all_to_all(summed, PLANE, split_axis=0, concat_axis=0, tiled=True)]
    all_gather x2, blocking collectives: 52.1 us -> 57.8 us  [local(): all_hidden = lax.all_gather(picked, ('zh', 'k'), axis=0, tiled=True)]
    dot_general x1, matrix products: 14.1 us -> 10.8 us  [local(): lax.dot_general(w_all, every, (((1,), (1,)), ((), ())), preferred_element...]
  transfers between devices with their start and end apart: 10 -> 12, of which waited for: 5 -> 5; matrix products, arithmetic and copies ran while one was open for 9% -> 12% of each run, Pallas kernels for 0% -> 0%
where the time goes in v5:
time: 306 us; the launch traced here: 305 us
  blocking collectives  117 us (38%)
  waiting for transfers between devices  74.9 us (24%)
  starting transfers between devices  52.5 us (17%)
  local copies, waits for them, and re-layouts  20.6 us (7%)
  matrix products  19.6 us (6%)
  between operations  13.8 us (5%)
  other arithmetic  6.08 us (2%)
    all_gather x1, blocking collectives, local(): line = lax.all_gather(tokens, LINE, axis=0, tiled=False)  59.6 us
    all_gather x2, blocking collectives, local(): all_hidden = lax.all_gather(picked, ('zh', 'k'), axis=0, tiled=True)  57.8 us
    all_gather x1, waiting for transfers between devices, local(): every = lax.all_gather(chip_rows, PLANE, axis=0, tiled=True)  24.6 us
    ppermute x1, waiting for transfers between devices, local(): up_pair = lax.ppermute(w_own[units:], 'p', PAIR)  22.2 us
    all_to_all x1, starting transfers between devices, local(): lax.all_to_all(send, ('zh', 'k', 'c'), split_axis=0, concat_axis=0, tiled...  17.3 us
    all_to_all x1, waiting for transfers between devices, local(): lax.all_to_all(send, ('zh', 'k', 'c'), split_axis=0, concat_axis=0, tiled...  16.1 us
    unnamed x17, local copies, waits for them, and re-layouts  11.3 us
    all_to_all x1, waiting for transfers between devices, local(): lax.all_to_all(summed, PLANE, split_axis=0, concat_axis=0, tiled=True)  10.9 us
  transfers between devices with their start and end apart: 12, of which 5 were waited for; matrix products, arithmetic and copies ran while one was open for 12% of the time, Pallas kernels for 0%

profile of v5, /device:TPU:1, one launch (start us, length us, event | category | flops | bytes accessed | tf_op | source)
XLA Modules:
  0.0 304.9 jit_solution(13426517531470577252)
XLA Ops:
  6.5 3.0 slice_bitcast_fusion
  9.6 4.4 %collective-permute-start.3 = (bf16[96,7168]{1,0:T(8,128)(2,1)S(1)}, bf16[96,7168]{1,0:T(8,128)(2,1)S(1)}, u32[]{:S(2)}, u32[]{:S(2)}) collective-permute-start(bf16[96,7168]{1,0:T(8,128)(2,1)S(1)} %get-tuple-element.19), channel_id=1, source_target_pairs={{0,32},{32,0},{1,33},{33,1},{2,34},{34,2},{3,35},{35,3},{4,36},{36... | collective-permute-start | bytes 4128776 | tf_op jit(solution)/shard_map/ppermute | solution.py:41
  14.0 59.6 %all-gather.1 = bf16[16,4,7168]{2,1,0:T(4,128)(2,1)S(1)} all-gather(bf16[1,4,7168]{2,1,0:T(4,128)(2,1)S(1)} %bitcast.95), channel_id=2, replica_groups=mesh['zh'=4,'k'=2,'p'=2,'x'=4,'y'=4,'c'=2] {'zh','k','p'}, dimensions={0}, use_global_device_ids=true | all-gather | bytes 974848 | tf_op jit(solution)/shard_map/all_gather | solution.py:42
  74.6 9.0 %collective-permute-start.6 = (bf16[4,4,7168]{2,1,0:T(4,128)(2,1)S(1)}, bf16[4,4,7168]{2,1,0:T(4,128)(2,1)S(1)}, u32[]{:S(2)}, u32[]{:S(2)}) collective-permute-start(bf16[4,4,7168]{2,1,0:T(4,128)(2,1)S(1)} %dynamic-slice_bitcast_fusion), channel_id=1, source_target_pairs={{0,1},{1,0},{2,3},{3,2},{4,5},{5,4},{6,7},{7,6},{8,9},{9,8},{10,11... | collective-permute-start | bytes 688136 | tf_op jit(solution)/shard_map/ppermute | solution.py:45
  87.3 2.3 collective-permute-start.2
  89.6 1.9 collective-permute-start
  91.5 2.1 collective-permute-start.7
  101.3 22.2 %collective-permute-done = bf16[96,7168]{1,0:T(8,128)(2,1)} collective-permute-done((bf16[96,7168]{1,0:T(8,128)(2,1)}, bf16[96,7168]{1,0:T(8,128)(2,1)}, u32[]{:S(2)}, u32[]{:S(2)}) %collective-permute-start) | collective-permute-done | bytes 1376288 | tf_op jit(solution)/shard_map/ppermute | solution.py:47
  123.5 2.1 collective-permute-start.1
  125.6 2.9 collective-permute-start.4
  130.5 3.6 %constant_dynamic-update-slice_fusion.4 = bf16[768,7168]{1,0:T(8,128)(2,1)} fusion(bf16[768,7168]{1,0:T(8,128)(2,1)} %constant_dynamic-update-slice_fusion.5, bf16[192,7168]{1,0:T(8,128)(2,1)} %collective-permute-done.2), kind=kLoop, calls=%fused_computation.52 | loop fusion | bytes 5505024
  135.3 2.5 constant_dynamic-update-slice_fusion.2
  140.3 24.6 %all-gather.4.cloned.1.call-done = bf16[512,7168]{1,0:T(8,128)(2,1)} async-done(((bf16[32,7168]{1,0:T(8,128)(2,1)}), bf16[512,7168]{1,0:T(8,128)(2,1)}) %all-gather.4.cloned.1.call-update) | async-done | bytes 7340048 | tf_op jit(solution)/shard_map/all_gather | solution.py:51
  164.9 10.8 %fusion.21 = f32[768,512]{1,0:T(8,128)S(1)} fusion(bf16[768,7168]{1,0:T(8,128)(2,1)} %constant_dynamic-update-slice_fusion, bf16[512,7168]{1,0:T(8,128)(2,1)} %all-gather.4.cloned.1.call-done), kind=kOutput, calls=%fused_computation.63 | convolution fusion | flops 5637144576 | bytes 19922944 | tf_op jit(solution)/shard_map/dot_general | solution.py:87
  176.3 2.6 collective-permute-start.8
  179.3 32.0 %all_gather.19 = bf16[1536,192]{1,0:T(8,128)(2,1)S(1)} all-gather(bf16[192,192]{1,0:T(8,128)(2,1)S(1)} %bitcast.82), channel_id=1, replica_groups=mesh['zh'=4,'k'=2,'p'=2,'x'=4,'y'=4,'c'=2] {'zh','k'}, dimensions={0}, use_global_device_ids=true | all-gather | bytes 663552 | tf_op jit(solution)/shard_map/all_gather | solution.py:105
  211.3 25.8 %all_gather.18 = bf16[1536,192]{1,0:T(8,128)(2,1)S(1)} all-gather(bf16[192,192]{1,0:T(8,128)(2,1)S(1)} %bitcast.83), channel_id=1, replica_groups=mesh['zh'=4,'k'=2,'p'=2,'x'=4,'y'=4,'c'=2] {'zh','k'}, dimensions={0}, use_global_device_ids=true | all-gather | bytes 663552 | tf_op jit(solution)/shard_map/all_gather | solution.py:105
  237.1 2.0 convolution_convert_fusion.3
  239.1 2.0 convolution_convert_fusion.4
  241.1 2.0 convolution_convert_fusion.2
  245.4 5.8 %all-to-all-start = ((bf16[16,32,896]{2,1,0:T(8,128)(2,1)}), bf16[16,32,896]{2,1,0:T(8,128)(2,1)S(1)}, u32[]{:S(2)}, u32[]{:S(2)}) async-start(bf16[16,32,896]{2,1,0:T(8,128)(2,1)} %bitcast.29), calls=%async_computation | async-start | bytes 1835008 | tf_op jit(solution)/shard_map/all_to_all | solution.py:120
  251.4 10.9 %all-to-all-done = bf16[16,32,896]{2,1,0:T(8,128)(2,1)S(1)} async-done(((bf16[16,32,896]{2,1,0:T(8,128)(2,1)}), bf16[16,32,896]{2,1,0:T(8,128)(2,1)S(1)}, u32[]{:S(2)}, u32[]{:S(2)}) %all-to-all-start) | async-done | bytes 917536 | tf_op jit(solution)/shard_map/all_to_all | solution.py:120
  263.1 17.3 %all-to-all-start.1 = ((bf16[16,4,896]{2,1,0:T(4,128)(2,1)}), bf16[16,4,896]{2,1,0:T(4,128)(2,1)S(1)}, u32[]{:S(2)}, u32[]{:S(2)}) async-start(bf16[16,4,896]{2,1,0:T(4,128)(2,1)} %bitcast_select_fusion.2), calls=%async_computation.1 | async-start | bytes 229376 | tf_op jit(solution)/shard_map/all_to_all | solution.py:128
  280.5 16.1 %all-to-all-done.1 = bf16[16,4,896]{2,1,0:T(4,128)(2,1)S(1)} async-done(((bf16[16,4,896]{2,1,0:T(4,128)(2,1)}), bf16[16,4,896]{2,1,0:T(4,128)(2,1)S(1)}, u32[]{:S(2)}, u32[]{:S(2)}) %all-to-all-start.1) | async-done | bytes 114720 | tf_op jit(solution)/shard_map/all_to_all | solution.py:128
  (78 shorter events, 23.5 us)
Async XLA Ops:
  6.5 7.4 %copy-start.4 = (bf16[4,7168]{1,0:T(4,128)(2,1)S(1)}, bf16[4,7168]{1,0:T(4,128)(2,1)}, u32[]{:S(2)}) copy-start(bf16[4,7168]{1,0:T(4,128)(2,1)} %param.6) | copy-start | bytes 172036
  6.5 158.4 %all-gather.4.cloned.1.call-start = ((), (), s32[]{:S(2)}) async-start(), calls=%async_computation.2 | async-start | bytes 7798784 | tf_op jit(solution)/shard_map/all_gather | solution.py:51
  9.6 64.0 %collective-permute-start.3 = (bf16[96,7168]{1,0:T(8,128)(2,1)S(1)}, bf16[96,7168]{1,0:T(8,128)(2,1)S(1)}, u32[]{:S(2)}, u32[]{:S(2)}) collective-permute-start(bf16[96,7168]{1,0:T(8,128)(2,1)S(1)} %get-tuple-element.19), channel_id=1, source_target_pairs={{0,32},{32,0},{1,33},{33,1},{2,34},{34,2},{3,35},{35,3},{4,36},{36... | collective-permute-start | bytes 4128776 | tf_op jit(solution)/shard_map/ppermute | solution.py:41
  73.6 0.9 copy-start.1
  73.6 10.1 %copy-start.2 = (bf16[96,7168]{1,0:T(8,128)(2,1)}, bf16[96,7168]{1,0:T(8,128)(2,1)S(1)}, u32[]{:S(2)}) copy-start(bf16[96,7168]{1,0:T(8,128)(2,1)S(1)} %collective-permute-done.3) | copy-start | bytes 4128772
  74.6 10.1 %collective-permute-start.6 = (bf16[4,4,7168]{2,1,0:T(4,128)(2,1)S(1)}, bf16[4,4,7168]{2,1,0:T(4,128)(2,1)S(1)}, u32[]{:S(2)}, u32[]{:S(2)}) collective-permute-start(bf16[4,4,7168]{2,1,0:T(4,128)(2,1)S(1)} %dynamic-slice_bitcast_fusion), channel_id=1, source_target_pairs={{0,1},{1,0},{2,3},{3,2},{4,5},{5,4},{6,7},{7,6},{8,9},{9,8},{10,11... | collective-permute-start | bytes 688136 | tf_op jit(solution)/shard_map/ppermute | solution.py:45
  84.8 2.5 copy-start
  86.1 9.6 %copy-start.5 = (s32[32]{0:T(128)S(1)}, s32[32]{0:T(128)}, u32[]{:S(2)}) copy-start(s32[32]{0:T(128)} %param.11) | copy-start | bytes 388
  87.3 43.2 %collective-permute-start.2 = (bf16[192,7168]{1,0:T(8,128)(2,1)S(1)}, bf16[192,7168]{1,0:T(8,128)(2,1)}, u32[]{:S(2)}, u32[]{:S(2)}) collective-permute-start(bf16[192,7168]{1,0:T(8,128)(2,1)S(1)} %bitcast.77), channel_id=1, source_target_pairs={{0,1},{1,0},{2,3},{3,2},{4,5},{5,4},{6,7},{7,6},{8,9},{9,8},{10,11... | collective-permute-start | bytes 8257544 | tf_op jit(solution)/shard_map/ppermute | solution.py:57
  89.6 33.9 %collective-permute-start = (bf16[96,7168]{1,0:T(8,128)(2,1)}, bf16[96,7168]{1,0:T(8,128)(2,1)}, u32[]{:S(2)}, u32[]{:S(2)}) collective-permute-start(bf16[96,7168]{1,0:T(8,128)(2,1)} %get-tuple-element.20), channel_id=1, source_target_pairs={{0,32},{32,0},{1,33},{33,1},{2,34},{34,2},{3,35},{35,3},{4,36},{36... | collective-permute-start | bytes 4128776 | tf_op jit(solution)/shard_map/ppermute | solution.py:47
  91.5 149.5 %collective-permute-start.7 = (bf16[1536,448]{0,1:T(8,128)(2,1)}, bf16[1536,448]{0,1:T(8,128)(2,1)}, u32[]{:S(2)}, u32[]{:S(2)}) collective-permute-start(bf16[1536,448]{0,1:T(8,128)(2,1)} %bitcast.10), channel_id=1, source_target_pairs={{0,1},{1,0},{2,3},{3,2},{4,5},{5,4},{6,7},{7,6},{8,9},{9,8},{10,11... | collective-permute-start | bytes 4128776 | tf_op jit(solution)/shard_map/ppermute | solution.py:67
  99.5 26.1 %copy-start.3 = (bf16[96,7168]{1,0:T(8,128)(2,1)S(1)}, bf16[96,7168]{1,0:T(8,128)(2,1)}, u32[]{:S(2)}) copy-start(bf16[96,7168]{1,0:T(8,128)(2,1)} %copy-done.2) | copy-start | bytes 4128772
  123.5 52.5 %collective-permute-start.1 = (bf16[1536,448]{0,1:T(8,128)(2,1)}, bf16[1536,448]{0,1:T(8,128)(2,1)}, u32[]{:S(2)}, u32[]{:S(2)}) collective-permute-start(bf16[1536,448]{0,1:T(8,128)(2,1)} %bitcast.10), channel_id=1, source_target_pairs={{0,32},{32,0},{1,33},{33,1},{2,34},{34,2},{3,35},{35,3},{4,36},{36... | collective-permute-start | bytes 4128776 | tf_op jit(solution)/shard_map/ppermute | solution.py:69
  125.6 12.2 %collective-permute-start.4 = (bf16[96,7168]{1,0:T(8,128)(2,1)S(1)}, bf16[96,7168]{1,0:T(8,128)(2,1)S(1)}, u32[]{:S(2)}, u32[]{:S(2)}) collective-permute-start(bf16[96,7168]{1,0:T(8,128)(2,1)S(1)} %copy-done.3), channel_id=1, source_target_pairs={{0,1},{1,0},{2,3},{3,2},{4,5},{5,4},{6,7},{7,6},{8,9},{9,8},{10,11... | collective-permute-start | bytes 4128776 | tf_op jit(solution)/shard_map/ppermute | solution.py:60
  128.5 10.6 %collective-permute-start.5 = (bf16[96,7168]{1,0:T(8,128)(2,1)}, bf16[96,7168]{1,0:T(8,128)(2,1)S(1)}, u32[]{:S(2)}, u32[]{:S(2)}) collective-permute-start(bf16[96,7168]{1,0:T(8,128)(2,1)} %collective-permute-done), channel_id=1, source_target_pairs={{0,1},{1,0},{2,3},{3,2},{4,5},{5,4},{6,7},{7,6},{8,9},{9,8},{10,11... | collective-permute-start | bytes 4128776 | tf_op jit(solution)/shard_map/ppermute | solution.py:61
  176.3 66.7 %collective-permute-start.8 = (bf16[1536,448]{0,1:T(8,128)(2,1)}, bf16[1536,448]{0,1:T(8,128)(2,1)S(1)}, u32[]{:S(2)}, u32[]{:S(2)}) collective-permute-start(bf16[1536,448]{0,1:T(8,128)(2,1)} %collective-permute-done.1), channel_id=1, source_target_pairs={{0,1},{1,0},{2,3},{3,2},{4,5},{5,4},{6,7},{7,6},{8,9},{9,8},{10,11... | collective-permute-start | bytes 4128776 | tf_op jit(solution)/shard_map/ppermute | solution.py:93
  245.4 16.9 %all-to-all-start = ((bf16[16,32,896]{2,1,0:T(8,128)(2,1)}), bf16[16,32,896]{2,1,0:T(8,128)(2,1)S(1)}, u32[]{:S(2)}, u32[]{:S(2)}) async-start(bf16[16,32,896]{2,1,0:T(8,128)(2,1)} %bitcast.29), calls=%async_computation | async-start | bytes 1835008 | tf_op jit(solution)/shard_map/all_to_all | solution.py:120
  263.1 33.4 %all-to-all-start.1 = ((bf16[16,4,896]{2,1,0:T(4,128)(2,1)}), bf16[16,4,896]{2,1,0:T(4,128)(2,1)S(1)}, u32[]{:S(2)}, u32[]{:S(2)}) async-start(bf16[16,4,896]{2,1,0:T(4,128)(2,1)} %bitcast_select_fusion.2), calls=%async_computation.1 | async-start | bytes 229376 | tf_op jit(solution)/shard_map/all_to_all | solution.py:128
Sparse Core Ops, SparseCore 0:
  87.4 77.4 all-gather.3

commit v6 on v5

--- a/solution.py
+++ b/solution.py
@@ -40,7 +40,6 @@
     w_own = gate_up[0].reshape(2 * units, width)
     gate_pair = lax.ppermute(w_own[:units], "p", PAIR)
     line = lax.all_gather(tokens, LINE, axis=0, tiled=False)
-    line, gate_pair = lax.optimization_barrier((line, gate_pair))
     mine = of_class(line, core)
     got = lax.ppermute(of_class(line, 1 - core), "c", PAIR)
     first = core == 0

time: 306 us -> 278 us (0.908)
  blocking collectives: 117 us -> 88.7 us
    all_gather x1, blocking collectives: 59.6 us -> 34.8 us  [local(): line = lax.all_gather(tokens, LINE, axis=0, tiled=False)]
    all_gather x1, waiting for transfers between devices: 24.6 us -> 0.01 us  [local(): every = lax.all_gather(chip_rows, PLANE, axis=0, tiled=True)]
    ppermute x1, waiting for transfers between devices: 0.01 us -> 24.1 us  [local(): gate_pair = lax.ppermute(w_own[:units], 'p', PAIR)]
    all_gather x2, blocking collectives: 57.8 us -> 53.9 us  [local(): all_hidden = lax.all_gather(picked, ('zh', 'k'), axis=0, tiled=True)]
    ppermute x1, waiting for transfers between devices: 0.01 us -> 3.94 us  [local(): d_pair = lax.ppermute(d_later, 'p', PAIR)]
    ppermute x1, waiting for transfers between devices: 22.2 us -> 18.5 us  [local(): up_pair = lax.ppermute(w_own[units:], 'p', PAIR)]
    unnamed x17 -> x11, local copies, waits for them, and re-layouts: 11.3 us -> 11.6 us
  transfers between devices with their start and end apart: 12 -> 12, of which waited for: 5 -> 6; matrix products, arithmetic and copies ran while one was open for 12% -> 14% of each run, Pallas kernels for 0% -> 0%
where the time goes in v6:
time: 278 us
  blocking collectives  88.7 us (32%)
  waiting for transfers between devices  74.6 us (27%)
  starting transfers between devices  55.4 us (20%)
  matrix products  19.6 us (7%)
  local copies, waits for them, and re-layouts  19.5 us (7%)
  between operations  13.8 us (5%)
  other arithmetic  5.96 us (2%)
    all_gather x2, blocking collectives, local(): all_hidden = lax.all_gather(picked, ('zh', 'k'), axis=0, tiled=True)  53.9 us
    all_gather x1, blocking collectives, local(): line = lax.all_gather(tokens, LINE, axis=0, tiled=False)  34.8 us
    ppermute x1, waiting for transfers between devices, local(): gate_pair = lax.ppermute(w_own[:units], 'p', PAIR)  24.1 us
    ppermute x1, waiting for transfers between devices, local(): up_pair = lax.ppermute(w_own[units:], 'p', PAIR)  18.5 us
    all_to_all x1, starting transfers between devices, local(): lax.all_to_all(send, ('zh', 'k', 'c'), split_axis=0, concat_axis=0, tiled...  17.8 us
    all_to_all x1, waiting for transfers between devices, local(): lax.all_to_all(send, ('zh', 'k', 'c'), split_axis=0, concat_axis=0, tiled...  16.1 us
    unnamed x11, local copies, waits for them, and re-layouts  11.6 us
    all_to_all x1, waiting for transfers between devices, local(): lax.all_to_all(summed, PLANE, split_axis=0, concat_axis=0, tiled=True)  10.9 us
  transfers between devices with their start and end apart: 12, of which 6 were waited for; matrix products, arithmetic and copies ran while one was open for 14% of the time, Pallas kernels for 0%

profile of v6, /device:TPU:1, one launch (start us, length us, event | category | flops | bytes accessed | tf_op | source)
XLA Modules:
  0.0 277.6 jit_solution(15044123758825593079)
XLA Ops:
  6.5 34.8 %all-gather.1 = bf16[16,4,7168]{2,1,0:T(4,128)(2,1)S(1)} all-gather(bf16[1,4,7168]{2,1,0:T(4,128)(2,1)} %bitcast.95), channel_id=2, replica_groups=mesh['zh'=4,'k'=2,'p'=2,'x'=4,'y'=4,'c'=2] {'zh','k','p'}, dimensions={0}, use_global_device_ids=true | all-gather | bytes 974848 | tf_op jit(solution)/shard_map/all_gather | solution.py:42
  41.5 9.5 %collective-permute-start.6 = (bf16[4,4,7168]{2,1,0:T(4,128)(2,1)S(1)}, bf16[4,4,7168]{2,1,0:T(4,128)(2,1)S(1)}, u32[]{:S(2)}, u32[]{:S(2)}) collective-permute-start(bf16[4,4,7168]{2,1,0:T(4,128)(2,1)S(1)} %dynamic-slice_bitcast_fusion), channel_id=1, source_target_pairs={{0,1},{1,0},{2,3},{3,2},{4,5},{5,4},{6,7},{7,6},{8,9},{9,8},{10,11... | collective-permute-start | bytes 688136 | tf_op jit(solution)/shard_map/ppermute | solution.py:44
  54.6 2.3 collective-permute-start.2
  60.5 3.4 %collective-permute-start.3 = (bf16[96,7168]{1,0:T(8,128)(2,1)}, bf16[96,7168]{1,0:T(8,128)(2,1)}, u32[]{:S(2)}, u32[]{:S(2)}) collective-permute-start(bf16[96,7168]{1,0:T(8,128)(2,1)} %get-tuple-element.15), channel_id=1, source_target_pairs={{0,32},{32,0},{1,33},{33,1},{2,34},{34,2},{3,35},{35,3},{4,36},{36... | collective-permute-start | bytes 4128776 | tf_op jit(solution)/shard_map/ppermute | solution.py:41
  63.9 2.6 collective-permute-start.7
  73.9 18.5 %collective-permute-done = bf16[96,7168]{1,0:T(8,128)(2,1)} collective-permute-done((bf16[96,7168]{1,0:T(8,128)(2,1)}, bf16[96,7168]{1,0:T(8,128)(2,1)}, u32[]{:S(2)}, u32[]{:S(2)}) %collective-permute-start) | collective-permute-done | bytes 1376288 | tf_op jit(solution)/shard_map/ppermute | solution.py:46
  92.5 2.2 collective-permute-start.1
  94.6 3.2 %collective-permute-start.5 = (bf16[96,7168]{1,0:T(8,128)(2,1)}, bf16[96,7168]{1,0:T(8,128)(2,1)S(1)}, u32[]{:S(2)}, u32[]{:S(2)}) collective-permute-start(bf16[96,7168]{1,0:T(8,128)(2,1)} %collective-permute-done), channel_id=1, source_target_pairs={{0,1},{1,0},{2,3},{3,2},{4,5},{5,4},{6,7},{7,6},{8,9},{9,8},{10,11... | collective-permute-start | bytes 4128776 | tf_op jit(solution)/shard_map/ppermute | solution.py:60
  97.8 24.1 %collective-permute-done.3 = bf16[96,7168]{1,0:T(8,128)(2,1)} collective-permute-done((bf16[96,7168]{1,0:T(8,128)(2,1)}, bf16[96,7168]{1,0:T(8,128)(2,1)}, u32[]{:S(2)}, u32[]{:S(2)}) %collective-permute-start.3) | collective-permute-done | bytes 1376288 | tf_op jit(solution)/shard_map/ppermute | solution.py:41
  122.0 3.4 %collective-permute-start.4 = (bf16[96,7168]{1,0:T(8,128)(2,1)}, bf16[96,7168]{1,0:T(8,128)(2,1)S(1)}, u32[]{:S(2)}, u32[]{:S(2)}) collective-permute-start(bf16[96,7168]{1,0:T(8,128)(2,1)} %collective-permute-done.3), channel_id=1, source_target_pairs={{0,1},{1,0},{2,3},{3,2},{4,5},{5,4},{6,7},{7,6},{8,9},{9,8},{10,11... | collective-permute-start | bytes 4128776 | tf_op jit(solution)/shard_map/ppermute | solution.py:59
  125.4 3.5 %constant_dynamic-update-slice_fusion.4 = bf16[768,7168]{1,0:T(8,128)(2,1)} fusion(bf16[768,7168]{1,0:T(8,128)(2,1)} %constant_dynamic-update-slice_fusion.5, bf16[192,7168]{1,0:T(8,128)(2,1)} %collective-permute-done.2), kind=kLoop, calls=%fused_computation.52 | loop fusion | bytes 5505024
  128.9 2.5 constant_dynamic-update-slice_fusion.3
  131.4 2.5 constant_dynamic-update-slice_fusion.2
  136.4 10.8 %fusion.21 = f32[768,512]{1,0:T(8,128)S(1)} fusion(bf16[768,7168]{1,0:T(8,128)(2,1)} %constant_dynamic-update-slice_fusion, bf16[512,7168]{1,0:T(8,128)(2,1)} %all-gather.4.cloned.1.call-done), kind=kOutput, calls=%fused_computation.63 | convolution fusion | flops 5637144576 | bytes 19922944 | tf_op jit(solution)/shard_map/dot_general | solution.py:86
  147.5 3.9 %collective-permute-done.1 = bf16[1536,448]{0,1:T(8,128)(2,1)} collective-permute-done((bf16[1536,448]{0,1:T(8,128)(2,1)}, bf16[1536,448]{0,1:T(8,128)(2,1)}, u32[]{:S(2)}, u32[]{:S(2)}) %collective-permute-start.1) | collective-permute-done | bytes 1376288 | tf_op jit(solution)/shard_map/ppermute | solution.py:68
  151.8 2.9 %collective-permute-start.8 = (bf16[1536,448]{0,1:T(8,128)(2,1)}, bf16[1536,448]{0,1:T(8,128)(2,1)S(1)}, u32[]{:S(2)}, u32[]{:S(2)}) collective-permute-start(bf16[1536,448]{0,1:T(8,128)(2,1)} %collective-permute-done.1), channel_id=1, source_target_pairs={{0,1},{1,0},{2,3},{3,2},{4,5},{5,4},{6,7},{7,6},{8,9},{9,8},{10,11... | collective-permute-start | bytes 4128776 | tf_op jit(solution)/shard_map/ppermute | solution.py:92
  155.1 27.0 %all_gather.19 = bf16[1536,192]{1,0:T(8,128)(2,1)S(1)} all-gather(bf16[192,192]{1,0:T(8,128)(2,1)S(1)} %bitcast.82), channel_id=1, replica_groups=mesh['zh'=4,'k'=2,'p'=2,'x'=4,'y'=4,'c'=2] {'zh','k'}, dimensions={0}, use_global_device_ids=true | all-gather | bytes 663552 | tf_op jit(solution)/shard_map/all_gather | solution.py:104
  182.1 26.8 %all_gather.18 = bf16[1536,192]{1,0:T(8,128)(2,1)S(1)} all-gather(bf16[192,192]{1,0:T(8,128)(2,1)S(1)} %bitcast.83), channel_id=1, replica_groups=mesh['zh'=4,'k'=2,'p'=2,'x'=4,'y'=4,'c'=2] {'zh','k'}, dimensions={0}, use_global_device_ids=true | all-gather | bytes 663552 | tf_op jit(solution)/shard_map/all_gather | solution.py:104
  208.9 2.0 convolution_convert_fusion.3
  212.9 2.0 convolution_convert_fusion.2
  217.2 6.3 %all-to-all-start = ((bf16[16,32,896]{2,1,0:T(8,128)(2,1)}), bf16[16,32,896]{2,1,0:T(8,128)(2,1)S(1)}, u32[]{:S(2)}, u32[]{:S(2)}) async-start(bf16[16,32,896]{2,1,0:T(8,128)(2,1)} %bitcast.29), calls=%async_computation | async-start | bytes 1835008 | tf_op jit(solution)/shard_map/all_to_all | solution.py:119
  223.6 10.9 %all-to-all-done = bf16[16,32,896]{2,1,0:T(8,128)(2,1)S(1)} async-done(((bf16[16,32,896]{2,1,0:T(8,128)(2,1)}), bf16[16,32,896]{2,1,0:T(8,128)(2,1)S(1)}, u32[]{:S(2)}, u32[]{:S(2)}) %all-to-all-start) | async-done | bytes 917536 | tf_op jit(solution)/shard_map/all_to_all | solution.py:119
  235.4 17.8 %all-to-all-start.1 = ((bf16[16,4,896]{2,1,0:T(4,128)(2,1)}), bf16[16,4,896]{2,1,0:T(4,128)(2,1)S(1)}, u32[]{:S(2)}, u32[]{:S(2)}) async-start(bf16[16,4,896]{2,1,0:T(4,128)(2,1)} %bitcast_select_fusion.2), calls=%async_computation.1 | async-start | bytes 229376 | tf_op jit(solution)/shard_map/all_to_all | solution.py:127
  253.2 16.1 %all-to-all-done.1 = bf16[16,4,896]{2,1,0:T(4,128)(2,1)S(1)} async-done(((bf16[16,4,896]{2,1,0:T(4,128)(2,1)}), bf16[16,4,896]{2,1,0:T(4,128)(2,1)S(1)}, u32[]{:S(2)}, u32[]{:S(2)}) %all-to-all-start.1) | async-done | bytes 114720 | tf_op jit(solution)/shard_map/all_to_all | solution.py:127
  (72 shorter events, 24.8 us)
Async XLA Ops:
  6.5 129.9 %all-gather.4.cloned.1.call-start = ((), (), s32[]{:S(2)}) async-start(), calls=%async_computation.2 | async-start | bytes 7798784 | tf_op jit(solution)/shard_map/all_gather | solution.py:50
  41.4 9.6 %copy-start.1 = (bf16[16,4,7168]{2,1,0:T(4,128)(2,1)}, bf16[16,4,7168]{2,1,0:T(4,128)(2,1)S(1)}, u32[]{:S(2)}) copy-start(bf16[16,4,7168]{2,1,0:T(4,128)(2,1)S(1)} %all-gather.1) | copy-start | bytes 2752516
  41.5 10.6 %collective-permute-start.6 = (bf16[4,4,7168]{2,1,0:T(4,128)(2,1)S(1)}, bf16[4,4,7168]{2,1,0:T(4,128)(2,1)S(1)}, u32[]{:S(2)}, u32[]{:S(2)}) collective-permute-start(bf16[4,4,7168]{2,1,0:T(4,128)(2,1)S(1)} %dynamic-slice_bitcast_fusion), channel_id=1, source_target_pairs={{0,1},{1,0},{2,3},{3,2},{4,5},{5,4},{6,7},{7,6},{8,9},{9,8},{10,11... | collective-permute-start | bytes 688136 | tf_op jit(solution)/shard_map/ppermute | solution.py:44
  52.1 2.5 copy-start
  54.6 13.9 %copy-start.2 = (s32[32]{0:T(128)S(1)}, s32[32]{0:T(128)}, u32[]{:S(2)}) copy-start(s32[32]{0:T(128)} %param.11) | copy-start | bytes 388
  54.6 70.7 %collective-permute-start.2 = (bf16[192,7168]{1,0:T(8,128)(2,1)S(1)}, bf16[192,7168]{1,0:T(8,128)(2,1)}, u32[]{:S(2)}, u32[]{:S(2)}) collective-permute-start(bf16[192,7168]{1,0:T(8,128)(2,1)S(1)} %bitcast.77), channel_id=1, source_target_pairs={{0,1},{1,0},{2,3},{3,2},{4,5},{5,4},{6,7},{7,6},{8,9},{9,8},{10,11... | collective-permute-start | bytes 8257544 | tf_op jit(solution)/shard_map/ppermute | solution.py:56
  58.6 33.8 %collective-permute-start = (bf16[96,7168]{1,0:T(8,128)(2,1)}, bf16[96,7168]{1,0:T(8,128)(2,1)}, u32[]{:S(2)}, u32[]{:S(2)}) collective-permute-start(bf16[96,7168]{1,0:T(8,128)(2,1)} %get-tuple-element.16), channel_id=1, source_target_pairs={{0,32},{32,0},{1,33},{33,1},{2,34},{34,2},{3,35},{35,3},{4,36},{36... | collective-permute-start | bytes 4128776 | tf_op jit(solution)/shard_map/ppermute | solution.py:46
  60.5 61.4 %collective-permute-start.3 = (bf16[96,7168]{1,0:T(8,128)(2,1)}, bf16[96,7168]{1,0:T(8,128)(2,1)}, u32[]{:S(2)}, u32[]{:S(2)}) collective-permute-start(bf16[96,7168]{1,0:T(8,128)(2,1)} %get-tuple-element.15), channel_id=1, source_target_pairs={{0,32},{32,0},{1,33},{33,1},{2,34},{34,2},{3,35},{35,3},{4,36},{36... | collective-permute-start | bytes 4128776 | tf_op jit(solution)/shard_map/ppermute | solution.py:41
  63.9 149.0 %collective-permute-start.7 = (bf16[1536,448]{0,1:T(8,128)(2,1)}, bf16[1536,448]{0,1:T(8,128)(2,1)}, u32[]{:S(2)}, u32[]{:S(2)}) collective-permute-start(bf16[1536,448]{0,1:T(8,128)(2,1)} %bitcast.10), channel_id=1, source_target_pairs={{0,1},{1,0},{2,3},{3,2},{4,5},{5,4},{6,7},{7,6},{8,9},{9,8},{10,11... | collective-permute-start | bytes 4128776 | tf_op jit(solution)/shard_map/ppermute | solution.py:66
  92.5 59.0 %collective-permute-start.1 = (bf16[1536,448]{0,1:T(8,128)(2,1)}, bf16[1536,448]{0,1:T(8,128)(2,1)}, u32[]{:S(2)}, u32[]{:S(2)}) collective-permute-start(bf16[1536,448]{0,1:T(8,128)(2,1)} %bitcast.10), channel_id=1, source_target_pairs={{0,32},{32,0},{1,33},{33,1},{2,34},{34,2},{3,35},{35,3},{4,36},{36... | collective-permute-start | bytes 4128776 | tf_op jit(solution)/shard_map/ppermute | solution.py:68
  94.6 40.6 %collective-permute-start.5 = (bf16[96,7168]{1,0:T(8,128)(2,1)}, bf16[96,7168]{1,0:T(8,128)(2,1)S(1)}, u32[]{:S(2)}, u32[]{:S(2)}) collective-permute-start(bf16[96,7168]{1,0:T(8,128)(2,1)} %collective-permute-done), channel_id=1, source_target_pairs={{0,1},{1,0},{2,3},{3,2},{4,5},{5,4},{6,7},{7,6},{8,9},{9,8},{10,11... | collective-permute-start | bytes 4128776 | tf_op jit(solution)/shard_map/ppermute | solution.py:60
  122.0 12.0 %collective-permute-start.4 = (bf16[96,7168]{1,0:T(8,128)(2,1)}, bf16[96,7168]{1,0:T(8,128)(2,1)S(1)}, u32[]{:S(2)}, u32[]{:S(2)}) collective-permute-start(bf16[96,7168]{1,0:T(8,128)(2,1)} %collective-permute-done.3), channel_id=1, source_target_pairs={{0,1},{1,0},{2,3},{3,2},{4,5},{5,4},{6,7},{7,6},{8,9},{9,8},{10,11... | collective-permute-start | bytes 4128776 | tf_op jit(solution)/shard_map/ppermute | solution.py:59
  151.8 63.0 %collective-permute-start.8 = (bf16[1536,448]{0,1:T(8,128)(2,1)}, bf16[1536,448]{0,1:T(8,128)(2,1)S(1)}, u32[]{:S(2)}, u32[]{:S(2)}) collective-permute-start(bf16[1536,448]{0,1:T(8,128)(2,1)} %collective-permute-done.1), channel_id=1, source_target_pairs={{0,1},{1,0},{2,3},{3,2},{4,5},{5,4},{6,7},{7,6},{8,9},{9,8},{10,11... | collective-permute-start | bytes 4128776 | tf_op jit(solution)/shard_map/ppermute | solution.py:92
  217.2 17.3 %all-to-all-start = ((bf16[16,32,896]{2,1,0:T(8,128)(2,1)}), bf16[16,32,896]{2,1,0:T(8,128)(2,1)S(1)}, u32[]{:S(2)}, u32[]{:S(2)}) async-start(bf16[16,32,896]{2,1,0:T(8,128)(2,1)} %bitcast.29), calls=%async_computation | async-start | bytes 1835008 | tf_op jit(solution)/shard_map/all_to_all | solution.py:119
  235.4 33.9 %all-to-all-start.1 = ((bf16[16,4,896]{2,1,0:T(4,128)(2,1)}), bf16[16,4,896]{2,1,0:T(4,128)(2,1)S(1)}, u32[]{:S(2)}, u32[]{:S(2)}) async-start(bf16[16,4,896]{2,1,0:T(4,128)(2,1)} %bitcast_select_fusion.2), calls=%async_computation.1 | async-start | bytes 229376 | tf_op jit(solution)/shard_map/all_to_all | solution.py:127
Sparse Core Ops, SparseCore 0:
  54.7 77.1 all-gather.3

commit v7 on v3

--- a/solution.py
+++ b/solution.py
@@ -5,6 +5,7 @@
 
 SLOTS = 48
 LINE = ("zh", "k", "p")
+RING = ("zh", "k")
 PLANE = ("x", "y")
 PAIR = [(0, 1), (1, 0)]
 
@@ -36,23 +37,24 @@
             lax.dynamic_index_in_dim(values, p, 2, keepdims=False), which, 1, keepdims=False
         )
 
-    line = lax.all_gather(tokens, LINE, axis=0, tiled=False)
-    mine = of_class(line, core)
-    got = lax.ppermute(of_class(line, 1 - core), "c", PAIR)
+    units = gate_up.shape[2]
+    w_own = gate_up[0].reshape(2 * units, width)
+    w_pair = lax.ppermute(w_own, "p", PAIR)
+
+    line = lax.all_gather(tokens, RING, axis=0, tiled=False).reshape(far, 2, own, width)
+    mine = lax.dynamic_index_in_dim(line, core, 1, keepdims=False)
+    got = lax.ppermute(lax.dynamic_index_in_dim(line, 1 - core, 1, keepdims=False), "c", PAIR)
     first = core == 0
     chip_rows = jnp.stack([jnp.where(first, mine, got), jnp.where(first, got, mine)])
     chip_rows = chip_rows.reshape(2 * far * own, width)
     every = lax.all_gather(chip_rows, PLANE, axis=0, tiled=True)
 
-    units = gate_up.shape[2]
-    w_own = gate_up[0].reshape(2 * units, width)
-    w_pair = lax.ppermute(w_own, "p", PAIR)
+    w_other = lax.ppermute(w_own, "c", PAIR)
+    w_pair_other = lax.ppermute(w_pair, "c", PAIR)
     d_own = down[0]
-    d_pair = lax.ppermute(d_own, "p", PAIR)
-    w_all = jnp.concatenate(
-        [w_own, lax.ppermute(w_own, "c", PAIR), w_pair, lax.ppermute(w_pair, "c", PAIR)], axis=0
-    )
-    d_all = [[d_own, d_pair], [lax.ppermute(d_own, "c", PAIR), lax.ppermute(d_pair, "c", PAIR)]]
+    d_own_other = lax.ppermute(d_own, "c", PAIR)
+    d_later, w_pair = lax.optimization_barrier((d_own, w_pair))
+    d_pair = lax.ppermute(d_later, "p", PAIR)
 
     ids = of_class(expert_ids.reshape(far * 4, group_rows, -1), core)
     gates = of_class(gate_weights.reshape(far * 4, group_rows, -1), core)
@@ -70,30 +72,43 @@
         combine.append(jnp.where(hit, by_row(weights)[:, None], 0.0).astype(jnp.bfloat16))
     combine = jnp.concatenate(combine, axis=1)
 
-    both = lax.dot_general(
-        w_all, every, (((1,), (1,)), ((), ())), preferred_element_type=jnp.float32
+    def hidden_of(w):
+        both = lax.dot_general(
+            w, every, (((1,), (1,)), ((), ())), preferred_element_type=jnp.float32
+        )
+        return (jax.nn.silu(both[:units]) * both[units:]).astype(jnp.bfloat16)
+
+    near = [hidden_of(w) for w in (w_own, w_other)]
+    far_z = [hidden_of(w) for w in (w_pair, w_pair_other)]
+    hidden = [jnp.concatenate([near[e], far_z[e]], axis=0) for e in range(2)]
+    picked = jnp.concatenate(
+        [
+            jnp.dot(hidden[e], hits[e], preferred_element_type=jnp.float32).astype(jnp.bfloat16)
+            for e in range(2)
+        ],
+        axis=1,
     )
-    both = both.reshape(2, 2, 2, units, class_rows)
-    hidden = (jax.nn.silu(both[:, :, 0]) * both[:, :, 1]).astype(jnp.bfloat16)
+    picked = jnp.where(p == 0, picked, jnp.roll(picked, units, axis=0))
+    d_pair, picked = lax.optimization_barrier((d_pair, picked))
+    d_pair_other = lax.ppermute(d_pair, "c", PAIR)
+
+    most = 2 * units * 7 // 8
+    members = far * 2
+    rest = jnp.broadcast_to(picked[most:], (members, 2 * units - most, 2 * class_slots))
+    rest = lax.all_to_all(rest, RING, split_axis=0, concat_axis=0, tiled=True)
+    main = lax.all_gather(picked[:most], RING, axis=0, tiled=False)
+    all_hidden = jnp.concatenate([main, rest], axis=1).reshape(-1, 2 * class_slots)
 
     outputs = []
-    for e in range(2):
-        picked = lax.dot_general(
-            hidden[:, e].reshape(2 * units, class_rows),
-            hits[e],
-            (((1,), (0,)), ((), ())),
-            preferred_element_type=jnp.float32,
-        ).astype(jnp.bfloat16)
-        picked = picked.reshape(2, units, class_slots)
-        picked = jnp.where(p == 0, picked, picked[::-1]).reshape(2 * units, class_slots)
-        all_hidden = lax.all_gather(picked, ("zh", "k"), axis=0, tiled=True)
+    for e, ds in enumerate([(d_own, d_pair), (d_own_other, d_pair_other)]):
+        of_expert = all_hidden[:, e * class_slots : (e + 1) * class_slots]
         outputs.append(
             jnp.concatenate(
                 [
                     lax.dot_general(
-                        all_hidden, d, (((0,), (0,)), ((), ())), preferred_element_type=jnp.float32
+                        of_expert, d, (((0,), (0,)), ((), ())), preferred_element_type=jnp.float32
                     ).astype(jnp.bfloat16)
-                    for d in d_all[e]
+                    for d in ds
                 ],
                 axis=1,
             )

time: 296 us -> 272 us (0.919)
  blocking collectives: 87.1 us -> 66.3 us
  waiting for transfers between devices: 110 us -> 99.4 us
  matrix products: 22.9 us -> 27.3 us
    all_gather x3 -> x2, blocking collectives: 87.1 us -> 66.3 us  [the longest x1 33.7 us: local(): main = lax.all_gather(picked[:most], RING, axis=0, tiled=False)]
    ppermute x6, waiting for transfers between devices: 25 us -> 13.3 us  [the longest x1 12.2 us: local(): d_pair = lax.ppermute(d_later, 'p', PAIR)]
    all_to_all x0 -> x1, starting transfers between devices: none -> 7.17 us  [local(): rest = lax.all_to_all(rest, RING, split_axis=0, concat_axis=0, tiled=True)]
    all_to_all x1, starting transfers between devices: 11.6 us -> 6.83 us  [local(): lax.all_to_all(summed, PLANE, split_axis=0, concat_axis=0, tiled=True)]
    dot_general x7 -> x10, matrix products: 21.3 us -> 25.6 us  [the longest x4 17.8 us: hidden_of(): lax.dot_general(w, every, (((1,), (1,)), ((), ())), preferred_element_typ...]
  transfers between devices with their start and end apart: 10 -> 11, of which waited for: 5 -> 5; matrix products, arithmetic and copies ran while one was open for 9% -> 11% of each run, Pallas kernels for 0% -> 0%
where the time goes in v7:
time: 272 us; the launch traced here: 271 us
  waiting for transfers between devices  99.4 us (37%)
  blocking collectives  66.3 us (24%)
  starting transfers between devices  52.4 us (19%)
  matrix products  27.3 us (10%)
  between operations  13.8 us (5%)
  local copies, waits for them, and re-layouts  6.24 us (2%)
  other arithmetic  5.29 us (2%)
    ppermute x1, waiting for transfers between devices, local(): w_pair = lax.ppermute(w_own, 'p', PAIR)  60.2 us
    all_gather x1, blocking collectives, local(): main = lax.all_gather(picked[:most], RING, axis=0, tiled=False)  33.7 us
    all_gather x1, blocking collectives, local(): lax.all_gather(tokens, RING, axis=0, tiled=False)  32.6 us
    dot_general x4, matrix products, hidden_of(): lax.dot_general(w, every, (((1,), (1,)), ((), ())), preferred_element_typ...  17.8 us
    all_to_all x1, waiting for transfers between devices, local(): lax.all_to_all(send, ('zh', 'k', 'c'), split_axis=0, concat_axis=0, tiled...  14.9 us
    all_to_all x1, starting transfers between devices, local(): lax.all_to_all(send, ('zh', 'k', 'c'), split_axis=0, concat_axis=0, tiled...  14.7 us
    ppermute x1, waiting for transfers between devices, local(): d_pair = lax.ppermute(d_later, 'p', PAIR)  12.2 us
    all_to_all x1, waiting for transfers between devices, local(): lax.all_to_all(summed, PLANE, split_axis=0, concat_axis=0, tiled=True)  11 us
  transfers between devices with their start and end apart: 11, of which 5 were waited for; matrix products, arithmetic and copies ran while one was open for 11% of the time, Pallas kernels for 0%

profile of v7, /device:TPU:1, one launch (start us, length us, event | category | flops | bytes accessed | tf_op | source)
XLA Modules:
  0.0 270.7 jit_solution(15890734072422071104)
XLA Ops:
  6.5 32.6 %all-gather.2 = bf16[8,4,7168]{2,1,0:T(4,128)(2,1)S(1)} all-gather(bf16[1,4,7168]{2,1,0:T(4,128)(2,1)} %bitcast.76), channel_id=2, replica_groups=mesh['zh'=4,'k'=2,'p'=2,'x'=4,'y'=4,'c'=2] {'zh','k'}, dimensions={0}, use_global_device_ids=true | all-gather | bytes 516096 | tf_op jit(solution)/shard_map/all_gather | solution.py:44
  39.3 7.9 %collective-permute-start.2 = (bf16[4,4,7168]{2,1,0:T(4,128)(2,1)S(1)}, bf16[4,4,7168]{2,1,0:T(4,128)(2,1)S(1)}, u32[]{:S(2)}, u32[]{:S(2)}) collective-permute-start(bf16[4,4,7168]{2,1,0:T(4,128)(2,1)S(1)} %dynamic-slice_bitcast_fusion), channel_id=1, source_target_pairs={{0,1},{1,0},{2,3},{3,2},{4,5},{5,4},{6,7},{7,6},{8,9},{9,8},{10,11... | collective-permute-start | bytes 688136 | tf_op jit(solution)/shard_map/ppermute | solution.py:46
  50.2 2.7 collective-permute-start
  52.9 60.2 %collective-permute-done = bf16[192,7168]{1,0:T(8,128)(2,1)} collective-permute-done((bf16[192,7168]{1,0:T(8,128)(2,1)S(1)}, bf16[192,7168]{1,0:T(8,128)(2,1)}, u32[]{:S(2)}, u32[]{:S(2)}) %collective-permute-start) | collective-permute-done | bytes 2752544 | tf_op jit(solution)/shard_map/ppermute | solution.py:42
  113.0 3.1 %collective-permute-start.4 = (bf16[192,7168]{1,0:T(8,128)(2,1)}, bf16[192,7168]{1,0:T(8,128)(2,1)}, u32[]{:S(2)}, u32[]{:S(2)}) collective-permute-start(bf16[192,7168]{1,0:T(8,128)(2,1)} %collective-permute-done), channel_id=1, source_target_pairs={{0,1},{1,0},{2,3},{3,2},{4,5},{5,4},{6,7},{7,6},{8,9},{9,8},{10,11... | collective-permute-start | bytes 8257544 | tf_op jit(solution)/shard_map/ppermute | solution.py:53
  116.1 1.9 collective-permute-start.3
  118.1 2.4 collective-permute-start.5
  126.1 2.7 collective-permute-start.1
  128.9 6.6 %fusion.37 = f32[192,512]{1,0:T(8,128)S(1)} fusion(bf16[192,7168]{1,0:T(8,128)(2,1)} %collective-permute-done, bf16[512,7168]{1,0:T(8,128)(2,1)} %all-gather.5.cloned.1.call-done), kind=kOutput, calls=%fused_computation.80 | convolution fusion | flops 1409286144 | bytes 10485760 | tf_op jit(solution)/shard_map/dot_general | solution.py:76
  135.6 4.3 %convolution_bitcast_fusion = f32[192,512]{1,0:T(8,128)S(1)} fusion(bf16[512,7168]{1,0:T(8,128)(2,1)S(1)} %copy-done.1, bf16[192,7168]{1,0:T(8,128)(2,1)} %collective-permute-done.4), kind=kOutput, calls=%fused_computation.1 | convolution fusion | flops 1409286144 | bytes 10485760 | tf_op jit(solution)/shard_map/dot_general | solution.py:76
  140.0 4.3 %convolution_bitcast_fusion.1 = f32[192,512]{1,0:T(8,128)S(1)} fusion(bf16[512,7168]{1,0:T(8,128)(2,1)S(1)} %copy-done.1, bf16[192,7168]{1,0:T(8,128)(2,1)} %collective-permute-done.3), kind=kOutput, calls=%fused_computation.2 | convolution fusion | flops 1409286144 | bytes 10485760 | tf_op jit(solution)/shard_map/dot_general | solution.py:76
  144.8 2.6 convolution_bitcast_fusion.2
  147.9 12.2 %collective-permute-done.1 = bf16[1536,448]{0,1:T(8,128)(2,1)} collective-permute-done((bf16[1536,448]{0,1:T(8,128)(2,1)}, bf16[1536,448]{0,1:T(8,128)(2,1)}, u32[]{:S(2)}, u32[]{:S(2)}) %collective-permute-start.1) | collective-permute-done | bytes 1376288 | tf_op jit(solution)/shard_map/ppermute | solution.py:57
  160.8 7.2 %all-to-all-start = ((bf16[8,24,384]{2,1,0:T(8,128)(2,1)}), bf16[8,24,384]{2,1,0:T(8,128)(2,1)S(1)}, u32[]{:S(2)}, u32[]{:S(2)}) async-start(bf16[8,24,384]{2,1,0:T(8,128)(2,1)} %broadcast_in_dim.77), calls=%async_computation | async-start | bytes 294912 | tf_op jit(solution)/shard_map/all_to_all | solution.py:98
  168.2 3.0 %collective-permute-start.6 = (bf16[1536,448]{0,1:T(8,128)(2,1)}, bf16[1536,448]{0,1:T(8,128)(2,1)}, u32[]{:S(2)}, u32[]{:S(2)}) collective-permute-start(bf16[1536,448]{0,1:T(8,128)(2,1)} %collective-permute-done.1), channel_id=1, source_target_pairs={{0,1},{1,0},{2,3},{3,2},{4,5},{5,4},{6,7},{7,6},{8,9},{9,8},{10,11... | collective-permute-start | bytes 4128776 | tf_op jit(solution)/shard_map/ppermute | solution.py:93
  171.2 33.7 %all-gather.1 = bf16[1344,384]{1,0:T(8,128)(2,1)S(1)} all-gather(bf16[168,384]{1,0:T(8,128)(2,1)S(1)} %slice.54), channel_id=3, replica_groups=mesh['zh'=4,'k'=2,'p'=2,'x'=4,'y'=4,'c'=2] {'zh','k'}, dimensions={0}, use_global_device_ids=true | all-gather | bytes 1161216 | tf_op jit(solution)/shard_map/all_gather | solution.py:99
  205.0 2.1 convolution_convert_fusion.3
  207.8 2.2 convolution_convert_fusion.2
  210.0 2.2 convolution_convert_fusion.1
  212.2 1.7 convolution_convert_fusion
  213.9 6.8 %all-to-all-start.1 = ((bf16[16,32,896]{2,1,0:T(8,128)(2,1)}), bf16[16,32,896]{2,1,0:T(8,128)(2,1)S(1)}, u32[]{:S(2)}, u32[]{:S(2)}) async-start(bf16[16,32,896]{2,1,0:T(8,128)(2,1)} %bitcast.23), calls=%async_computation.1 | async-start | bytes 1835008 | tf_op jit(solution)/shard_map/all_to_all | solution.py:119
  220.9 11.0 %all-to-all-done.1 = bf16[16,32,896]{2,1,0:T(8,128)(2,1)S(1)} async-done(((bf16[16,32,896]{2,1,0:T(8,128)(2,1)}), bf16[16,32,896]{2,1,0:T(8,128)(2,1)S(1)}, u32[]{:S(2)}, u32[]{:S(2)}) %all-to-all-start.1) | async-done | bytes 917536 | tf_op jit(solution)/shard_map/all_to_all | solution.py:119
  232.8 14.7 %all-to-all-start.2 = ((bf16[16,4,896]{2,1,0:T(4,128)(2,1)}), bf16[16,4,896]{2,1,0:T(4,128)(2,1)S(1)}, u32[]{:S(2)}, u32[]{:S(2)}) async-start(bf16[16,4,896]{2,1,0:T(4,128)(2,1)} %bitcast_select_fusion.2), calls=%async_computation.2 | async-start | bytes 229376 | tf_op jit(solution)/shard_map/all_to_all | solution.py:127
  247.5 14.9 %all-to-all-done.2 = bf16[16,4,896]{2,1,0:T(4,128)(2,1)S(1)} async-done(((bf16[16,4,896]{2,1,0:T(4,128)(2,1)}), bf16[16,4,896]{2,1,0:T(4,128)(2,1)S(1)}, u32[]{:S(2)}, u32[]{:S(2)}) %all-to-all-start.2) | async-done | bytes 114720 | tf_op jit(solution)/shard_map/all_to_all | solution.py:127
  (73 shorter events, 13.9 us)
Async XLA Ops:
  6.5 122.3 %all-gather.5.cloned.1.call-start = ((), (), s32[]{:S(2)}) async-start(), calls=%async_computation.3 | async-start | bytes 7798784 | tf_op jit(solution)/shard_map/all_gather | solution.py:50
  39.3 9.0 %collective-permute-start.2 = (bf16[4,4,7168]{2,1,0:T(4,128)(2,1)S(1)}, bf16[4,4,7168]{2,1,0:T(4,128)(2,1)S(1)}, u32[]{:S(2)}, u32[]{:S(2)}) collective-permute-start(bf16[4,4,7168]{2,1,0:T(4,128)(2,1)S(1)} %dynamic-slice_bitcast_fusion), channel_id=1, source_target_pairs={{0,1},{1,0},{2,3},{3,2},{4,5},{5,4},{6,7},{7,6},{8,9},{9,8},{10,11... | collective-permute-start | bytes 688136 | tf_op jit(solution)/shard_map/ppermute | solution.py:46
  48.2 1.9 copy-start.2
  48.4 74.0 %copy-start = (s32[32]{0:T(128)S(1)}, s32[32]{0:T(128)}, u32[]{:S(2)}) copy-start(s32[32]{0:T(128)} %param.11) | copy-start | bytes 388
  50.2 62.9 %collective-permute-start = (bf16[192,7168]{1,0:T(8,128)(2,1)S(1)}, bf16[192,7168]{1,0:T(8,128)(2,1)}, u32[]{:S(2)}, u32[]{:S(2)}) collective-permute-start(bf16[192,7168]{1,0:T(8,128)(2,1)S(1)} %bitcast.79), channel_id=1, source_target_pairs={{0,32},{32,0},{1,33},{33,1},{2,34},{34,2},{3,35},{35,3},{4,36},{36... | collective-permute-start | bytes 8257544 | tf_op jit(solution)/shard_map/ppermute | solution.py:42
  113.0 22.5 %collective-permute-start.4 = (bf16[192,7168]{1,0:T(8,128)(2,1)}, bf16[192,7168]{1,0:T(8,128)(2,1)}, u32[]{:S(2)}, u32[]{:S(2)}) collective-permute-start(bf16[192,7168]{1,0:T(8,128)(2,1)} %collective-permute-done), channel_id=1, source_target_pairs={{0,1},{1,0},{2,3},{3,2},{4,5},{5,4},{6,7},{7,6},{8,9},{9,8},{10,11... | collective-permute-start | bytes 8257544 | tf_op jit(solution)/shard_map/ppermute | solution.py:53
  116.1 23.9 %collective-permute-start.3 = (bf16[192,7168]{1,0:T(8,128)(2,1)S(1)}, bf16[192,7168]{1,0:T(8,128)(2,1)}, u32[]{:S(2)}, u32[]{:S(2)}) collective-permute-start(bf16[192,7168]{1,0:T(8,128)(2,1)S(1)} %bitcast.80), channel_id=1, source_target_pairs={{0,1},{1,0},{2,3},{3,2},{4,5},{5,4},{6,7},{7,6},{8,9},{9,8},{10,11... | collective-permute-start | bytes 8257544 | tf_op jit(solution)/shard_map/ppermute | solution.py:52
  118.1 89.7 %collective-permute-start.5 = (bf16[1536,448]{0,1:T(8,128)(2,1)}, bf16[1536,448]{0,1:T(8,128)(2,1)}, u32[]{:S(2)}, u32[]{:S(2)}) collective-permute-start(bf16[1536,448]{0,1:T(8,128)(2,1)} %bitcast.82), channel_id=1, source_target_pairs={{0,1},{1,0},{2,3},{3,2},{4,5},{5,4},{6,7},{7,6},{8,9},{9,8},{10,11... | collective-permute-start | bytes 4128776 | tf_op jit(solution)/shard_map/ppermute | solution.py:55
  126.1 34.0 %collective-permute-start.1 = (bf16[1536,448]{0,1:T(8,128)(2,1)}, bf16[1536,448]{0,1:T(8,128)(2,1)}, u32[]{:S(2)}, u32[]{:S(2)}) collective-permute-start(bf16[1536,448]{0,1:T(8,128)(2,1)} %bitcast.83), channel_id=1, source_target_pairs={{0,32},{32,0},{1,33},{33,1},{2,34},{34,2},{3,35},{35,3},{4,36},{36... | collective-permute-start | bytes 4128776 | tf_op jit(solution)/shard_map/ppermute | solution.py:57
  128.9 6.7 %copy-start.1 = (bf16[512,7168]{1,0:T(8,128)(2,1)S(1)}, bf16[512,7168]{1,0:T(8,128)(2,1)}, u32[]{:S(2)}) copy-start(bf16[512,7168]{1,0:T(8,128)(2,1)} %all-gather.5.cloned.1.call-done) | copy-start | bytes 22020100
  160.8 44.1 %all-to-all-start = ((bf16[8,24,384]{2,1,0:T(8,128)(2,1)}), bf16[8,24,384]{2,1,0:T(8,128)(2,1)S(1)}, u32[]{:S(2)}, u32[]{:S(2)}) async-start(bf16[8,24,384]{2,1,0:T(8,128)(2,1)} %broadcast_in_dim.77), calls=%async_computation | async-start | bytes 294912 | tf_op jit(solution)/shard_map/all_to_all | solution.py:98
  168.2 41.8 %collective-permute-start.6 = (bf16[1536,448]{0,1:T(8,128)(2,1)}, bf16[1536,448]{0,1:T(8,128)(2,1)}, u32[]{:S(2)}, u32[]{:S(2)}) collective-permute-start(bf16[1536,448]{0,1:T(8,128)(2,1)} %collective-permute-done.1), channel_id=1, source_target_pairs={{0,1},{1,0},{2,3},{3,2},{4,5},{5,4},{6,7},{7,6},{8,9},{9,8},{10,11... | collective-permute-start | bytes 4128776 | tf_op jit(solution)/shard_map/ppermute | solution.py:93
  205.0 2.1 copy-start.3
  213.9 18.0 %all-to-all-start.1 = ((bf16[16,32,896]{2,1,0:T(8,128)(2,1)}), bf16[16,32,896]{2,1,0:T(8,128)(2,1)S(1)}, u32[]{:S(2)}, u32[]{:S(2)}) async-start(bf16[16,32,896]{2,1,0:T(8,128)(2,1)} %bitcast.23), calls=%async_computation.1 | async-start | bytes 1835008 | tf_op jit(solution)/shard_map/all_to_all | solution.py:119
  232.8 29.6 %all-to-all-start.2 = ((bf16[16,4,896]{2,1,0:T(4,128)(2,1)}), bf16[16,4,896]{2,1,0:T(4,128)(2,1)S(1)}, u32[]{:S(2)}, u32[]{:S(2)}) async-start(bf16[16,4,896]{2,1,0:T(4,128)(2,1)} %bitcast_select_fusion.2), calls=%async_computation.2 | async-start | bytes 229376 | tf_op jit(solution)/shard_map/all_to_all | solution.py:127
Sparse Core Ops, SparseCore 0:
  49.8 77.9 all-gather.4

commit v8 on v7

v8 whole, which is shorter than its diff:
```python
import jax
import jax.numpy as jnp
from jax import lax
from jax.experimental import pallas as pl
from jax.experimental.pallas import tpu as pltpu
from jax.sharding import Mesh, PartitionSpec as P

SLOTS = 48
LINE = ("zh", "k", "p")
RING = ("zh", "k")
PLANE = ("x", "y")
PAIR = [(0, 1), (1, 0)]


def routing(expert_ids, gate_weights, capacity, expert):
    member = expert_ids == expert
    hits = jnp.sum(member.astype(jnp.int32), axis=2)
    rank = jnp.cumsum(hits, axis=1) - hits
    cap = lax.dynamic_index_in_dim(capacity, expert, 0, keepdims=False)
    weights = jnp.sum(jnp.where(member, gate_weights, 0.0), axis=2)
    offset = jnp.arange(hits.shape[0], dtype=jnp.int32)[:, None] * SLOTS
    return jnp.where((hits > 0) & (rank < cap), rank + offset, -1), weights


def hidden_kernel(p_ref, own_a, pair_a, own_b, pair_b, tokens, hits, out, total):
    step = pl.program_id(0)

    @pl.when(step == 0)
    def _():
        total[...] = jnp.zeros_like(total)

    w = jnp.concatenate([own_a[...], pair_a[...], own_b[...], pair_b[...]], axis=0)
    total[...] += lax.dot_general(
        w, tokens[...], (((1,), (1,)), ((), ())), preferred_element_type=jnp.float32
    )

    @pl.when(step == pl.num_programs(0) - 1)
    def _():
        rows = own_a.shape[0]
        units = rows // 2
        for z in range(2):
            hidden = []
            for expert in range(2):
                base = (2 * expert + z) * rows
                gate = total[base : base + units]
                up = total[base + units : base + rows]
                hidden.append((gate / (1.0 + jnp.exp(-gate)) * up).astype(jnp.bfloat16))
            picked = jnp.dot(
                jnp.concatenate(hidden, axis=1), hits[...], preferred_element_type=jnp.float32
            )
            place = p_ref[0] if z == 0 else 1 - p_ref[0]
            out[pl.ds(pl.multiple_of(place * units, 16), units), :] = picked.astype(jnp.bfloat16)


def slotted_hidden(p, own_a, pair_a, own_b, pair_b, tokens, hits):
    rows, width = own_a.shape
    count, slots = tokens.shape[0], hits.shape[1]
    depth = 1024 if width % 1024 == 0 else width
    weights = pl.BlockSpec((rows, depth), lambda i, p: (0, i))
    return pl.pallas_call(
        hidden_kernel,
        grid_spec=pltpu.PrefetchScalarGridSpec(
            num_scalar_prefetch=1,
            grid=(width // depth,),
            in_specs=[weights] * 4
            + [
                pl.BlockSpec((count, depth), lambda i, p: (0, i)),
                pl.BlockSpec(hits.shape, lambda i, p: (0, 0)),
            ],
            out_specs=pl.BlockSpec((rows, slots), lambda i, p: (0, 0)),
            scratch_shapes=[pltpu.VMEM((4 * rows, count), jnp.float32)],
        ),
        out_shape=jax.ShapeDtypeStruct((rows, slots), jnp.bfloat16),
        compiler_params=pltpu.CompilerParams(vmem_limit_bytes=40 * 2**20),
        cost_estimate=pl.CostEstimate(
            flops=2 * 4 * rows * width * count,
            bytes_accessed=2 * width * (4 * rows + count),
            transcendentals=2 * rows * count,
        ),
    )(p.reshape(1), own_a, pair_a, own_b, pair_b, tokens, hits)


def output_kernel(main, rest, own_a, pair_a, own_b, pair_b, combine, out):
    members = main.shape[0]
    pieces = []
    for i in range(members):
        pieces += [main[i], rest[i]]
    hidden = jnp.concatenate(pieces, axis=0)
    slots = hidden.shape[1]
    for z, (d_a, d_b) in enumerate([(own_a, own_b), (pair_a, pair_b)]):
        of_a = jnp.dot(d_a[...], hidden, preferred_element_type=jnp.float32)
        of_b = jnp.dot(d_b[...], hidden, preferred_element_type=jnp.float32)
        is_a = lax.broadcasted_iota(jnp.int32, of_a.shape, 1) < slots // 2
        outputs = jnp.where(is_a, of_a, of_b).astype(jnp.bfloat16)
        summed = lax.dot_general(
            combine[...], outputs, (((1,), (1,)), ((), ())), preferred_element_type=jnp.float32
        )
        out[:, z] = summed.astype(jnp.bfloat16).reshape(out.shape[0], out.shape[2], out.shape[3])


def token_sums(main, rest, own_a, pair_a, own_b, pair_b, combine, chips):
    features, count = own_a.shape[0], combine.shape[0]
    return pl.pallas_call(
        output_kernel,
        in_specs=[pl.BlockSpec(memory_space=pltpu.VMEM)] * 7,
        out_specs=pl.BlockSpec(memory_space=pltpu.VMEM),
        out_shape=jax.ShapeDtypeStruct((chips, 2, count // chips, features), jnp.bfloat16),
        compiler_params=pltpu.CompilerParams(vmem_limit_bytes=40 * 2**20),
        cost_estimate=pl.CostEstimate(
            flops=8 * features * own_a.shape[1] * combine.shape[1],
            bytes_accessed=8 * features * own_a.shape[1],
            transcendentals=0,
        ),
    )(main, rest, own_a, pair_a, own_b, pair_b, combine)


def local(tokens, gate_up, down, expert_ids, gate_weights, capacity):
    core = lax.axis_index("c")
    k, p = lax.axis_index("k"), lax.axis_index("p")
    plane_index = lax.axis_index(PLANE)
    chips = lax.axis_size("x") * lax.axis_size("y")
    far = lax.axis_size("zh")
    own, width = tokens.shape
    group_rows = chips * 2 * own
    class_rows = far * group_rows
    class_slots = far * SLOTS

    def of_class(values, which):
        values = values.reshape((far, 2, 2) + values.shape[1:])
        return lax.dynamic_index_in_dim(
            lax.dynamic_index_in_dim(values, p, 2, keepdims=False), which, 1, keepdims=False
        )

    units = gate_up.shape[2]
    w_own = gate_up[0].reshape(2 * units, width)
    w_pair = lax.ppermute(w_own, "p", PAIR)

    line = lax.all_gather(tokens, RING, axis=0, tiled=False).reshape(far, 2, own, width)
    mine = lax.dynamic_index_in_dim(line, core, 1, keepdims=False)
    got = lax.ppermute(lax.dynamic_index_in_dim(line, 1 - core, 1, keepdims=False), "c", PAIR)
    first = core == 0
    chip_rows = jnp.stack([jnp.where(first, mine, got), jnp.where(first, got, mine)])
    chip_rows = chip_rows.reshape(2 * far * own, width)
    every = lax.all_gather(chip_rows, PLANE, axis=0, tiled=True)

    w_other = lax.ppermute(w_own, "c", PAIR)
    d_own = down[0].T
    d_other = lax.ppermute(d_own, "c", PAIR)
    w_pair, w_other, d_other = lax.optimization_barrier((w_pair, w_other, d_other))
    d_later, w_pair = lax.optimization_barrier((d_own, w_pair))
    d_pair = lax.ppermute(d_later, "p", PAIR)
    w_pair_other = lax.ppermute(w_pair, "c", PAIR)

    ids = of_class(expert_ids.reshape(far * 4, group_rows, -1), core)
    gates = of_class(gate_weights.reshape(far * 4, group_rows, -1), core)

    def by_row(values):
        values = values.reshape(far, chips, 2, own).transpose(1, 2, 0, 3)
        return values.reshape(class_rows)

    slot_index = jnp.arange(2 * class_slots, dtype=jnp.int32)
    hits, combine = [], []
    for e, expert in enumerate((plane_index * 2 + core, plane_index * 2 + 1 - core)):
        slots, weights = routing(ids, gates, capacity, expert)
        slots = by_row(jnp.where(slots >= 0, slots + e * class_slots, -1))
        hit = slots[:, None] == slot_index[None, :]
        hits.append(hit.astype(jnp.bfloat16))
        combine.append(jnp.where(hit, by_row(weights)[:, None], 0.0))
    hits = jnp.concatenate(hits, axis=0)
    combine = (combine[0] + combine[1]).astype(jnp.bfloat16)
    hits, combine = lax.optimization_barrier((hits, combine))

    picked = slotted_hidden(p, w_own, w_pair, w_other, w_pair_other, every, hits)

    most = 2 * units * 5 // 6
    members = far * 2
    rest = jnp.broadcast_to(picked[most:], (members, 2 * units - most, 2 * class_slots))
    rest = lax.all_to_all(rest, RING, split_axis=0, concat_axis=0, tiled=True)
    main = lax.all_gather(picked[:most], RING, axis=0, tiled=False)
    d_pair, main = lax.optimization_barrier((d_pair, main))
    d_pair_other = lax.ppermute(d_pair, "c", PAIR)
    summed = token_sums(main, rest, d_own, d_pair, d_other, d_pair_other, combine, chips)

    arrived = lax.all_to_all(summed, PLANE, split_axis=0, concat_axis=0, tiled=True)
    rows = jnp.sum(arrived.astype(jnp.float32), axis=0).astype(jnp.bfloat16)
    features = rows.shape[2]

    rows = rows.reshape(2, 2, far, own, features).transpose(2, 1, 0, 3, 4)[:, None]
    here = (jnp.arange(2) == core)[None, :, None, None, None, None]
    send = jnp.where(here, rows, jnp.zeros((), rows.dtype))
    send = send.reshape(far * 4, 2 * own, features)
    recv = lax.all_to_all(send, ("zh", "k", "c"), split_axis=0, concat_axis=0, tiled=True)
    recv = recv.reshape(far, 2, 2, 2, own, features)
    recv = lax.dynamic_index_in_dim(recv, k, 2, keepdims=False)
    recv = jnp.where(p == 0, recv, recv[:, :, ::-1])
    return recv.transpose(3, 0, 1, 2, 4).reshape(own, width)


def solution(mesh):
    rows, cols = mesh.devices.shape
    side = 4
    shape = (rows // 4, 2, 2, side, cols // (2 * side), 2)
    fine = Mesh(mesh.devices.reshape(shape), LINE + PLANE + ("c",))
    row, col = LINE, PLANE + ("c",)
    in_specs = (
        P(row + col, None),
        P(col, None, row, None),
        P(col, None, row),
        P(),
        P(),
        P(),
    )
    out_specs = P(row + col, None)
    return jax.shard_map(local, mesh=fine, in_specs=in_specs, out_specs=out_specs, check_vma=False)
```

time: 272 us -> 273 us (level)
  blocking collectives: 66.3 us -> 94.8 us
  matrix products: 27.3 us -> 0 us
  Pallas kernels: 0 us -> 16.8 us
  waiting for transfers between devices: 99.4 us -> 87.4 us
  starting transfers between devices: 52.4 us -> 41.9 us
  local copies, waits for them, and re-layouts: 6.24 us -> 11.1 us
    dot_general x11 -> x0, matrix products: 27.3 us -> none  [the longest x4 17.8 us: hidden_of(): lax.dot_general(w, every, (((1,), (1,)), ((), ())), preferred_element_typ...]
    all_to_all x0 -> x1, blocking collectives: none -> 24.4 us  [local(): rest = lax.all_to_all(rest, RING, split_axis=0, concat_axis=0, tiled=True)]
    pallas_call x0 -> x2, Pallas kernels: none -> 16.8 us  [the longest x1 10.7 us: slotted_hidden(): pl.pallas_call(hidden_kernel, grid_spec=pltpu.PrefetchScalarGridSpec(num_...]
    ppermute x1, waiting for transfers between devices: 12.2 us -> 0.01 us  [local(): d_pair = lax.ppermute(d_later, 'p', PAIR)]
    ppermute x1, waiting for transfers between devices: 60.2 us -> 51.1 us  [local(): w_pair = lax.ppermute(w_own, 'p', PAIR)]
    all_to_all x1, starting transfers between devices: 14.7 us -> 6.54 us  [local(): lax.all_to_all(send, ('zh', 'k', 'c'), split_axis=0, concat_axis=0, tiled...]
    all_to_all x1 -> x0, starting transfers between devices: 7.17 us -> none  [local(): rest = lax.all_to_all(rest, RING, split_axis=0, concat_axis=0, tiled=True)]
    unnamed x8 -> x12, local copies, waits for them, and re-layouts: 0.51 us -> 6.22 us
  transfers between devices with their start and end apart: 11 -> 10, of which waited for: 5 -> 6; matrix products, arithmetic and copies ran while one was open for 11% -> 3% of each run, Pallas kernels for 0% -> 4%
where the time goes in v8:
time: 273 us; the launch traced here: 272 us
  blocking collectives  94.8 us (35%)
  waiting for transfers between devices  87.4 us (32%)
  starting transfers between devices  41.9 us (15%)
  Pallas kernels  16.8 us (6%)
  between operations  13.7 us (5%)
  local copies, waits for them, and re-layouts  11.1 us (4%)
  other arithmetic  6.03 us (2%)
    ppermute x1, waiting for transfers between devices, local(): w_pair = lax.ppermute(w_own, 'p', PAIR)  51.1 us
    all_gather x1, blocking collectives, local(): main = lax.all_gather(picked[:most], RING, axis=0, tiled=False)  37.6 us
    all_gather x1, blocking collectives, local(): lax.all_gather(tokens, RING, axis=0, tiled=False)  32.8 us
    all_to_all x1, blocking collectives, local(): rest = lax.all_to_all(rest, RING, split_axis=0, concat_axis=0, tiled=True)  24.4 us
    all_to_all x1, waiting for transfers between devices, local(): lax.all_to_all(summed, PLANE, split_axis=0, concat_axis=0, tiled=True)  15.3 us
    all_to_all x1, waiting for transfers between devices, local(): lax.all_to_all(send, ('zh', 'k', 'c'), split_axis=0, concat_axis=0, tiled...  14.7 us
    pallas_call x1, Pallas kernels, slotted_hidden(): pl.pallas_call(hidden_kernel, grid_spec=pltpu.PrefetchScalarGridSpec(num_...  10.7 us
    ppermute x1, starting transfers between devices, local(): lax.ppermute(lax.dynamic_index_in_dim(line, 1 - core, 1, keepdims=False),...  7.87 us
  transfers between devices with their start and end apart: 10, of which 6 were waited for; matrix products, arithmetic and copies ran while one was open for 3% of the time, Pallas kernels for 4%

profile of v8, /device:TPU:1, one launch (start us, length us, event | category | flops | bytes accessed | tf_op | source)
XLA Modules:
  0.0 271.7 jit_solution(6230275152239064279)
XLA Ops:
  6.5 32.8 %all-gather.2 = bf16[8,4,7168]{2,1,0:T(4,128)(2,1)S(1)} all-gather(bf16[1,4,7168]{2,1,0:T(4,128)(2,1)} %bitcast.58), channel_id=2, replica_groups=mesh['zh'=4,'k'=2,'p'=2,'x'=4,'y'=4,'c'=2] {'zh','k'}, dimensions={0}, use_global_device_ids=true | all-gather | bytes 516096 | tf_op jit(solution)/shard_map/all_gather | solution.py:138
  39.4 7.9 %collective-permute-start.5 = (bf16[4,4,7168]{2,1,0:T(4,128)(2,1)S(1)}, bf16[4,4,7168]{2,1,0:T(4,128)(2,1)S(1)}, u32[]{:S(2)}, u32[]{:S(2)}) collective-permute-start(bf16[4,4,7168]{2,1,0:T(4,128)(2,1)S(1)} %dynamic-slice_bitcast_fusion), channel_id=1, source_target_pairs={{0,1},{1,0},{2,3},{3,2},{4,5},{5,4},{6,7},{7,6},{8,9},{9,8},{10,11... | collective-permute-start | bytes 688136 | tf_op jit(solution)/shard_map/ppermute | solution.py:140
  47.3 1.1 collective-permute-done.5
  49.8 2.7 collective-permute-start
  52.5 2.6 collective-permute-start.1
  55.1 1.9 collective-permute-start.2
  57.0 4.7 %collective-permute-done.2.own_b = bf16[448,1536]{1,0:T(8,128)(2,1)S(1)} collective-permute-done((bf16[448,1536]{1,0:T(8,128)(2,1)S(1)}, bf16[448,1536]{1,0:T(8,128)(2,1)S(1)}, u32[]{:S(2)}, u32[]{:S(2)}) %collective-permute-start.2) | collective-permute-done | bytes 1376288 | tf_op jit(solution)/shard_map/ppermute | solution.py:148
  61.8 51.1 %collective-permute-done.pair_a = bf16[192,7168]{1,0:T(8,128)(2,1)} collective-permute-done((bf16[192,7168]{1,0:T(8,128)(2,1)}, bf16[192,7168]{1,0:T(8,128)(2,1)}, u32[]{:S(2)}, u32[]{:S(2)}) %collective-permute-start) | collective-permute-done | bytes 2752544 | tf_op jit(solution)/shard_map/ppermute | solution.py:136
  112.9 1.5 copy-done.3
  114.5 3.1 %collective-permute-start.4 = (bf16[192,7168]{1,0:T(8,128)(2,1)}, bf16[192,7168]{1,0:T(8,128)(2,1)}, u32[]{:S(2)}, u32[]{:S(2)}) collective-permute-start(bf16[192,7168]{1,0:T(8,128)(2,1)} %collective-permute-done.pair_a), channel_id=1, source_target_pairs={{0,1},{1,0},{2,3},{3,2},{4,5},{5,4},{6,7},{7,6},{8,9},{9,8},{10,11... | collective-permute-start | bytes 8257544 | tf_op jit(solution)/shard_map/ppermute | solution.py:152
  120.2 1.4 fusion.3
  122.6 2.7 collective-permute-start.3
  128.0 1.1 copy-done.1
  129.1 1.8 copy-done.2
  130.9 1.8 copy-done.4
  132.6 10.7 %shard_map.64 = bf16[192,384]{1,0:T(8,128)(2,1)S(1)} custom-call(s32[1]{0:T(128)} %bitcast.4.p_ref, bf16[192,7168]{1,0:T(8,128)(2,1)S(1)} %bitcast.48, bf16[192,7168]{1,0:T(8,128)(2,1)} %collective-permute-done.pair_a, bf16[192,7168]{1,0:T(8,128)(2,1)S(1)} %copy-done.4, bf16[192,7168]{1,0:T(8,128)(2,1)} %collective-permute-done.4.pair_b, ...), custom_call_target="tpu_custom_call" | custom-call | flops 5637144576 | bytes 18350080 | tf_op jit(solution)/shard_map/pallas_call | solution.py:60
  143.4 37.6 %all-gather.1 = bf16[1280,384]{1,0:T(8,128)(2,1)S(1)} all-gather(bf16[160,384]{1,0:T(8,128)(2,1)S(1)} %slice.8), channel_id=3, replica_groups=mesh['zh'=4,'k'=2,'p'=2,'x'=4,'y'=4,'c'=2] {'zh','k'}, dimensions={0}, use_global_device_ids=true | all-gather | bytes 1105920 | tf_op jit(solution)/shard_map/all_gather | solution.py:179
  181.0 7.4 %collective-permute-start.6 = (bf16[448,1536]{1,0:T(8,128)(2,1)}, bf16[448,1536]{1,0:T(8,128)(2,1)S(1)}, u32[]{:S(2)}, u32[]{:S(2)}) collective-permute-start(bf16[448,1536]{1,0:T(8,128)(2,1)} %collective-permute-done.3.pair_a), channel_id=1, source_target_pairs={{0,1},{1,0},{2,3},{3,2},{4,5},{5,4},{6,7},{7,6},{8,9},{9,8},{10,11... | collective-permute-start | bytes 4128776 | tf_op jit(solution)/shard_map/ppermute | solution.py:181
  188.4 24.4 %all_to_all.15.rest = bf16[8,32,384]{2,1,0:T(8,128)(2,1)S(1)} all-to-all(bf16[8,32,384]{2,1,0:T(8,128)(2,1)S(1)} %broadcast_in_dim.79), channel_id=1, replica_groups=mesh['zh'=4,'k'=2,'p'=2,'x'=4,'y'=4,'c'=2] {'zh','k'}, dimensions={0} | all-to-all | bytes 393216 | tf_op jit(solution)/shard_map/all_to_all | solution.py:178
  212.8 6.1 %shard_map.65 = bf16[16,2,32,448]{3,2,1,0:T(8,128)(2,1)} custom-call(bf16[8,160,384]{2,1,0:T(8,128)(2,1)S(1)} %bitcast.42, bf16[8,32,384]{2,1,0:T(8,128)(2,1)S(1)} %all_to_all.15.rest, bf16[448,1536]{1,0:T(8,128)(2,1)S(1)} %bitcast.45, bf16[448,1536]{1,0:T(8,128)(2,1)} %collective-permute-done.3.pair_a, bf16[448,1536]{1,0:T(8,128)(2,1)S(1)} %collective-permute-done.2.own_b, ...), custom_call_target="tpu_custom_call" | custom-call | flops 2113929216 | bytes 5505024 | tf_op jit(solution)/shard_map/pallas_call | solution.py:103
  218.9 7.2 %all-to-all-start.1 = ((bf16[16,2,32,448]{3,2,1,0:T(8,128)(2,1)}), bf16[16,2,32,448]{3,2,1,0:T(8,128)(2,1)S(1)}, u32[]{:S(2)}, u32[]{:S(2)}) async-start(bf16[16,2,32,448]{3,2,1,0:T(8,128)(2,1)} %shard_map.65), calls=%async_computation.1 | async-start | bytes 2097152 | tf_op jit(solution)/shard_map/all_to_all | solution.py:184
  226.2 15.3 %all-to-all-done.1 = bf16[16,2,32,448]{3,2,1,0:T(8,128)(2,1)S(1)} async-done(((bf16[16,2,32,448]{3,2,1,0:T(8,128)(2,1)}), bf16[16,2,32,448]{3,2,1,0:T(8,128)(2,1)S(1)}, u32[]{:S(2)}, u32[]{:S(2)}) %all-to-all-start.1) | async-done | bytes 917536 | tf_op jit(solution)/shard_map/all_to_all | solution.py:184
  242.6 6.5 %all-to-all-start.2 = ((bf16[16,8,448]{2,1,0:T(8,128)(2,1)}), bf16[16,8,448]{2,1,0:T(8,128)(2,1)S(1)}, u32[]{:S(2)}, u32[]{:S(2)}) async-start(bf16[16,8,448]{2,1,0:T(8,128)(2,1)} %broadcast_select_fusion), calls=%async_computation.2 | async-start | bytes 262144 | tf_op jit(solution)/shard_map/all_to_all | solution.py:192
  249.2 14.7 %all-to-all-done.2 = bf16[16,8,448]{2,1,0:T(8,128)(2,1)S(1)} async-done(((bf16[16,8,448]{2,1,0:T(8,128)(2,1)}), bf16[16,8,448]{2,1,0:T(8,128)(2,1)S(1)}, u32[]{:S(2)}, u32[]{:S(2)}) %all-to-all-start.2) | async-done | bytes 114720 | tf_op jit(solution)/shard_map/all_to_all | solution.py:192
  (64 shorter events, 10.0 us)
Async XLA Ops:
  6.5 48.6 %copy-start = (bf16[1,1536,448]{1,2,0:T(8,128)(2,1)S(1)}, bf16[1,1536,448]{1,2,0:T(8,128)(2,1)}, u32[]{:S(2)}) copy-start(bf16[1,1536,448]{1,2,0:T(8,128)(2,1)} %param.8) | copy-start | bytes 4128772
  6.5 113.0 %copy-start.5 = (s32[32]{0:T(128)S(1)}, s32[32]{0:T(128)}, u32[]{:S(2)}) copy-start(s32[32]{0:T(128)} %param.11) | copy-start | bytes 388
  6.5 121.4 %all-gather.5.cloned.1.call-start = ((), (), s32[]{:S(2)}) async-start(), calls=%async_computation.3 | async-start | bytes 7798784 | tf_op jit(solution)/shard_map/all_gather | solution.py:144
  39.4 9.0 %collective-permute-start.5 = (bf16[4,4,7168]{2,1,0:T(4,128)(2,1)S(1)}, bf16[4,4,7168]{2,1,0:T(4,128)(2,1)S(1)}, u32[]{:S(2)}, u32[]{:S(2)}) collective-permute-start(bf16[4,4,7168]{2,1,0:T(4,128)(2,1)S(1)} %dynamic-slice_bitcast_fusion), channel_id=1, source_target_pairs={{0,1},{1,0},{2,3},{3,2},{4,5},{5,4},{6,7},{7,6},{8,9},{9,8},{10,11... | collective-permute-start | bytes 688136 | tf_op jit(solution)/shard_map/ppermute | solution.py:140
  49.8 63.1 %collective-permute-start = (bf16[192,7168]{1,0:T(8,128)(2,1)}, bf16[192,7168]{1,0:T(8,128)(2,1)}, u32[]{:S(2)}, u32[]{:S(2)}) collective-permute-start(bf16[192,7168]{1,0:T(8,128)(2,1)} %bitcast.46), channel_id=1, source_target_pairs={{0,32},{32,0},{1,33},{33,1},{2,34},{34,2},{3,35},{35,3},{4,36},{36... | collective-permute-start | bytes 8257544 | tf_op jit(solution)/shard_map/ppermute | solution.py:136
  52.5 60.4 %collective-permute-start.1 = (bf16[192,7168]{1,0:T(8,128)(2,1)}, bf16[192,7168]{1,0:T(8,128)(2,1)S(1)}, u32[]{:S(2)}, u32[]{:S(2)}) collective-permute-start(bf16[192,7168]{1,0:T(8,128)(2,1)} %bitcast.47), channel_id=1, source_target_pairs={{0,1},{1,0},{2,3},{3,2},{4,5},{5,4},{6,7},{7,6},{8,9},{9,8},{10,11... | collective-permute-start | bytes 8257544 | tf_op jit(solution)/shard_map/ppermute | solution.py:146
  55.1 6.7 %collective-permute-start.2 = (bf16[448,1536]{1,0:T(8,128)(2,1)S(1)}, bf16[448,1536]{1,0:T(8,128)(2,1)S(1)}, u32[]{:S(2)}, u32[]{:S(2)}) collective-permute-start(bf16[448,1536]{1,0:T(8,128)(2,1)S(1)} %bitcast.43), channel_id=1, source_target_pairs={{0,1},{1,0},{2,3},{3,2},{4,5},{5,4},{6,7},{7,6},{8,9},{9,8},{10,11... | collective-permute-start | bytes 4128776 | tf_op jit(solution)/shard_map/ppermute | solution.py:148
  112.9 1.5 copy-start.3
  114.5 13.1 %collective-permute-start.4 = (bf16[192,7168]{1,0:T(8,128)(2,1)}, bf16[192,7168]{1,0:T(8,128)(2,1)}, u32[]{:S(2)}, u32[]{:S(2)}) collective-permute-start(bf16[192,7168]{1,0:T(8,128)(2,1)} %collective-permute-done.pair_a), channel_id=1, source_target_pairs={{0,1},{1,0},{2,3},{3,2},{4,5},{5,4},{6,7},{7,6},{8,9},{9,8},{10,11... | collective-permute-start | bytes 8257544 | tf_op jit(solution)/shard_map/ppermute | solution.py:152
  122.6 58.3 %collective-permute-start.3 = (bf16[448,1536]{1,0:T(8,128)(2,1)S(1)}, bf16[448,1536]{1,0:T(8,128)(2,1)}, u32[]{:S(2)}, u32[]{:S(2)}) collective-permute-start(bf16[448,1536]{1,0:T(8,128)(2,1)S(1)} %bitcast.44), channel_id=1, source_target_pairs={{0,32},{32,0},{1,33},{33,1},{2,34},{34,2},{3,35},{35,3},{4,36},{36... | collective-permute-start | bytes 4128776 | tf_op jit(solution)/shard_map/ppermute | solution.py:151
  128.0 1.1 copy-start.1
  129.1 1.8 copy-start.2
  130.9 1.8 copy-start.4
  181.0 31.8 %collective-permute-start.6 = (bf16[448,1536]{1,0:T(8,128)(2,1)}, bf16[448,1536]{1,0:T(8,128)(2,1)S(1)}, u32[]{:S(2)}, u32[]{:S(2)}) collective-permute-start(bf16[448,1536]{1,0:T(8,128)(2,1)} %collective-permute-done.3.pair_a), channel_id=1, source_target_pairs={{0,1},{1,0},{2,3},{3,2},{4,5},{5,4},{6,7},{7,6},{8,9},{9,8},{10,11... | collective-permute-start | bytes 4128776 | tf_op jit(solution)/shard_map/ppermute | solution.py:181
  218.9 22.6 %all-to-all-start.1 = ((bf16[16,2,32,448]{3,2,1,0:T(8,128)(2,1)}), bf16[16,2,32,448]{3,2,1,0:T(8,128)(2,1)S(1)}, u32[]{:S(2)}, u32[]{:S(2)}) async-start(bf16[16,2,32,448]{3,2,1,0:T(8,128)(2,1)} %shard_map.65), calls=%async_computation.1 | async-start | bytes 2097152 | tf_op jit(solution)/shard_map/all_to_all | solution.py:184
  242.6 21.2 %all-to-all-start.2 = ((bf16[16,8,448]{2,1,0:T(8,128)(2,1)}), bf16[16,8,448]{2,1,0:T(8,128)(2,1)S(1)}, u32[]{:S(2)}, u32[]{:S(2)}) async-start(bf16[16,8,448]{2,1,0:T(8,128)(2,1)} %broadcast_select_fusion), calls=%async_computation.2 | async-start | bytes 262144 | tf_op jit(solution)/shard_map/all_to_all | solution.py:192
Sparse Core Ops, SparseCore 0:
  49.9 77.9 all-gather.4

commit v9 on v8

--- a/solution.py
+++ b/solution.py
@@ -55,7 +55,7 @@
 def slotted_hidden(p, own_a, pair_a, own_b, pair_b, tokens, hits):
     rows, width = own_a.shape
     count, slots = tokens.shape[0], hits.shape[1]
-    depth = 1024 if width % 1024 == 0 else width
+    depth = width // 4
     weights = pl.BlockSpec((rows, depth), lambda i, p: (0, i))
     return pl.pallas_call(
         hidden_kernel,
@@ -71,7 +71,7 @@
             scratch_shapes=[pltpu.VMEM((4 * rows, count), jnp.float32)],
         ),
         out_shape=jax.ShapeDtypeStruct((rows, slots), jnp.bfloat16),
-        compiler_params=pltpu.CompilerParams(vmem_limit_bytes=40 * 2**20),
+        compiler_params=pltpu.CompilerParams(vmem_limit_bytes=60 * 2**20),
         cost_estimate=pl.CostEstimate(
             flops=2 * 4 * rows * width * count,
             bytes_accessed=2 * width * (4 * rows + count),
@@ -87,24 +87,25 @@
         pieces += [main[i], rest[i]]
     hidden = jnp.concatenate(pieces, axis=0)
     slots = hidden.shape[1]
-    for z, (d_a, d_b) in enumerate([(own_a, own_b), (pair_a, pair_b)]):
+    outputs = []
+    for d_a, d_b in [(own_a, own_b), (pair_a, pair_b)]:
         of_a = jnp.dot(d_a[...], hidden, preferred_element_type=jnp.float32)
         of_b = jnp.dot(d_b[...], hidden, preferred_element_type=jnp.float32)
         is_a = lax.broadcasted_iota(jnp.int32, of_a.shape, 1) < slots // 2
-        outputs = jnp.where(is_a, of_a, of_b).astype(jnp.bfloat16)
-        summed = lax.dot_general(
-            combine[...], outputs, (((1,), (1,)), ((), ())), preferred_element_type=jnp.float32
-        )
-        out[:, z] = summed.astype(jnp.bfloat16).reshape(out.shape[0], out.shape[2], out.shape[3])
-
-
-def token_sums(main, rest, own_a, pair_a, own_b, pair_b, combine, chips):
+        outputs.append(jnp.where(is_a, of_a, of_b).astype(jnp.bfloat16))
+    outputs = jnp.concatenate(outputs, axis=0)
+    out[...] = lax.dot_general(
+        combine[...], outputs, (((1,), (1,)), ((), ())), preferred_element_type=jnp.float32
+    ).astype(jnp.bfloat16)
+
+
+def token_sums(main, rest, own_a, pair_a, own_b, pair_b, combine):
     features, count = own_a.shape[0], combine.shape[0]
     return pl.pallas_call(
         output_kernel,
         in_specs=[pl.BlockSpec(memory_space=pltpu.VMEM)] * 7,
         out_specs=pl.BlockSpec(memory_space=pltpu.VMEM),
-        out_shape=jax.ShapeDtypeStruct((chips, 2, count // chips, features), jnp.bfloat16),
+        out_shape=jax.ShapeDtypeStruct((count, 2 * features), jnp.bfloat16),
         compiler_params=pltpu.CompilerParams(vmem_limit_bytes=40 * 2**20),
         cost_estimate=pl.CostEstimate(
             flops=8 * features * own_a.shape[1] * combine.shape[1],
@@ -143,14 +144,6 @@
     chip_rows = chip_rows.reshape(2 * far * own, width)
     every = lax.all_gather(chip_rows, PLANE, axis=0, tiled=True)
 
-    w_other = lax.ppermute(w_own, "c", PAIR)
-    d_own = down[0].T
-    d_other = lax.ppermute(d_own, "c", PAIR)
-    w_pair, w_other, d_other = lax.optimization_barrier((w_pair, w_other, d_other))
-    d_later, w_pair = lax.optimization_barrier((d_own, w_pair))
-    d_pair = lax.ppermute(d_later, "p", PAIR)
-    w_pair_other = lax.ppermute(w_pair, "c", PAIR)
-
     ids = of_class(expert_ids.reshape(far * 4, group_rows, -1), core)
     gates = of_class(gate_weights.reshape(far * 4, group_rows, -1), core)
 
@@ -168,7 +161,16 @@
         combine.append(jnp.where(hit, by_row(weights)[:, None], 0.0))
     hits = jnp.concatenate(hits, axis=0)
     combine = (combine[0] + combine[1]).astype(jnp.bfloat16)
-    hits, combine = lax.optimization_barrier((hits, combine))
+
+    w_other = lax.ppermute(w_own, "c", PAIR)
+    d_own = down[0].T
+    d_other = lax.ppermute(d_own, "c", PAIR)
+    w_pair, w_other, d_other, hits, combine = lax.optimization_barrier(
+        (w_pair, w_other, d_other, hits, combine)
+    )
+    d_later, w_pair = lax.optimization_barrier((d_own, w_pair))
+    d_pair = lax.ppermute(d_later, "p", PAIR)
+    w_pair_other = lax.ppermute(w_pair, "c", PAIR)
 
     picked = slotted_hidden(p, w_own, w_pair, w_other, w_pair_other, every, hits)
 
@@ -177,23 +179,24 @@
     rest = jnp.broadcast_to(picked[most:], (members, 2 * units - most, 2 * class_slots))
     rest = lax.all_to_all(rest, RING, split_axis=0, concat_axis=0, tiled=True)
     main = lax.all_gather(picked[:most], RING, axis=0, tiled=False)
-    d_pair, main = lax.optimization_barrier((d_pair, main))
+    d_pair, main, rest = lax.optimization_barrier((d_pair, main, rest))
     d_pair_other = lax.ppermute(d_pair, "c", PAIR)
-    summed = token_sums(main, rest, d_own, d_pair, d_other, d_pair_other, combine, chips)
+    summed = token_sums(main, rest, d_own, d_pair, d_other, d_pair_other, combine)
 
     arrived = lax.all_to_all(summed, PLANE, split_axis=0, concat_axis=0, tiled=True)
-    rows = jnp.sum(arrived.astype(jnp.float32), axis=0).astype(jnp.bfloat16)
-    features = rows.shape[2]
-
-    rows = rows.reshape(2, 2, far, own, features).transpose(2, 1, 0, 3, 4)[:, None]
-    here = (jnp.arange(2) == core)[None, :, None, None, None, None]
-    send = jnp.where(here, rows, jnp.zeros((), rows.dtype))
-    send = send.reshape(far * 4, 2 * own, features)
+    arrived = arrived.reshape(chips, 2 * far * own, arrived.shape[1]).astype(jnp.float32)
+    rows = jnp.sum(arrived, axis=0).astype(jnp.bfloat16)
+    features = rows.shape[1]
+
+    rows = rows.reshape(2, far, own, features).transpose(1, 0, 2, 3)[:, None]
+    here = (jnp.arange(2) == core)[None, :, None, None, None]
+    send = jnp.where(here, rows, jnp.zeros((), rows.dtype)).reshape(far * 4 * own, features)
     recv = lax.all_to_all(send, ("zh", "k", "c"), split_axis=0, concat_axis=0, tiled=True)
-    recv = recv.reshape(far, 2, 2, 2, own, features)
+    recv = recv.reshape(far, 2, 2, own, features)
     recv = lax.dynamic_index_in_dim(recv, k, 2, keepdims=False)
-    recv = jnp.where(p == 0, recv, recv[:, :, ::-1])
-    return recv.transpose(3, 0, 1, 2, 4).reshape(own, width)
+    recv = recv.reshape(far, 2, own, 2, features // 2)
+    recv = jnp.where(p == 0, recv, recv[:, :, :, ::-1])
+    return recv.transpose(2, 0, 1, 3, 4).reshape(own, width)
 
 
 def solution(mesh):

time: 273 us -> 261 us (0.956)
  blocking collectives: 94.8 us -> 72.6 us
  starting transfers between devices: 41.9 us -> 52 us
  local copies, waits for them, and re-layouts: 11.1 us -> 7.45 us
  waiting for transfers between devices: 87.4 us -> 91 us
    all_to_all x1 -> x0, blocking collectives: 24.4 us -> none  [local(): rest = lax.all_to_all(rest, RING, split_axis=0, concat_axis=0, tiled=True)]
    all_to_all x0 -> x1, starting transfers between devices: none -> 11.9 us  [local(): rest = lax.all_to_all(rest, RING, split_axis=0, concat_axis=0, tiled=True)]
    all_gather x1, waiting for transfers between devices: 0.38 us -> 6.87 us  [local(): every = lax.all_gather(chip_rows, PLANE, axis=0, tiled=True)]
    unnamed x12 -> x4, local copies, waits for them, and re-layouts: 6.22 us -> 0.01 us
    ppermute x1, waiting for transfers between devices: 4.73 us -> 0.01 us  [local(): d_other = lax.ppermute(d_own, 'c', PAIR)]
    all_to_all x1, starting transfers between devices: 6.54 us -> 9.57 us  [local(): lax.all_to_all(send, ('zh', 'k', 'c'), split_axis=0, concat_axis=0, tiled...]
    ppermute x1, waiting for transfers between devices: 0.01 us -> 2.94 us  [local(): d_pair_other = lax.ppermute(d_pair, 'c', PAIR)]
  transfers between devices with their start and end apart: 10 -> 11, of which waited for: 6 -> 7; matrix products, arithmetic and copies ran while one was open for 3% -> 4% of each run, Pallas kernels for 4% -> 4%
where the time goes in v9:
time: 261 us; the launch traced here: 260 us
  waiting for transfers between devices  91 us (35%)
  blocking collectives  72.6 us (28%)
  starting transfers between devices  52 us (20%)
  Pallas kernels  17.7 us (7%)
  between operations  13.6 us (5%)
  local copies, waits for them, and re-layouts  7.45 us (3%)
  other arithmetic  5.9 us (2%)
    ppermute x1, waiting for transfers between devices, local(): w_pair = lax.ppermute(w_own, 'p', PAIR)  48.7 us
    all_gather x1, blocking collectives, local(): main = lax.all_gather(picked[:most], RING, axis=0, tiled=False)  39.9 us
    all_gather x1, blocking collectives, local(): lax.all_gather(tokens, RING, axis=0, tiled=False)  32.8 us
    all_to_all x1, waiting for transfers between devices, local(): lax.all_to_all(send, ('zh', 'k', 'c'), split_axis=0, concat_axis=0, tiled...  15.2 us
    all_to_all x1, waiting for transfers between devices, local(): lax.all_to_all(summed, PLANE, split_axis=0, concat_axis=0, tiled=True)  13.8 us
    all_to_all x1, starting transfers between devices, local(): rest = lax.all_to_all(rest, RING, split_axis=0, concat_axis=0, tiled=True)  11.9 us
    pallas_call x1, Pallas kernels, slotted_hidden(): pl.pallas_call(hidden_kernel, grid_spec=pltpu.PrefetchScalarGridSpec(num_...  11.5 us
    all_to_all x1, starting transfers between devices, local(): lax.all_to_all(send, ('zh', 'k', 'c'), split_axis=0, concat_axis=0, tiled...  9.57 us
  transfers between devices with their start and end apart: 11, of which 7 were waited for; matrix products, arithmetic and copies ran while one was open for 4% of the time, Pallas kernels for 4%

profile of v9, /device:TPU:1, one launch (start us, length us, event | category | flops | bytes accessed | tf_op | source)
XLA Modules:
  0.0 260.4 jit_solution(9619701552384388453)
XLA Ops:
  6.5 32.8 %all-gather.2 = bf16[8,4,7168]{2,1,0:T(4,128)(2,1)S(1)} all-gather(bf16[1,4,7168]{2,1,0:T(4,128)(2,1)} %bitcast.58), channel_id=2, replica_groups=mesh['zh'=4,'k'=2,'p'=2,'x'=4,'y'=4,'c'=2] {'zh','k'}, dimensions={0}, use_global_device_ids=true | all-gather | bytes 516096 | tf_op jit(solution)/shard_map/all_gather | solution.py:139
  39.4 7.9 %collective-permute-start.5 = (bf16[4,4,7168]{2,1,0:T(4,128)(2,1)S(1)}, bf16[4,4,7168]{2,1,0:T(4,128)(2,1)S(1)}, u32[]{:S(2)}, u32[]{:S(2)}) collective-permute-start(bf16[4,4,7168]{2,1,0:T(4,128)(2,1)S(1)} %dynamic-slice_bitcast_fusion), channel_id=1, source_target_pairs={{0,1},{1,0},{2,3},{3,2},{4,5},{5,4},{6,7},{7,6},{8,9},{9,8},{10,11... | collective-permute-start | bytes 688136 | tf_op jit(solution)/shard_map/ppermute | solution.py:141
  47.3 1.1 collective-permute-done.5
  49.8 2.7 %collective-permute-start = (bf16[192,7168]{1,0:T(8,128)(2,1)}, bf16[192,7168]{1,0:T(8,128)(2,1)}, u32[]{:S(2)}, u32[]{:S(2)}) collective-permute-start(bf16[192,7168]{1,0:T(8,128)(2,1)} %bitcast.61), channel_id=1, source_target_pairs={{0,32},{32,0},{1,33},{33,1},{2,34},{34,2},{3,35},{35,3},{4,36},{36... | collective-permute-start | bytes 8257544 | tf_op jit(solution)/shard_map/ppermute | solution.py:137
  52.5 2.6 collective-permute-start.1
  55.1 1.9 collective-permute-start.2
  59.6 1.3 fusion.3
  62.8 1.0 add_convert_fusion.hits
  64.2 48.7 %collective-permute-done.pair_a = bf16[192,7168]{1,0:T(8,128)(2,1)} collective-permute-done((bf16[192,7168]{1,0:T(8,128)(2,1)}, bf16[192,7168]{1,0:T(8,128)(2,1)}, u32[]{:S(2)}, u32[]{:S(2)}) %collective-permute-start) | collective-permute-done | bytes 2752544 | tf_op jit(solution)/shard_map/ppermute | solution.py:137
  112.9 3.1 %collective-permute-start.4 = (bf16[192,7168]{1,0:T(8,128)(2,1)}, bf16[192,7168]{1,0:T(8,128)(2,1)}, u32[]{:S(2)}, u32[]{:S(2)}) collective-permute-start(bf16[192,7168]{1,0:T(8,128)(2,1)} %collective-permute-done.pair_a), channel_id=1, source_target_pairs={{0,1},{1,0},{2,3},{3,2},{4,5},{5,4},{6,7},{7,6},{8,9},{9,8},{10,11... | collective-permute-start | bytes 8257544 | tf_op jit(solution)/shard_map/ppermute | solution.py:173
  116.0 2.7 %collective-permute-start.3 = (bf16[448,1536]{1,0:T(8,128)(2,1)S(1)}, bf16[448,1536]{1,0:T(8,128)(2,1)}, u32[]{:S(2)}, u32[]{:S(2)}) collective-permute-start(bf16[448,1536]{1,0:T(8,128)(2,1)S(1)} %bitcast.47), channel_id=1, source_target_pairs={{0,32},{32,0},{1,33},{33,1},{2,34},{34,2},{3,35},{35,3},{4,36},{36... | collective-permute-start | bytes 4128776 | tf_op jit(solution)/shard_map/ppermute | solution.py:172
  118.7 2.3 collective-permute-done.4.pair_b
  121.1 6.9 %all-gather.5.cloned.1.call-done.tokens = bf16[512,7168]{1,0:T(8,128)(2,1)} async-done(((bf16[32,7168]{1,0:T(8,128)(2,1)}), bf16[512,7168]{1,0:T(8,128)(2,1)}) %all-gather.5.cloned.1.call-update) | async-done | bytes 7340048 | tf_op jit(solution)/shard_map/all_gather | solution.py:145
  127.9 11.5 %shard_map.64 = bf16[192,384]{1,0:T(8,128)(2,1)} custom-call(s32[1]{0:T(128)} %bitcast.16.p_ref, bf16[192,7168]{1,0:T(8,128)(2,1)} %bitcast.63, bf16[192,7168]{1,0:T(8,128)(2,1)} %collective-permute-done.pair_a, bf16[192,7168]{1,0:T(8,128)(2,1)} %collective-permute-done.1.own_b, bf16[192,7168]{1,0:T(8,128)(2,1)} %collective-permute-done.4.pair_b, ...), custom_call_target="tpu_custom_call" | custom-call | flops 5637144576 | bytes 18350080 | tf_op jit(solution)/shard_map/pallas_call | solution.py:60
  140.8 11.9 %all-to-all-start = ((bf16[8,32,384]{2,1,0:T(8,128)(2,1)}), bf16[8,32,384]{2,1,0:T(8,128)(2,1)S(1)}, u32[]{:S(2)}, u32[]{:S(2)}) async-start(bf16[8,32,384]{2,1,0:T(8,128)(2,1)} %broadcast_in_dim.79), calls=%async_computation | async-start | bytes 393216 | tf_op jit(solution)/shard_map/all_to_all | solution.py:180
  152.8 0.9 slice.8
  153.7 39.9 %all-gather.1 = bf16[1280,384]{1,0:T(8,128)(2,1)S(1)} all-gather(bf16[160,384]{1,0:T(8,128)(2,1)S(1)} %slice.8), channel_id=3, replica_groups=mesh['zh'=4,'k'=2,'p'=2,'x'=4,'y'=4,'c'=2] {'zh','k'}, dimensions={0}, use_global_device_ids=true | all-gather | bytes 1105920 | tf_op jit(solution)/shard_map/all_gather | solution.py:181
  193.5 4.7 %collective-permute-start.6 = (bf16[448,1536]{1,0:T(8,128)(2,1)}, bf16[448,1536]{1,0:T(8,128)(2,1)S(1)}, u32[]{:S(2)}, u32[]{:S(2)}) collective-permute-start(bf16[448,1536]{1,0:T(8,128)(2,1)} %collective-permute-done.3.pair_a), channel_id=1, source_target_pairs={{0,1},{1,0},{2,3},{3,2},{4,5},{5,4},{6,7},{7,6},{8,9},{9,8},{10,11... | collective-permute-start | bytes 4128776 | tf_op jit(solution)/shard_map/ppermute | solution.py:183
  198.3 2.9 %collective-permute-done.6.pair_b = bf16[448,1536]{1,0:T(8,128)(2,1)S(1)} collective-permute-done((bf16[448,1536]{1,0:T(8,128)(2,1)}, bf16[448,1536]{1,0:T(8,128)(2,1)S(1)}, u32[]{:S(2)}, u32[]{:S(2)}) %collective-permute-start.6) | collective-permute-done | bytes 1376288 | tf_op jit(solution)/shard_map/ppermute | solution.py:183
  201.2 6.2 %shard_map.65 = bf16[512,896]{1,0:T(8,128)(2,1)} custom-call(bf16[8,160,384]{2,1,0:T(8,128)(2,1)S(1)} %bitcast.45, bf16[8,32,384]{2,1,0:T(8,128)(2,1)S(1)} %all-to-all-done.rest, bf16[448,1536]{1,0:T(8,128)(2,1)S(1)} %bitcast.48, bf16[448,1536]{1,0:T(8,128)(2,1)} %collective-permute-done.3.pair_a, bf16[448,1536]{1,0:T(8,128)(2,1)} %collective-permute-done.2.own_b, ...), custom_call_target="tpu_custom_call" | custom-call | flops 2113929216 | bytes 5505024 | tf_op jit(solution)/shard_map/pallas_call | solution.py:104
  207.4 5.0 %all-to-all-start.1 = ((bf16[16,32,896]{2,1,0:T(8,128)(2,1)}), bf16[16,32,896]{2,1,0:T(8,128)(2,1)S(1)}, u32[]{:S(2)}, u32[]{:S(2)}) async-start(bf16[16,32,896]{2,1,0:T(8,128)(2,1)} %bitcast.24), calls=%async_computation.1 | async-start | bytes 1835008 | tf_op jit(solution)/shard_map/all_to_all | solution.py:186
  212.6 13.8 %all-to-all-done.1 = bf16[16,32,896]{2,1,0:T(8,128)(2,1)S(1)} async-done(((bf16[16,32,896]{2,1,0:T(8,128)(2,1)}), bf16[16,32,896]{2,1,0:T(8,128)(2,1)S(1)}, u32[]{:S(2)}, u32[]{:S(2)}) %all-to-all-start.1) | async-done | bytes 917536 | tf_op jit(solution)/shard_map/all_to_all | solution.py:186
  227.3 9.6 %all-to-all-start.2 = ((bf16[16,4,896]{2,1,0:T(4,128)(2,1)}), bf16[16,4,896]{2,1,0:T(4,128)(2,1)S(1)}, u32[]{:S(2)}, u32[]{:S(2)}) async-start(bf16[16,4,896]{2,1,0:T(4,128)(2,1)} %bitcast_select_fusion.2), calls=%async_computation.2 | async-start | bytes 229376 | tf_op jit(solution)/shard_map/all_to_all | solution.py:194
  236.9 15.2 %all-to-all-done.2 = bf16[16,4,896]{2,1,0:T(4,128)(2,1)S(1)} async-done(((bf16[16,4,896]{2,1,0:T(4,128)(2,1)}), bf16[16,4,896]{2,1,0:T(4,128)(2,1)S(1)}, u32[]{:S(2)}, u32[]{:S(2)}) %all-to-all-start.2) | async-done | bytes 114720 | tf_op jit(solution)/shard_map/all_to_all | solution.py:194
  (55 shorter events, 10.2 us)
Async XLA Ops:
  6.5 48.5 %copy-start = (bf16[1,1536,448]{1,2,0:T(8,128)(2,1)S(1)}, bf16[1,1536,448]{1,2,0:T(8,128)(2,1)}, u32[]{:S(2)}) copy-start(bf16[1,1536,448]{1,2,0:T(8,128)(2,1)} %param.8) | copy-start | bytes 4128772
  6.5 52.5 %copy-start.1 = (s32[32]{0:T(128)S(1)}, s32[32]{0:T(128)}, u32[]{:S(2)}) copy-start(s32[32]{0:T(128)} %param.11) | copy-start | bytes 388
  6.5 121.4 %all-gather.5.cloned.1.call-start = ((), (), s32[]{:S(2)}) async-start(), calls=%async_computation.3 | async-start | bytes 7798784 | tf_op jit(solution)/shard_map/all_gather | solution.py:145
  39.4 9.0 %collective-permute-start.5 = (bf16[4,4,7168]{2,1,0:T(4,128)(2,1)S(1)}, bf16[4,4,7168]{2,1,0:T(4,128)(2,1)S(1)}, u32[]{:S(2)}, u32[]{:S(2)}) collective-permute-start(bf16[4,4,7168]{2,1,0:T(4,128)(2,1)S(1)} %dynamic-slice_bitcast_fusion), channel_id=1, source_target_pairs={{0,1},{1,0},{2,3},{3,2},{4,5},{5,4},{6,7},{7,6},{8,9},{9,8},{10,11... | collective-permute-start | bytes 688136 | tf_op jit(solution)/shard_map/ppermute | solution.py:141
  49.8 63.1 %collective-permute-start = (bf16[192,7168]{1,0:T(8,128)(2,1)}, bf16[192,7168]{1,0:T(8,128)(2,1)}, u32[]{:S(2)}, u32[]{:S(2)}) collective-permute-start(bf16[192,7168]{1,0:T(8,128)(2,1)} %bitcast.61), channel_id=1, source_target_pairs={{0,32},{32,0},{1,33},{33,1},{2,34},{34,2},{3,35},{35,3},{4,36},{36... | collective-permute-start | bytes 8257544 | tf_op jit(solution)/shard_map/ppermute | solution.py:137
  52.5 60.4 %collective-permute-start.1 = (bf16[192,7168]{1,0:T(8,128)(2,1)}, bf16[192,7168]{1,0:T(8,128)(2,1)}, u32[]{:S(2)}, u32[]{:S(2)}) collective-permute-start(bf16[192,7168]{1,0:T(8,128)(2,1)} %bitcast.62), channel_id=1, source_target_pairs={{0,1},{1,0},{2,3},{3,2},{4,5},{5,4},{6,7},{7,6},{8,9},{9,8},{10,11... | collective-permute-start | bytes 8257544 | tf_op jit(solution)/shard_map/ppermute | solution.py:165
  55.1 9.1 %collective-permute-start.2 = (bf16[448,1536]{1,0:T(8,128)(2,1)S(1)}, bf16[448,1536]{1,0:T(8,128)(2,1)}, u32[]{:S(2)}, u32[]{:S(2)}) collective-permute-start(bf16[448,1536]{1,0:T(8,128)(2,1)S(1)} %bitcast.46), channel_id=1, source_target_pairs={{0,1},{1,0},{2,3},{3,2},{4,5},{5,4},{6,7},{7,6},{8,9},{9,8},{10,11... | collective-permute-start | bytes 4128776 | tf_op jit(solution)/shard_map/ppermute | solution.py:167
  112.9 8.2 %collective-permute-start.4 = (bf16[192,7168]{1,0:T(8,128)(2,1)}, bf16[192,7168]{1,0:T(8,128)(2,1)}, u32[]{:S(2)}, u32[]{:S(2)}) collective-permute-start(bf16[192,7168]{1,0:T(8,128)(2,1)} %collective-permute-done.pair_a), channel_id=1, source_target_pairs={{0,1},{1,0},{2,3},{3,2},{4,5},{5,4},{6,7},{7,6},{8,9},{9,8},{10,11... | collective-permute-start | bytes 8257544 | tf_op jit(solution)/shard_map/ppermute | solution.py:173
  116.0 77.5 %collective-permute-start.3 = (bf16[448,1536]{1,0:T(8,128)(2,1)S(1)}, bf16[448,1536]{1,0:T(8,128)(2,1)}, u32[]{:S(2)}, u32[]{:S(2)}) collective-permute-start(bf16[448,1536]{1,0:T(8,128)(2,1)S(1)} %bitcast.47), channel_id=1, source_target_pairs={{0,32},{32,0},{1,33},{33,1},{2,34},{34,2},{3,35},{35,3},{4,36},{36... | collective-permute-start | bytes 4128776 | tf_op jit(solution)/shard_map/ppermute | solution.py:172
  140.8 52.7 %all-to-all-start = ((bf16[8,32,384]{2,1,0:T(8,128)(2,1)}), bf16[8,32,384]{2,1,0:T(8,128)(2,1)S(1)}, u32[]{:S(2)}, u32[]{:S(2)}) async-start(bf16[8,32,384]{2,1,0:T(8,128)(2,1)} %broadcast_in_dim.79), calls=%async_computation | async-start | bytes 393216 | tf_op jit(solution)/shard_map/all_to_all | solution.py:180
  193.5 7.7 %collective-permute-start.6 = (bf16[448,1536]{1,0:T(8,128)(2,1)}, bf16[448,1536]{1,0:T(8,128)(2,1)S(1)}, u32[]{:S(2)}, u32[]{:S(2)}) collective-permute-start(bf16[448,1536]{1,0:T(8,128)(2,1)} %collective-permute-done.3.pair_a), channel_id=1, source_target_pairs={{0,1},{1,0},{2,3},{3,2},{4,5},{5,4},{6,7},{7,6},{8,9},{9,8},{10,11... | collective-permute-start | bytes 4128776 | tf_op jit(solution)/shard_map/ppermute | solution.py:183
  207.4 19.0 %all-to-all-start.1 = ((bf16[16,32,896]{2,1,0:T(8,128)(2,1)}), bf16[16,32,896]{2,1,0:T(8,128)(2,1)S(1)}, u32[]{:S(2)}, u32[]{:S(2)}) async-start(bf16[16,32,896]{2,1,0:T(8,128)(2,1)} %bitcast.24), calls=%async_computation.1 | async-start | bytes 1835008 | tf_op jit(solution)/shard_map/all_to_all | solution.py:186
  227.3 24.8 %all-to-all-start.2 = ((bf16[16,4,896]{2,1,0:T(4,128)(2,1)}), bf16[16,4,896]{2,1,0:T(4,128)(2,1)S(1)}, u32[]{:S(2)}, u32[]{:S(2)}) async-start(bf16[16,4,896]{2,1,0:T(4,128)(2,1)} %bitcast_select_fusion.2), calls=%async_computation.2 | async-start | bytes 229376 | tf_op jit(solution)/shard_map/all_to_all | solution.py:194
Sparse Core Ops, SparseCore 0:
  49.9 77.9 all-gather.4

commit v10 on v9

--- a/solution.py
+++ b/solution.py
@@ -165,11 +165,13 @@
     w_other = lax.ppermute(w_own, "c", PAIR)
     d_own = down[0].T
     d_other = lax.ppermute(d_own, "c", PAIR)
-    w_pair, w_other, d_other, hits, combine = lax.optimization_barrier(
-        (w_pair, w_other, d_other, hits, combine)
+    line = far * 4
+    swap = [(z, (z + 1) % line if z % 2 else (z - 1) % line) for z in range(line)]
+    d_pair = lax.ppermute(d_own, LINE, swap)
+    d_pair_other = lax.ppermute(d_pair, "c", PAIR)
+    w_pair, w_other, d_other, d_pair_other, hits, combine = lax.optimization_barrier(
+        (w_pair, w_other, d_other, d_pair_other, hits, combine)
     )
-    d_later, w_pair = lax.optimization_barrier((d_own, w_pair))
-    d_pair = lax.ppermute(d_later, "p", PAIR)
     w_pair_other = lax.ppermute(w_pair, "c", PAIR)
 
     picked = slotted_hidden(p, w_own, w_pair, w_other, w_pair_other, every, hits)
@@ -179,8 +181,6 @@
     rest = jnp.broadcast_to(picked[most:], (members, 2 * units - most, 2 * class_slots))
     rest = lax.all_to_all(rest, RING, split_axis=0, concat_axis=0, tiled=True)
     main = lax.all_gather(picked[:most], RING, axis=0, tiled=False)
-    d_pair, main, rest = lax.optimization_barrier((d_pair, main, rest))
-    d_pair_other = lax.ppermute(d_pair, "c", PAIR)
     summed = token_sums(main, rest, d_own, d_pair, d_other, d_pair_other, combine)
 
     arrived = lax.all_to_all(summed, PLANE, split_axis=0, concat_axis=0, tiled=True)
@@ -194,9 +194,11 @@
     recv = lax.all_to_all(send, ("zh", "k", "c"), split_axis=0, concat_axis=0, tiled=True)
     recv = recv.reshape(far, 2, 2, own, features)
     recv = lax.dynamic_index_in_dim(recv, k, 2, keepdims=False)
-    recv = recv.reshape(far, 2, own, 2, features // 2)
-    recv = jnp.where(p == 0, recv, recv[:, :, :, ::-1])
-    return recv.transpose(2, 0, 1, 3, 4).reshape(own, width)
+    recv = recv.reshape(far * 2, own, 2, features // 2)
+    own_z, pair_z = recv[:, :, 0], recv[:, :, 1]
+    even = jnp.where(p == 0, own_z, jnp.roll(pair_z, 1, axis=0))
+    odd = jnp.where(p == 0, jnp.roll(pair_z, -1, axis=0), own_z)
+    return jnp.stack([even, odd], axis=1).transpose(2, 0, 1, 3).reshape(own, width)
 
 
 def solution(mesh):

time: 261 us -> 252 us (0.966)
  waiting for transfers between devices: 91 us -> 82.4 us
    ppermute x1, waiting for transfers between devices: 0.01 us -> 22.9 us  [local(): d_pair = lax.ppermute(d_own, LINE, swap)]
    ppermute x1, waiting for transfers between devices: 48.7 us -> 26.4 us  [local(): w_pair = lax.ppermute(w_own, 'p', PAIR)]
    all_gather x1, waiting for transfers between devices: 6.87 us -> 0.5 us  [local(): every = lax.all_gather(chip_rows, PLANE, axis=0, tiled=True)]
    ppermute x1, waiting for transfers between devices: 2.94 us -> 0.01 us  [local(): d_pair_other = lax.ppermute(d_pair, 'c', PAIR)]
    ppermute x1, waiting for transfers between devices: 2.34 us -> 5.04 us  [local(): w_pair_other = lax.ppermute(w_pair, 'c', PAIR)]
    all_to_all x1, waiting for transfers between devices: 13.8 us -> 11.1 us  [local(): lax.all_to_all(summed, PLANE, split_axis=0, concat_axis=0, tiled=True)]
  transfers between devices with their start and end apart: 11 -> 11, of which waited for: 7 -> 7; matrix products, arithmetic and copies ran while one was open for 4% -> 3% of each run, Pallas kernels for 4% -> 0%
where the time goes in v10:
time: 252 us; the launch traced here: 251 us
  waiting for transfers between devices  82.4 us (33%)
  blocking collectives  71.9 us (29%)
  starting transfers between devices  51.8 us (21%)
  Pallas kernels  18.2 us (7%)
  between operations  13.7 us (5%)
  local copies, waits for them, and re-layouts  7.25 us (3%)
  other arithmetic  5.97 us (2%)
    all_gather x1, blocking collectives, local(): main = lax.all_gather(picked[:most], RING, axis=0, tiled=False)  39.1 us
    all_gather x1, blocking collectives, local(): lax.all_gather(tokens, RING, axis=0, tiled=False)  32.8 us
    ppermute x1, waiting for transfers between devices, local(): w_pair = lax.ppermute(w_own, 'p', PAIR)  26.4 us
    ppermute x1, waiting for transfers between devices, local(): d_pair = lax.ppermute(d_own, LINE, swap)  22.9 us
    all_to_all x1, waiting for transfers between devices, local(): lax.all_to_all(send, ('zh', 'k', 'c'), split_axis=0, concat_axis=0, tiled...  15.3 us
    all_to_all x1, starting transfers between devices, local(): rest = lax.all_to_all(rest, RING, split_axis=0, concat_axis=0, tiled=True)  11.9 us
    pallas_call x1, Pallas kernels, slotted_hidden(): pl.pallas_call(hidden_kernel, grid_spec=pltpu.PrefetchScalarGridSpec(num_...  11.5 us
    all_to_all x1, waiting for transfers between devices, local(): lax.all_to_all(summed, PLANE, split_axis=0, concat_axis=0, tiled=True)  11.1 us
  transfers between devices with their start and end apart: 11, of which 7 were waited for; matrix products, arithmetic and copies ran while one was open for 3% of the time, Pallas kernels for 0%

profile of v10, /device:TPU:1, one launch (start us, length us, event | category | flops | bytes accessed | tf_op | source)
XLA Modules:
  0.0 251.2 jit_solution(10266303889625711751)
XLA Ops:
  6.5 32.8 %all-gather.2 = bf16[8,4,7168]{2,1,0:T(4,128)(2,1)S(1)} all-gather(bf16[1,4,7168]{2,1,0:T(4,128)(2,1)} %bitcast.75), channel_id=2, replica_groups=mesh['zh'=4,'k'=2,'p'=2,'x'=4,'y'=4,'c'=2] {'zh','k'}, dimensions={0}, use_global_device_ids=true | all-gather | bytes 516096 | tf_op jit(solution)/shard_map/all_gather | solution.py:139
  39.4 7.9 %collective-permute-start.6 = (bf16[4,4,7168]{2,1,0:T(4,128)(2,1)S(1)}, bf16[4,4,7168]{2,1,0:T(4,128)(2,1)S(1)}, u32[]{:S(2)}, u32[]{:S(2)}) collective-permute-start(bf16[4,4,7168]{2,1,0:T(4,128)(2,1)S(1)} %dynamic-slice_bitcast_fusion), channel_id=1, source_target_pairs={{0,1},{1,0},{2,3},{3,2},{4,5},{5,4},{6,7},{7,6},{8,9},{9,8},{10,11... | collective-permute-start | bytes 688136 | tf_op jit(solution)/shard_map/ppermute | solution.py:141
  47.3 1.1 collective-permute-done.6
  48.9 0.9 reshape.179
  49.8 3.8 %collective-permute-start.3 = (bf16[448,1536]{1,0:T(8,128)(2,1)S(1)}, bf16[448,1536]{1,0:T(8,128)(2,1)}, u32[]{:S(2)}, u32[]{:S(2)}) collective-permute-start(bf16[448,1536]{1,0:T(8,128)(2,1)S(1)} %bitcast.60), channel_id=1, source_target_pairs={{0,480},{32,64},{64,32},{96,128},{128,96},{160,192},{192,160},{224... | collective-permute-start | bytes 4128776 | tf_op jit(solution)/shard_map/ppermute | solution.py:170
  53.6 2.6 %collective-permute-start.1 = (bf16[192,7168]{1,0:T(8,128)(2,1)}, bf16[192,7168]{1,0:T(8,128)(2,1)}, u32[]{:S(2)}, u32[]{:S(2)}) collective-permute-start(bf16[192,7168]{1,0:T(8,128)(2,1)} %bitcast.78), channel_id=1, source_target_pairs={{0,1},{1,0},{2,3},{3,2},{4,5},{5,4},{6,7},{7,6},{8,9},{9,8},{10,11... | collective-permute-start | bytes 8257544 | tf_op jit(solution)/shard_map/ppermute | solution.py:165
  56.2 1.9 collective-permute-start
  58.1 1.9 collective-permute-start.2
  61.5 22.9 %collective-permute-done.3.pair_a = bf16[448,1536]{1,0:T(8,128)(2,1)} collective-permute-done((bf16[448,1536]{1,0:T(8,128)(2,1)S(1)}, bf16[448,1536]{1,0:T(8,128)(2,1)}, u32[]{:S(2)}, u32[]{:S(2)}) %collective-permute-start.3) | collective-permute-done | bytes 1376288 | tf_op jit(solution)/shard_map/ppermute | solution.py:170
  84.4 3.1 %collective-permute-start.4 = (bf16[448,1536]{1,0:T(8,128)(2,1)}, bf16[448,1536]{1,0:T(8,128)(2,1)}, u32[]{:S(2)}, u32[]{:S(2)}) collective-permute-start(bf16[448,1536]{1,0:T(8,128)(2,1)} %collective-permute-done.3.pair_a), channel_id=1, source_target_pairs={{0,1},{1,0},{2,3},{3,2},{4,5},{5,4},{6,7},{7,6},{8,9},{9,8},{10,11... | collective-permute-start | bytes 4128776 | tf_op jit(solution)/shard_map/ppermute | solution.py:171
  88.7 1.3 fusion.2
  91.9 1.0 add_convert_fusion.hits
  93.3 26.4 %collective-permute-done.pair_a = bf16[192,7168]{1,0:T(8,128)(2,1)} collective-permute-done((bf16[192,7168]{1,0:T(8,128)(2,1)}, bf16[192,7168]{1,0:T(8,128)(2,1)}, u32[]{:S(2)}, u32[]{:S(2)}) %collective-permute-start) | collective-permute-done | bytes 2752544 | tf_op jit(solution)/shard_map/ppermute | solution.py:137
  119.7 2.7 %collective-permute-start.5 = (bf16[192,7168]{1,0:T(8,128)(2,1)}, bf16[192,7168]{1,0:T(8,128)(2,1)}, u32[]{:S(2)}, u32[]{:S(2)}) collective-permute-start(bf16[192,7168]{1,0:T(8,128)(2,1)} %collective-permute-done.pair_a), channel_id=1, source_target_pairs={{0,1},{1,0},{2,3},{3,2},{4,5},{5,4},{6,7},{7,6},{8,9},{9,8},{10,11... | collective-permute-start | bytes 8257544 | tf_op jit(solution)/shard_map/ppermute | solution.py:175
  122.4 5.0 %collective-permute-done.5.pair_b = bf16[192,7168]{1,0:T(8,128)(2,1)} collective-permute-done((bf16[192,7168]{1,0:T(8,128)(2,1)}, bf16[192,7168]{1,0:T(8,128)(2,1)}, u32[]{:S(2)}, u32[]{:S(2)}) %collective-permute-start.5) | collective-permute-done | bytes 2752544 | tf_op jit(solution)/shard_map/ppermute | solution.py:175
  127.9 11.5 %shard_map.64 = bf16[192,384]{1,0:T(8,128)(2,1)} custom-call(s32[1]{0:T(128)} %bitcast.p_ref, bf16[192,7168]{1,0:T(8,128)(2,1)} %bitcast.80, bf16[192,7168]{1,0:T(8,128)(2,1)} %collective-permute-done.pair_a, bf16[192,7168]{1,0:T(8,128)(2,1)} %collective-permute-done.1.own_b, bf16[192,7168]{1,0:T(8,128)(2,1)} %collective-permute-done.5.pair_b, ...), custom_call_target="tpu_custom_call" | custom-call | flops 5637144576 | bytes 18350080 | tf_op jit(solution)/shard_map/pallas_call | solution.py:60
  140.9 11.9 %all-to-all-start = ((bf16[8,32,384]{2,1,0:T(8,128)(2,1)}), bf16[8,32,384]{2,1,0:T(8,128)(2,1)S(1)}, u32[]{:S(2)}, u32[]{:S(2)}) async-start(bf16[8,32,384]{2,1,0:T(8,128)(2,1)} %broadcast_in_dim.79), calls=%async_computation | async-start | bytes 393216 | tf_op jit(solution)/shard_map/all_to_all | solution.py:182
  152.8 0.9 slice.41
  153.7 39.1 %all-gather.1 = bf16[1280,384]{1,0:T(8,128)(2,1)S(1)} all-gather(bf16[160,384]{1,0:T(8,128)(2,1)S(1)} %slice.41), channel_id=3, replica_groups=mesh['zh'=4,'k'=2,'p'=2,'x'=4,'y'=4,'c'=2] {'zh','k'}, dimensions={0}, use_global_device_ids=true | all-gather | bytes 1105920 | tf_op jit(solution)/shard_map/all_gather | solution.py:183
  192.8 6.6 %shard_map.65 = bf16[512,896]{1,0:T(8,128)(2,1)} custom-call(bf16[8,160,384]{2,1,0:T(8,128)(2,1)S(1)} %bitcast.59, bf16[8,32,384]{2,1,0:T(8,128)(2,1)S(1)} %all-to-all-done.rest, bf16[448,1536]{1,0:T(8,128)(2,1)S(1)} %bitcast.62, bf16[448,1536]{1,0:T(8,128)(2,1)} %collective-permute-done.3.pair_a, bf16[448,1536]{1,0:T(8,128)(2,1)} %collective-permute-done.2.own_b, ...), custom_call_target="tpu_custom_call" | custom-call | flops 2113929216 | bytes 5505024 | tf_op jit(solution)/shard_map/pallas_call | solution.py:104
  199.5 5.2 %all-to-all-start.1 = ((bf16[16,32,896]{2,1,0:T(8,128)(2,1)}), bf16[16,32,896]{2,1,0:T(8,128)(2,1)S(1)}, u32[]{:S(2)}, u32[]{:S(2)}) async-start(bf16[16,32,896]{2,1,0:T(8,128)(2,1)} %bitcast.24), calls=%async_computation.1 | async-start | bytes 1835008 | tf_op jit(solution)/shard_map/all_to_all | solution.py:186
  204.9 11.1 %all-to-all-done.1 = bf16[16,32,896]{2,1,0:T(8,128)(2,1)S(1)} async-done(((bf16[16,32,896]{2,1,0:T(8,128)(2,1)}), bf16[16,32,896]{2,1,0:T(8,128)(2,1)S(1)}, u32[]{:S(2)}, u32[]{:S(2)}) %all-to-all-start.1) | async-done | bytes 917536 | tf_op jit(solution)/shard_map/all_to_all | solution.py:186
  216.9 10.8 %all-to-all-start.2 = ((bf16[16,4,896]{2,1,0:T(4,128)(2,1)}), bf16[16,4,896]{2,1,0:T(4,128)(2,1)S(1)}, u32[]{:S(2)}, u32[]{:S(2)}) async-start(bf16[16,4,896]{2,1,0:T(4,128)(2,1)} %bitcast_select_fusion.2), calls=%async_computation.2 | async-start | bytes 229376 | tf_op jit(solution)/shard_map/all_to_all | solution.py:194
  227.8 15.3 %all-to-all-done.2 = bf16[16,4,896]{2,1,0:T(4,128)(2,1)S(1)} async-done(((bf16[16,4,896]{2,1,0:T(4,128)(2,1)}), bf16[16,4,896]{2,1,0:T(4,128)(2,1)S(1)}, u32[]{:S(2)}, u32[]{:S(2)}) %all-to-all-start.2) | async-done | bytes 114720 | tf_op jit(solution)/shard_map/all_to_all | solution.py:194
  (59 shorter events, 9.6 us)
Async XLA Ops:
  6.5 43.3 %copy-start = (bf16[1,1536,448]{1,2,0:T(8,128)(2,1)S(1)}, bf16[1,1536,448]{1,2,0:T(8,128)(2,1)}, u32[]{:S(2)}) copy-start(bf16[1,1536,448]{1,2,0:T(8,128)(2,1)} %param.8) | copy-start | bytes 4128772
  6.5 81.5 %copy-start.1 = (s32[32]{0:T(128)S(1)}, s32[32]{0:T(128)}, u32[]{:S(2)}) copy-start(s32[32]{0:T(128)} %param.11) | copy-start | bytes 388
  6.5 121.4 %all-gather.5.cloned.1.call-start = ((), (), s32[]{:S(2)}) async-start(), calls=%async_computation.3 | async-start | bytes 7798784 | tf_op jit(solution)/shard_map/all_gather | solution.py:145
  39.4 9.0 %collective-permute-start.6 = (bf16[4,4,7168]{2,1,0:T(4,128)(2,1)S(1)}, bf16[4,4,7168]{2,1,0:T(4,128)(2,1)S(1)}, u32[]{:S(2)}, u32[]{:S(2)}) collective-permute-start(bf16[4,4,7168]{2,1,0:T(4,128)(2,1)S(1)} %dynamic-slice_bitcast_fusion), channel_id=1, source_target_pairs={{0,1},{1,0},{2,3},{3,2},{4,5},{5,4},{6,7},{7,6},{8,9},{9,8},{10,11... | collective-permute-start | bytes 688136 | tf_op jit(solution)/shard_map/ppermute | solution.py:141
  49.8 34.6 %collective-permute-start.3 = (bf16[448,1536]{1,0:T(8,128)(2,1)S(1)}, bf16[448,1536]{1,0:T(8,128)(2,1)}, u32[]{:S(2)}, u32[]{:S(2)}) collective-permute-start(bf16[448,1536]{1,0:T(8,128)(2,1)S(1)} %bitcast.60), channel_id=1, source_target_pairs={{0,480},{32,64},{64,32},{96,128},{128,96},{160,192},{192,160},{224... | collective-permute-start | bytes 4128776 | tf_op jit(solution)/shard_map/ppermute | solution.py:170
  53.6 39.8 %collective-permute-start.1 = (bf16[192,7168]{1,0:T(8,128)(2,1)}, bf16[192,7168]{1,0:T(8,128)(2,1)}, u32[]{:S(2)}, u32[]{:S(2)}) collective-permute-start(bf16[192,7168]{1,0:T(8,128)(2,1)} %bitcast.78), channel_id=1, source_target_pairs={{0,1},{1,0},{2,3},{3,2},{4,5},{5,4},{6,7},{7,6},{8,9},{9,8},{10,11... | collective-permute-start | bytes 8257544 | tf_op jit(solution)/shard_map/ppermute | solution.py:165
  56.2 63.5 %collective-permute-start = (bf16[192,7168]{1,0:T(8,128)(2,1)}, bf16[192,7168]{1,0:T(8,128)(2,1)}, u32[]{:S(2)}, u32[]{:S(2)}) collective-permute-start(bf16[192,7168]{1,0:T(8,128)(2,1)} %bitcast.79), channel_id=1, source_target_pairs={{0,32},{32,0},{1,33},{33,1},{2,34},{34,2},{3,35},{35,3},{4,36},{36... | collective-permute-start | bytes 8257544 | tf_op jit(solution)/shard_map/ppermute | solution.py:137
  58.1 35.2 %collective-permute-start.2 = (bf16[448,1536]{1,0:T(8,128)(2,1)S(1)}, bf16[448,1536]{1,0:T(8,128)(2,1)}, u32[]{:S(2)}, u32[]{:S(2)}) collective-permute-start(bf16[448,1536]{1,0:T(8,128)(2,1)S(1)} %bitcast.61), channel_id=1, source_target_pairs={{0,1},{1,0},{2,3},{3,2},{4,5},{5,4},{6,7},{7,6},{8,9},{9,8},{10,11... | collective-permute-start | bytes 4128776 | tf_op jit(solution)/shard_map/ppermute | solution.py:167
  84.4 8.9 %collective-permute-start.4 = (bf16[448,1536]{1,0:T(8,128)(2,1)}, bf16[448,1536]{1,0:T(8,128)(2,1)}, u32[]{:S(2)}, u32[]{:S(2)}) collective-permute-start(bf16[448,1536]{1,0:T(8,128)(2,1)} %collective-permute-done.3.pair_a), channel_id=1, source_target_pairs={{0,1},{1,0},{2,3},{3,2},{4,5},{5,4},{6,7},{7,6},{8,9},{9,8},{10,11... | collective-permute-start | bytes 4128776 | tf_op jit(solution)/shard_map/ppermute | solution.py:171
  119.7 7.7 %collective-permute-start.5 = (bf16[192,7168]{1,0:T(8,128)(2,1)}, bf16[192,7168]{1,0:T(8,128)(2,1)}, u32[]{:S(2)}, u32[]{:S(2)}) collective-permute-start(bf16[192,7168]{1,0:T(8,128)(2,1)} %collective-permute-done.pair_a), channel_id=1, source_target_pairs={{0,1},{1,0},{2,3},{3,2},{4,5},{5,4},{6,7},{7,6},{8,9},{9,8},{10,11... | collective-permute-start | bytes 8257544 | tf_op jit(solution)/shard_map/ppermute | solution.py:175
  140.9 52.0 %all-to-all-start = ((bf16[8,32,384]{2,1,0:T(8,128)(2,1)}), bf16[8,32,384]{2,1,0:T(8,128)(2,1)S(1)}, u32[]{:S(2)}, u32[]{:S(2)}) async-start(bf16[8,32,384]{2,1,0:T(8,128)(2,1)} %broadcast_in_dim.79), calls=%async_computation | async-start | bytes 393216 | tf_op jit(solution)/shard_map/all_to_all | solution.py:182
  199.5 16.5 %all-to-all-start.1 = ((bf16[16,32,896]{2,1,0:T(8,128)(2,1)}), bf16[16,32,896]{2,1,0:T(8,128)(2,1)S(1)}, u32[]{:S(2)}, u32[]{:S(2)}) async-start(bf16[16,32,896]{2,1,0:T(8,128)(2,1)} %bitcast.24), calls=%async_computation.1 | async-start | bytes 1835008 | tf_op jit(solution)/shard_map/all_to_all | solution.py:186
  216.9 26.2 %all-to-all-start.2 = ((bf16[16,4,896]{2,1,0:T(4,128)(2,1)}), bf16[16,4,896]{2,1,0:T(4,128)(2,1)S(1)}, u32[]{:S(2)}, u32[]{:S(2)}) async-start(bf16[16,4,896]{2,1,0:T(4,128)(2,1)} %bitcast_select_fusion.2), calls=%async_computation.2 | async-start | bytes 229376 | tf_op jit(solution)/shard_map/all_to_all | solution.py:194
Sparse Core Ops, SparseCore 0:
  49.9 77.9 all-gather.4

commit v11 on v10

--- a/solution.py
+++ b/solution.py
@@ -80,30 +80,31 @@
     )(p.reshape(1), own_a, pair_a, own_b, pair_b, tokens, hits)
 
 
-def output_kernel(main, rest, own_a, pair_a, own_b, pair_b, combine, out):
-    members = main.shape[0]
-    pieces = []
-    for i in range(members):
-        pieces += [main[i], rest[i]]
-    hidden = jnp.concatenate(pieces, axis=0)
-    slots = hidden.shape[1]
+def output_kernel(hidden, own_a, pair_a, own_b, pair_b, combine, out):
+    cut = hidden.shape[1] // 2
+    low, high = cut // 128 * 128, -(-cut // 128) * 128
     outputs = []
     for d_a, d_b in [(own_a, own_b), (pair_a, pair_b)]:
-        of_a = jnp.dot(d_a[...], hidden, preferred_element_type=jnp.float32)
-        of_b = jnp.dot(d_b[...], hidden, preferred_element_type=jnp.float32)
-        is_a = lax.broadcasted_iota(jnp.int32, of_a.shape, 1) < slots // 2
-        outputs.append(jnp.where(is_a, of_a, of_b).astype(jnp.bfloat16))
+        of_a = jnp.dot(d_a[...], hidden[:, :high], preferred_element_type=jnp.float32)
+        of_b = jnp.dot(d_b[...], hidden[:, low:], preferred_element_type=jnp.float32)
+        pieces = [of_a[:, :low]]
+        if high > low:
+            middle = of_a[:, low:]
+            is_a = lax.broadcasted_iota(jnp.int32, middle.shape, 1) < cut - low
+            pieces.append(jnp.where(is_a, middle, of_b[:, : high - low]))
+        pieces.append(of_b[:, high - low :])
+        outputs.append(jnp.concatenate(pieces, axis=1).astype(jnp.bfloat16))
     outputs = jnp.concatenate(outputs, axis=0)
     out[...] = lax.dot_general(
         combine[...], outputs, (((1,), (1,)), ((), ())), preferred_element_type=jnp.float32
     ).astype(jnp.bfloat16)
 
 
-def token_sums(main, rest, own_a, pair_a, own_b, pair_b, combine):
+def token_sums(hidden, own_a, pair_a, own_b, pair_b, combine):
     features, count = own_a.shape[0], combine.shape[0]
     return pl.pallas_call(
         output_kernel,
-        in_specs=[pl.BlockSpec(memory_space=pltpu.VMEM)] * 7,
+        in_specs=[pl.BlockSpec(memory_space=pltpu.VMEM)] * 6,
         out_specs=pl.BlockSpec(memory_space=pltpu.VMEM),
         out_shape=jax.ShapeDtypeStruct((count, 2 * features), jnp.bfloat16),
         compiler_params=pltpu.CompilerParams(vmem_limit_bytes=40 * 2**20),
@@ -112,7 +113,7 @@
             bytes_accessed=8 * features * own_a.shape[1],
             transcendentals=0,
         ),
-    )(main, rest, own_a, pair_a, own_b, pair_b, combine)
+    )(hidden, own_a, pair_a, own_b, pair_b, combine)
 
 
 def local(tokens, gate_up, down, expert_ids, gate_weights, capacity):
@@ -136,11 +137,9 @@
     w_own = gate_up[0].reshape(2 * units, width)
     w_pair = lax.ppermute(w_own, "p", PAIR)
 
-    line = lax.all_gather(tokens, RING, axis=0, tiled=False).reshape(far, 2, own, width)
-    mine = lax.dynamic_index_in_dim(line, core, 1, keepdims=False)
-    got = lax.ppermute(lax.dynamic_index_in_dim(line, 1 - core, 1, keepdims=False), "c", PAIR)
-    first = core == 0
-    chip_rows = jnp.stack([jnp.where(first, mine, got), jnp.where(first, got, mine)])
+    chip_rows = lax.all_gather(tokens, RING + ("c",), axis=0, tiled=False)
+    chip_rows = chip_rows.reshape(far, 2, 2, own, width)
+    chip_rows = lax.dynamic_index_in_dim(chip_rows, core, 1, keepdims=False)
     chip_rows = chip_rows.reshape(2 * far * own, width)
     every = lax.all_gather(chip_rows, PLANE, axis=0, tiled=True)
 
@@ -148,7 +147,7 @@
     gates = of_class(gate_weights.reshape(far * 4, group_rows, -1), core)
 
     def by_row(values):
-        values = values.reshape(far, chips, 2, own).transpose(1, 2, 0, 3)
+        values = values.reshape(far, chips, 2, own).transpose(1, 0, 2, 3)
         return values.reshape(class_rows)
 
     slot_index = jnp.arange(2 * class_slots, dtype=jnp.int32)
@@ -176,19 +175,15 @@
 
     picked = slotted_hidden(p, w_own, w_pair, w_other, w_pair_other, every, hits)
 
-    most = 2 * units * 5 // 6
-    members = far * 2
-    rest = jnp.broadcast_to(picked[most:], (members, 2 * units - most, 2 * class_slots))
-    rest = lax.all_to_all(rest, RING, split_axis=0, concat_axis=0, tiled=True)
-    main = lax.all_gather(picked[:most], RING, axis=0, tiled=False)
-    summed = token_sums(main, rest, d_own, d_pair, d_other, d_pair_other, combine)
+    all_hidden = lax.all_gather(picked, RING, axis=0, tiled=True)
+    summed = token_sums(all_hidden, d_own, d_pair, d_other, d_pair_other, combine)
 
     arrived = lax.all_to_all(summed, PLANE, split_axis=0, concat_axis=0, tiled=True)
     arrived = arrived.reshape(chips, 2 * far * own, arrived.shape[1]).astype(jnp.float32)
     rows = jnp.sum(arrived, axis=0).astype(jnp.bfloat16)
     features = rows.shape[1]
 
-    rows = rows.reshape(2, far, own, features).transpose(1, 0, 2, 3)[:, None]
+    rows = rows.reshape(far, 2, own, features)[:, None]
     here = (jnp.arange(2) == core)[None, :, None, None, None]
     send = jnp.where(here, rows, jnp.zeros((), rows.dtype)).reshape(far * 4 * own, features)
     recv = lax.all_to_all(send, ("zh", "k", "c"), split_axis=0, concat_axis=0, tiled=True)

time: 252 us -> 241 us (0.956)
  waiting for transfers between devices: 82.4 us -> 133 us
  blocking collectives: 71.9 us -> 32.7 us
  starting transfers between devices: 51.8 us -> 33.4 us
    all_gather x0 -> x1, waiting for transfers between devices: none -> 52.9 us  [local(): all_hidden = lax.all_gather(picked, RING, axis=0, tiled=True)]
    all_gather x2 -> x1, blocking collectives: 71.9 us -> 32.7 us  [local(): chip_rows = lax.all_gather(tokens, RING + ('c',), axis=0, tiled=False)]
    all_to_all x1 -> x0, starting transfers between devices: 11.9 us -> none  [local(): rest = lax.all_to_all(rest, RING, split_axis=0, concat_axis=0, tiled=True)]
    ppermute x1 -> x0, starting transfers between devices: 7.87 us -> none  [local(): lax.ppermute(lax.dynamic_index_in_dim(line, 1 - core, 1, keepdims=False),...]
    all_to_all x1, starting transfers between devices: 10.8 us -> 14.6 us  [local(): lax.all_to_all(send, ('zh', 'k', 'c'), split_axis=0, concat_axis=0, tiled...]
  transfers between devices with their start and end apart: 11 -> 10, of which waited for: 7 -> 7; matrix products, arithmetic and copies ran while one was open for 3% -> 3% of each run, Pallas kernels for 0% -> 0%
where the time goes in v11:
time: 241 us
  waiting for transfers between devices  133 us (55%)
  starting transfers between devices  33.4 us (14%)
  blocking collectives  32.7 us (14%)
  Pallas kernels  16.3 us (7%)
  between operations  13.7 us (6%)
  local copies, waits for them, and re-layouts  6.28 us (3%)
  other arithmetic  5.46 us (2%)
    all_gather x1, waiting for transfers between devices, local(): all_hidden = lax.all_gather(picked, RING, axis=0, tiled=True)  52.9 us
    all_gather x1, blocking collectives, local(): chip_rows = lax.all_gather(tokens, RING + ('c',), axis=0, tiled=False)  32.7 us
    ppermute x1, waiting for transfers between devices, local(): d_pair = lax.ppermute(d_own, LINE, swap)  25 us
    ppermute x1, waiting for transfers between devices, local(): w_pair = lax.ppermute(w_own, 'p', PAIR)  24.2 us
    all_to_all x1, starting transfers between devices, local(): lax.all_to_all(send, ('zh', 'k', 'c'), split_axis=0, concat_axis=0, tiled...  14.6 us
    all_to_all x1, waiting for transfers between devices, local(): lax.all_to_all(send, ('zh', 'k', 'c'), split_axis=0, concat_axis=0, tiled...  14.3 us
    pallas_call x1, Pallas kernels, slotted_hidden(): pl.pallas_call(hidden_kernel, grid_spec=pltpu.PrefetchScalarGridSpec(num_...  11.5 us
    all_to_all x1, waiting for transfers between devices, local(): lax.all_to_all(summed, PLANE, split_axis=0, concat_axis=0, tiled=True)  11 us
  transfers between devices with their start and end apart: 10, of which 7 were waited for; matrix products, arithmetic and copies ran while one was open for 3% of the time, Pallas kernels for 0%

profile of v11, /device:TPU:1, one launch (start us, length us, event | category | flops | bytes accessed | tf_op | source)
XLA Modules:
  0.0 240.7 jit_solution(4718193133569202811)
XLA Ops:
  6.5 32.7 %all-gather.1 = bf16[16,4,7168]{2,1,0:T(4,128)(2,1)S(1)} all-gather(bf16[1,4,7168]{2,1,0:T(4,128)(2,1)} %bitcast.59), channel_id=2, replica_groups=mesh['zh'=4,'k'=2,'p'=2,'x'=4,'y'=4,'c'=2] {'zh','k','c'}, dimensions={0}, use_global_device_ids=true | all-gather | bytes 974848 | tf_op jit(solution)/shard_map/all_gather | solution.py:140
  39.4 0.9 reshape.177
  40.3 1.9 collective-permute-start.3
  42.3 2.3 collective-permute-start.1
  44.5 1.9 collective-permute-start
  46.5 2.1 collective-permute-start.2
  48.6 0.8 select_reduce_fusion.1
  50.1 25.0 %collective-permute-done.3.pair_a = bf16[448,1536]{1,0:T(8,128)(2,1)S(1)} collective-permute-done((bf16[448,1536]{1,0:T(8,128)(2,1)S(1)}, bf16[448,1536]{1,0:T(8,128)(2,1)S(1)}, u32[]{:S(2)}, u32[]{:S(2)}) %collective-permute-start.3) | collective-permute-done | bytes 1376288 | tf_op jit(solution)/shard_map/ppermute | solution.py:169
  75.1 2.9 %collective-permute-start.4 = (bf16[448,1536]{1,0:T(8,128)(2,1)S(1)}, bf16[448,1536]{1,0:T(8,128)(2,1)}, u32[]{:S(2)}, u32[]{:S(2)}) collective-permute-start(bf16[448,1536]{1,0:T(8,128)(2,1)S(1)} %collective-permute-done.3.pair_a), channel_id=1, source_target_pairs={{0,1},{1,0},{2,3},{3,2},{4,5},{5,4},{6,7},{7,6},{8,9},{9,8},{10,11... | collective-permute-start | bytes 4128776 | tf_op jit(solution)/shard_map/ppermute | solution.py:170
  79.0 1.3 fusion
  82.2 1.0 add_convert_fusion.hits
  83.6 24.2 %collective-permute-done.pair_a = bf16[192,7168]{1,0:T(8,128)(2,1)} collective-permute-done((bf16[192,7168]{1,0:T(8,128)(2,1)}, bf16[192,7168]{1,0:T(8,128)(2,1)}, u32[]{:S(2)}, u32[]{:S(2)}) %collective-permute-start) | collective-permute-done | bytes 2752544 | tf_op jit(solution)/shard_map/ppermute | solution.py:138
  107.9 2.9 %collective-permute-start.5 = (bf16[192,7168]{1,0:T(8,128)(2,1)}, bf16[192,7168]{1,0:T(8,128)(2,1)}, u32[]{:S(2)}, u32[]{:S(2)}) collective-permute-start(bf16[192,7168]{1,0:T(8,128)(2,1)} %collective-permute-done.pair_a), channel_id=1, source_target_pairs={{0,1},{1,0},{2,3},{3,2},{4,5},{5,4},{6,7},{7,6},{8,9},{9,8},{10,11... | collective-permute-start | bytes 8257544 | tf_op jit(solution)/shard_map/ppermute | solution.py:174
  110.7 5.0 %collective-permute-done.5.pair_b = bf16[192,7168]{1,0:T(8,128)(2,1)} collective-permute-done((bf16[192,7168]{1,0:T(8,128)(2,1)}, bf16[192,7168]{1,0:T(8,128)(2,1)}, u32[]{:S(2)}, u32[]{:S(2)}) %collective-permute-start.5) | collective-permute-done | bytes 2752544 | tf_op jit(solution)/shard_map/ppermute | solution.py:174
  116.3 11.5 %shard_map.64 = bf16[192,384]{1,0:T(8,128)(2,1)} custom-call(s32[1]{0:T(128)} %bitcast.p_ref, bf16[192,7168]{1,0:T(8,128)(2,1)} %bitcast.64, bf16[192,7168]{1,0:T(8,128)(2,1)} %collective-permute-done.pair_a, bf16[192,7168]{1,0:T(8,128)(2,1)} %collective-permute-done.1.own_b, bf16[192,7168]{1,0:T(8,128)(2,1)} %collective-permute-done.5.pair_b, ...), custom_call_target="tpu_custom_call" | custom-call | flops 5637144576 | bytes 18350080 | tf_op jit(solution)/shard_map/pallas_call | solution.py:60
  127.9 52.9 %all-gather.7.cloned.1.call-done.hidden = bf16[1536,384]{1,0:T(8,128)(2,1)} async-done(((bf16[192,384]{1,0:T(8,128)(2,1)}), bf16[1536,384]{1,0:T(8,128)(2,1)}) %all-gather.7.cloned.1.call-update) | async-done | bytes 1179664 | tf_op jit(solution)/shard_map/all_gather | solution.py:178
  180.7 1.3 copy-done.1
  182.0 4.8 %shard_map.65 = bf16[512,896]{1,0:T(8,128)(2,1)} custom-call(bf16[1536,384]{1,0:T(8,128)(2,1)S(1)} %copy-done.1, bf16[448,1536]{1,0:T(8,128)(2,1)S(1)} %bitcast.47, bf16[448,1536]{1,0:T(8,128)(2,1)S(1)} %collective-permute-done.3.pair_a, bf16[448,1536]{1,0:T(8,128)(2,1)} %collective-permute-done.2.own_b, bf16[448,1536]{1,0:T(8,128)(2,1)} %collective-permute-done.4.pair_b, ...), custom_call_target="tpu_custom_call" | custom-call | flops 2113929216 | bytes 5505024 | tf_op jit(solution)/shard_map/pallas_call | solution.py:105
  186.8 4.9 %all-to-all-start = ((bf16[16,32,896]{2,1,0:T(8,128)(2,1)}), bf16[16,32,896]{2,1,0:T(8,128)(2,1)S(1)}, u32[]{:S(2)}, u32[]{:S(2)}) async-start(bf16[16,32,896]{2,1,0:T(8,128)(2,1)} %bitcast.19), calls=%async_computation | async-start | bytes 1835008 | tf_op jit(solution)/shard_map/all_to_all | solution.py:181
  191.9 11.0 %all-to-all-done = bf16[16,32,896]{2,1,0:T(8,128)(2,1)S(1)} async-done(((bf16[16,32,896]{2,1,0:T(8,128)(2,1)}), bf16[16,32,896]{2,1,0:T(8,128)(2,1)S(1)}, u32[]{:S(2)}, u32[]{:S(2)}) %all-to-all-start) | async-done | bytes 917536 | tf_op jit(solution)/shard_map/all_to_all | solution.py:181
  203.0 0.8 bitcast_select_fusion
  203.8 14.6 %all-to-all-start.1 = ((bf16[16,4,896]{2,1,0:T(4,128)(2,1)}), bf16[16,4,896]{2,1,0:T(4,128)(2,1)S(1)}, u32[]{:S(2)}, u32[]{:S(2)}) async-start(bf16[16,4,896]{2,1,0:T(4,128)(2,1)} %bitcast_select_fusion), calls=%async_computation.1 | async-start | bytes 229376 | tf_op jit(solution)/shard_map/all_to_all | solution.py:189
  218.4 14.3 %all-to-all-done.1 = bf16[16,4,896]{2,1,0:T(4,128)(2,1)S(1)} async-done(((bf16[16,4,896]{2,1,0:T(4,128)(2,1)}), bf16[16,4,896]{2,1,0:T(4,128)(2,1)S(1)}, u32[]{:S(2)}, u32[]{:S(2)}) %all-to-all-start.1) | async-done | bytes 114720 | tf_op jit(solution)/shard_map/all_to_all | solution.py:189
  233.2 0.8 reshape.180
  (54 shorter events, 5.6 us)
Async XLA Ops:
  6.5 33.8 %copy-start = (bf16[1,1536,448]{1,2,0:T(8,128)(2,1)S(1)}, bf16[1,1536,448]{1,2,0:T(8,128)(2,1)}, u32[]{:S(2)}) copy-start(bf16[1,1536,448]{1,2,0:T(8,128)(2,1)} %param.8) | copy-start | bytes 4128772
  6.5 71.8 %copy-start.2 = (s32[32]{0:T(128)S(1)}, s32[32]{0:T(128)}, u32[]{:S(2)}) copy-start(s32[32]{0:T(128)} %param.11) | copy-start | bytes 388
  6.5 109.8 %all-gather.5.cloned.1.call-start = ((), (), s32[]{:S(2)}) async-start(), calls=%async_computation.2 | async-start | bytes 7798784 | tf_op jit(solution)/shard_map/all_gather | solution.py:144
  40.3 140.5 %all-gather.7.cloned.1.call-start = ((), (), s32[]{:S(2)}) async-start(), calls=%async_computation.3 | async-start | bytes 1327104 | tf_op jit(solution)/shard_map/all_gather | solution.py:178
  40.3 34.7 %collective-permute-start.3 = (bf16[448,1536]{1,0:T(8,128)(2,1)S(1)}, bf16[448,1536]{1,0:T(8,128)(2,1)S(1)}, u32[]{:S(2)}, u32[]{:S(2)}) collective-permute-start(bf16[448,1536]{1,0:T(8,128)(2,1)S(1)} %bitcast.45), channel_id=1, source_target_pairs={{0,480},{32,64},{64,32},{96,128},{128,96},{160,192},{192,160},{224... | collective-permute-start | bytes 4128776 | tf_op jit(solution)/shard_map/ppermute | solution.py:169
  42.3 41.4 %collective-permute-start.1 = (bf16[192,7168]{1,0:T(8,128)(2,1)}, bf16[192,7168]{1,0:T(8,128)(2,1)}, u32[]{:S(2)}, u32[]{:S(2)}) collective-permute-start(bf16[192,7168]{1,0:T(8,128)(2,1)} %bitcast.62), channel_id=1, source_target_pairs={{0,1},{1,0},{2,3},{3,2},{4,5},{5,4},{6,7},{7,6},{8,9},{9,8},{10,11... | collective-permute-start | bytes 8257544 | tf_op jit(solution)/shard_map/ppermute | solution.py:164
  44.5 63.3 %collective-permute-start = (bf16[192,7168]{1,0:T(8,128)(2,1)}, bf16[192,7168]{1,0:T(8,128)(2,1)}, u32[]{:S(2)}, u32[]{:S(2)}) collective-permute-start(bf16[192,7168]{1,0:T(8,128)(2,1)} %bitcast.63), channel_id=1, source_target_pairs={{0,32},{32,0},{1,33},{33,1},{2,34},{34,2},{3,35},{35,3},{4,36},{36... | collective-permute-start | bytes 8257544 | tf_op jit(solution)/shard_map/ppermute | solution.py:138
  46.5 37.1 %collective-permute-start.2 = (bf16[448,1536]{1,0:T(8,128)(2,1)S(1)}, bf16[448,1536]{1,0:T(8,128)(2,1)}, u32[]{:S(2)}, u32[]{:S(2)}) collective-permute-start(bf16[448,1536]{1,0:T(8,128)(2,1)S(1)} %bitcast.46), channel_id=1, source_target_pairs={{0,1},{1,0},{2,3},{3,2},{4,5},{5,4},{6,7},{7,6},{8,9},{9,8},{10,11... | collective-permute-start | bytes 4128776 | tf_op jit(solution)/shard_map/ppermute | solution.py:166
  75.1 8.5 %collective-permute-start.4 = (bf16[448,1536]{1,0:T(8,128)(2,1)S(1)}, bf16[448,1536]{1,0:T(8,128)(2,1)}, u32[]{:S(2)}, u32[]{:S(2)}) collective-permute-start(bf16[448,1536]{1,0:T(8,128)(2,1)S(1)} %collective-permute-done.3.pair_a), channel_id=1, source_target_pairs={{0,1},{1,0},{2,3},{3,2},{4,5},{5,4},{6,7},{7,6},{8,9},{9,8},{10,11... | collective-permute-start | bytes 4128776 | tf_op jit(solution)/shard_map/ppermute | solution.py:170
  107.9 7.9 %collective-permute-start.5 = (bf16[192,7168]{1,0:T(8,128)(2,1)}, bf16[192,7168]{1,0:T(8,128)(2,1)}, u32[]{:S(2)}, u32[]{:S(2)}) collective-permute-start(bf16[192,7168]{1,0:T(8,128)(2,1)} %collective-permute-done.pair_a), channel_id=1, source_target_pairs={{0,1},{1,0},{2,3},{3,2},{4,5},{5,4},{6,7},{7,6},{8,9},{9,8},{10,11... | collective-permute-start | bytes 8257544 | tf_op jit(solution)/shard_map/ppermute | solution.py:174
  180.7 1.3 copy-start.1
  186.8 16.1 %all-to-all-start = ((bf16[16,32,896]{2,1,0:T(8,128)(2,1)}), bf16[16,32,896]{2,1,0:T(8,128)(2,1)S(1)}, u32[]{:S(2)}, u32[]{:S(2)}) async-start(bf16[16,32,896]{2,1,0:T(8,128)(2,1)} %bitcast.19), calls=%async_computation | async-start | bytes 1835008 | tf_op jit(solution)/shard_map/all_to_all | solution.py:181
  203.8 28.9 %all-to-all-start.1 = ((bf16[16,4,896]{2,1,0:T(4,128)(2,1)}), bf16[16,4,896]{2,1,0:T(4,128)(2,1)S(1)}, u32[]{:S(2)}, u32[]{:S(2)}) async-start(bf16[16,4,896]{2,1,0:T(4,128)(2,1)} %bitcast_select_fusion), calls=%async_computation.1 | async-start | bytes 229376 | tf_op jit(solution)/shard_map/all_to_all | solution.py:189
Sparse Core Ops, SparseCore 0:
  40.4 75.8 all-gather.4
  128.0 52.7 all-gather.6

commit v12 on v11

--- a/solution.py
+++ b/solution.py
@@ -22,65 +22,97 @@
     return jnp.where((hits > 0) & (rank < cap), rank + offset, -1), weights
 
 
-def hidden_kernel(p_ref, own_a, pair_a, own_b, pair_b, tokens, hits, out, total):
-    step = pl.program_id(0)
-
-    @pl.when(step == 0)
+def start_total(total):
+    @pl.when(pl.program_id(0) == 0)
     def _():
         total[...] = jnp.zeros_like(total)
 
-    w = jnp.concatenate([own_a[...], pair_a[...], own_b[...], pair_b[...]], axis=0)
+
+def add_product(total, rows, tokens):
     total[...] += lax.dot_general(
-        w, tokens[...], (((1,), (1,)), ((), ())), preferred_element_type=jnp.float32
-    )
-
-    @pl.when(step == pl.num_programs(0) - 1)
+        jnp.concatenate(rows, axis=0),
+        tokens[...],
+        (((1,), (1,)), ((), ())),
+        preferred_element_type=jnp.float32,
+    )
+
+
+def unit_values(gate, up):
+    return (gate / (1.0 + jnp.exp(-gate)) * up).astype(jnp.bfloat16)
+
+
+def pick(hidden, hits):
+    return jnp.dot(
+        jnp.concatenate(hidden, axis=1), hits[...], preferred_element_type=jnp.float32
+    ).astype(jnp.bfloat16)
+
+
+def rest_kernel(gate_a, up_a, gate_b, up_b, tokens, hits, out, total):
+    start_total(total)
+    add_product(total, [gate_a[...], up_a[...], gate_b[...], up_b[...]], tokens)
+
+    @pl.when(pl.program_id(0) == pl.num_programs(0) - 1)
     def _():
-        rows = own_a.shape[0]
-        units = rows // 2
-        for z in range(2):
-            hidden = []
-            for expert in range(2):
-                base = (2 * expert + z) * rows
-                gate = total[base : base + units]
-                up = total[base + units : base + rows]
-                hidden.append((gate / (1.0 + jnp.exp(-gate)) * up).astype(jnp.bfloat16))
-            picked = jnp.dot(
-                jnp.concatenate(hidden, axis=1), hits[...], preferred_element_type=jnp.float32
-            )
-            place = p_ref[0] if z == 0 else 1 - p_ref[0]
-            out[pl.ds(pl.multiple_of(place * units, 16), units), :] = picked.astype(jnp.bfloat16)
-
-
-def slotted_hidden(p, own_a, pair_a, own_b, pair_b, tokens, hits):
-    rows, width = own_a.shape
-    count, slots = tokens.shape[0], hits.shape[1]
+        n = gate_a.shape[0]
+        hidden = [unit_values(total[i * n : (i + 1) * n], total[(i + 1) * n : (i + 2) * n]) for i in (0, 2)]
+        picked = pick(hidden, hits)
+        for i in range(out.shape[0]):
+            out[i] = picked
+
+
+def main_kernel(own_a, pair_a, own_b, pair_b, tokens, hits, out, total):
+    start_total(total)
+    units = pair_a.shape[0] // 2
+    kept = out.shape[0] - units
+    rows = []
+    for own, pair in ((own_a, pair_a), (own_b, pair_b)):
+        rows += [own[:kept], own[units : units + kept], pair[...]]
+    add_product(total, rows, tokens)
+
+    @pl.when(pl.program_id(0) == pl.num_programs(0) - 1)
+    def _():
+        hidden = []
+        for expert in range(2):
+            base = expert * 2 * (kept + units)
+            middle = base + 2 * kept
+            near = unit_values(total[base : base + kept], total[base + kept : middle])
+            far = unit_values(total[middle : middle + units], total[middle + units : middle + 2 * units])
+            hidden.append(jnp.concatenate([near, far], axis=0))
+        out[...] = pick(hidden, hits)
+
+
+def slotted_hidden(kernel, weights, tokens, hits, total_rows, out_shape):
+    count, width = tokens.shape
     depth = width // 4
-    weights = pl.BlockSpec((rows, depth), lambda i, p: (0, i))
+    whole = lambda shape: pl.BlockSpec(shape, lambda i: (0,) * len(shape))
     return pl.pallas_call(
-        hidden_kernel,
-        grid_spec=pltpu.PrefetchScalarGridSpec(
-            num_scalar_prefetch=1,
-            grid=(width // depth,),
-            in_specs=[weights] * 4
-            + [
-                pl.BlockSpec((count, depth), lambda i, p: (0, i)),
-                pl.BlockSpec(hits.shape, lambda i, p: (0, 0)),
-            ],
-            out_specs=pl.BlockSpec((rows, slots), lambda i, p: (0, 0)),
-            scratch_shapes=[pltpu.VMEM((4 * rows, count), jnp.float32)],
-        ),
-        out_shape=jax.ShapeDtypeStruct((rows, slots), jnp.bfloat16),
+        kernel,
+        grid=(width // depth,),
+        in_specs=[pl.BlockSpec((size, depth), lambda i, at=at: (at, i)) for _, size, at in weights]
+        + [pl.BlockSpec((count, depth), lambda i: (0, i)), whole(hits.shape)],
+        out_specs=whole(out_shape),
+        scratch_shapes=[pltpu.VMEM((total_rows, count), jnp.float32)],
+        out_shape=jax.ShapeDtypeStruct(out_shape, jnp.bfloat16),
         compiler_params=pltpu.CompilerParams(vmem_limit_bytes=60 * 2**20),
         cost_estimate=pl.CostEstimate(
-            flops=2 * 4 * rows * width * count,
-            bytes_accessed=2 * width * (4 * rows + count),
-            transcendentals=2 * rows * count,
+            flops=2 * total_rows * width * count,
+            bytes_accessed=2 * width * (total_rows + count),
+            transcendentals=total_rows * count // 2,
         ),
-    )(p.reshape(1), own_a, pair_a, own_b, pair_b, tokens, hits)
-
-
-def output_kernel(hidden, own_a, pair_a, own_b, pair_b, combine, out):
+    )(*[w for w, _, _ in weights], tokens, hits)
+
+
+def output_kernel(p_ref, main, rest, own_a, pair_a, own_b, pair_b, combine, out, hidden):
+    members, ends = rest.shape[0], rest.shape[1]
+    both = main.shape[1] + ends
+    units = both // 2
+    kept = units - ends
+    for i in range(members):
+        own = pl.multiple_of(i * both + p_ref[0] * units, ends)
+        other = pl.multiple_of(i * both + (1 - p_ref[0]) * units, ends)
+        hidden[pl.ds(own, kept), :] = main[i, :kept]
+        hidden[pl.ds(own + kept, ends), :] = rest[i]
+        hidden[pl.ds(other, units), :] = main[i, kept:]
     cut = hidden.shape[1] // 2
     low, high = cut // 128 * 128, -(-cut // 128) * 128
     outputs = []
@@ -100,20 +132,23 @@
     ).astype(jnp.bfloat16)
 
 
-def token_sums(hidden, own_a, pair_a, own_b, pair_b, combine):
-    features, count = own_a.shape[0], combine.shape[0]
+def token_sums(p, main, rest, own_a, pair_a, own_b, pair_b, combine):
+    features, units = own_a.shape
+    count, slots = combine.shape
     return pl.pallas_call(
         output_kernel,
-        in_specs=[pl.BlockSpec(memory_space=pltpu.VMEM)] * 6,
+        in_specs=[pl.BlockSpec(memory_space=pltpu.SMEM)]
+        + [pl.BlockSpec(memory_space=pltpu.VMEM)] * 7,
         out_specs=pl.BlockSpec(memory_space=pltpu.VMEM),
+        scratch_shapes=[pltpu.VMEM((units, slots), jnp.bfloat16)],
         out_shape=jax.ShapeDtypeStruct((count, 2 * features), jnp.bfloat16),
         compiler_params=pltpu.CompilerParams(vmem_limit_bytes=40 * 2**20),
         cost_estimate=pl.CostEstimate(
-            flops=8 * features * own_a.shape[1] * combine.shape[1],
-            bytes_accessed=8 * features * own_a.shape[1],
+            flops=8 * features * units * slots,
+            bytes_accessed=8 * features * units,
             transcendentals=0,
         ),
-    )(hidden, own_a, pair_a, own_b, pair_b, combine)
+    )(p.reshape(1), main, rest, own_a, pair_a, own_b, pair_b, combine)
 
 
 def local(tokens, gate_up, down, expert_ids, gate_weights, capacity):
@@ -173,10 +208,30 @@
     )
     w_pair_other = lax.ppermute(w_pair, "c", PAIR)
 
-    picked = slotted_hidden(p, w_own, w_pair, w_other, w_pair_other, every, hits)
-
-    all_hidden = lax.all_gather(picked, RING, axis=0, tiled=True)
-    summed = token_sums(all_hidden, d_own, d_pair, d_other, d_pair_other, combine)
+    ends = units // 3
+    kept = units - ends
+    members = far * 2
+    places = (kept // ends, (units + kept) // ends)
+    rest = slotted_hidden(
+        rest_kernel,
+        [(w, ends, at) for w in (w_own, w_other) for at in places],
+        every,
+        hits,
+        4 * ends,
+        (members, ends, 2 * class_slots),
+    )
+    every, rest = lax.optimization_barrier((every, rest))
+    rest = lax.all_to_all(rest, RING, split_axis=0, concat_axis=0, tiled=True)
+    main = slotted_hidden(
+        main_kernel,
+        [(w, 2 * units, 0) for w in (w_own, w_pair, w_other, w_pair_other)],
+        every,
+        hits,
+        4 * (units + kept),
+        (units + kept, 2 * class_slots),
+    )
+    main = lax.all_gather(main, RING, axis=0, tiled=False)
+    summed = token_sums(p, main, rest, d_own, d_pair, d_other, d_pair_other, combine)
 
     arrived = lax.all_to_all(summed, PLANE, split_axis=0, concat_axis=0, tiled=True)
     arrived = arrived.reshape(chips, 2 * far * own, arrived.shape[1]).astype(jnp.float32)

time: 241 us -> 239 us (level)
  waiting for transfers between devices: 133 us -> 81 us
  blocking collectives: 32.7 us -> 66 us
  starting transfers between devices: 33.4 us -> 43.9 us
  Pallas kernels: 16.3 us -> 23.1 us
    all_gather x1 -> x0, waiting for transfers between devices: 52.9 us -> none  [local(): all_hidden = lax.all_gather(picked, RING, axis=0, tiled=True)]
    all_gather x0 -> x1, blocking collectives: none -> 33.4 us  [local(): main = lax.all_gather(main, RING, axis=0, tiled=False)]
    all_to_all x0 -> x1, starting transfers between devices: none -> 11.9 us  [local(): rest = lax.all_to_all(rest, RING, split_axis=0, concat_axis=0, tiled=True)]
    all_gather x1, waiting for transfers between devices: 0.56 us -> 8.07 us  [local(): every = lax.all_gather(chip_rows, PLANE, axis=0, tiled=True)]
    pallas_call x2 -> x3, Pallas kernels: 16.3 us -> 23 us  [the longest x2 17.7 us: slotted_hidden(): pl.pallas_call(kernel, grid=(width // depth,), in_specs=[pl.BlockSpec((si...]
    ppermute x1, waiting for transfers between devices: 5.04 us -> 0.01 us  [local(): w_pair_other = lax.ppermute(w_pair, 'c', PAIR)]
  transfers between devices with their start and end apart: 10 -> 10, of which waited for: 7 -> 5; matrix products, arithmetic and copies ran while one was open for 3% -> 3% of each run, Pallas kernels for 0% -> 7%
where the time goes in v12:
time: 239 us; the launch traced here: 238 us
  waiting for transfers between devices  81 us (34%)
  blocking collectives  66 us (28%)
  starting transfers between devices  43.9 us (18%)
  Pallas kernels  23.1 us (10%)
  between operations  13.7 us (6%)
  other arithmetic  5.44 us (2%)
  local copies, waits for them, and re-layouts  4.97 us (2%)
    all_gather x1, blocking collectives, local(): main = lax.all_gather(main, RING, axis=0, tiled=False)  33.4 us
    all_gather x1, blocking collectives, local(): chip_rows = lax.all_gather(tokens, RING + ('c',), axis=0, tiled=False)  32.7 us
    ppermute x1, waiting for transfers between devices, local(): d_pair = lax.ppermute(d_own, LINE, swap)  24.8 us
    ppermute x1, waiting for transfers between devices, local(): w_pair = lax.ppermute(w_own, 'p', PAIR)  21.9 us
    pallas_call x2, Pallas kernels, slotted_hidden(): pl.pallas_call(kernel, grid=(width // depth,), in_specs=[pl.BlockSpec((si...  17.7 us
    all_to_all x1, waiting for transfers between devices, local(): lax.all_to_all(send, ('zh', 'k', 'c'), split_axis=0, concat_axis=0, tiled...  15.3 us
    all_to_all x1, starting transfers between devices, local(): lax.all_to_all(send, ('zh', 'k', 'c'), split_axis=0, concat_axis=0, tiled...  12.9 us
    all_to_all x1, starting transfers between devices, local(): rest = lax.all_to_all(rest, RING, split_axis=0, concat_axis=0, tiled=True)  11.9 us
  transfers between devices with their start and end apart: 10, of which 5 were waited for; matrix products, arithmetic and copies ran while one was open for 3% of the time, Pallas kernels for 7%

profile of v12, /device:TPU:1, one launch (start us, length us, event | category | flops | bytes accessed | tf_op | source)
XLA Modules:
  0.0 238.0 jit_solution(13111725487507672845)
XLA Ops:
  6.5 32.7 %all-gather.2 = bf16[16,4,7168]{2,1,0:T(4,128)(2,1)S(1)} all-gather(bf16[1,4,7168]{2,1,0:T(4,128)(2,1)} %bitcast.66), channel_id=2, replica_groups=mesh['zh'=4,'k'=2,'p'=2,'x'=4,'y'=4,'c'=2] {'zh','k','c'}, dimensions={0}, use_global_device_ids=true | all-gather | bytes 974848 | tf_op jit(solution)/shard_map/all_gather | solution.py:175
  39.4 0.9 reshape.177
  40.3 1.9 collective-permute-start.3
  42.2 1.9 collective-permute-start
  44.1 2.3 collective-permute-start.1
  46.4 2.0 collective-permute-start.2
  48.5 0.8 select_reduce_fusion.1
  50.3 24.8 %collective-permute-done.3.pair_a = bf16[448,1536]{1,0:T(8,128)(2,1)} collective-permute-done((bf16[448,1536]{1,0:T(8,128)(2,1)S(1)}, bf16[448,1536]{1,0:T(8,128)(2,1)}, u32[]{:S(2)}, u32[]{:S(2)}) %collective-permute-start.3) | collective-permute-done | bytes 1376288 | tf_op jit(solution)/shard_map/ppermute | solution.py:204
  75.1 2.9 %collective-permute-start.4 = (bf16[448,1536]{1,0:T(8,128)(2,1)}, bf16[448,1536]{1,0:T(8,128)(2,1)}, u32[]{:S(2)}, u32[]{:S(2)}) collective-permute-start(bf16[448,1536]{1,0:T(8,128)(2,1)} %collective-permute-done.3.pair_a), channel_id=1, source_target_pairs={{0,1},{1,0},{2,3},{3,2},{4,5},{5,4},{6,7},{7,6},{8,9},{9,8},{10,11... | collective-permute-start | bytes 4128776 | tf_op jit(solution)/shard_map/ppermute | solution.py:205
  78.8 1.3 fusion
  82.0 1.0 add_convert_fusion.hits
  83.4 21.9 %collective-permute-done.pair_a = bf16[192,7168]{1,0:T(8,128)(2,1)} collective-permute-done((bf16[192,7168]{1,0:T(8,128)(2,1)}, bf16[192,7168]{1,0:T(8,128)(2,1)}, u32[]{:S(2)}, u32[]{:S(2)}) %collective-permute-start) | collective-permute-done | bytes 2752544 | tf_op jit(solution)/shard_map/ppermute | solution.py:173
  105.3 3.1 %collective-permute-start.5 = (bf16[192,7168]{1,0:T(8,128)(2,1)}, bf16[192,7168]{1,0:T(8,128)(2,1)}, u32[]{:S(2)}, u32[]{:S(2)}) collective-permute-start(bf16[192,7168]{1,0:T(8,128)(2,1)} %collective-permute-done.pair_a), channel_id=1, source_target_pairs={{0,1},{1,0},{2,3},{3,2},{4,5},{5,4},{6,7},{7,6},{8,9},{9,8},{10,11... | collective-permute-start | bytes 8257544 | tf_op jit(solution)/shard_map/ppermute | solution.py:209
  108.4 8.1 %all-gather.5.cloned.1.call-done.tokens = bf16[512,7168]{1,0:T(8,128)(2,1)} async-done(((bf16[32,7168]{1,0:T(8,128)(2,1)}), bf16[512,7168]{1,0:T(8,128)(2,1)}) %all-gather.5.cloned.1.call-update) | async-done | bytes 7340048 | tf_op jit(solution)/shard_map/all_gather | solution.py:179
  116.5 7.0 %shard_map.64 = bf16[8,32,384]{2,1,0:T(8,128)(2,1)} custom-call(bf16[192,7168]{1,0:T(8,128)(2,1)} %bitcast.52, bf16[192,7168]{1,0:T(8,128)(2,1)} %bitcast.53, bf16[192,7168]{1,0:T(8,128)(2,1)} %collective-permute-done.1.gate_b.up_b.own_b, bf16[192,7168]{1,0:T(8,128)(2,1)} %collective-permute-done.1.gate_b.up_b.own_b, ...), custom_call_target="tpu_custom_call" | custom-call | flops 939524096 | bytes 9175040 | tf_op jit(solution)/shard_map/pallas_call | solution.py:88
  123.4 11.9 %all-to-all-start = ((bf16[8,32,384]{2,1,0:T(8,128)(2,1)}), bf16[8,32,384]{2,1,0:T(8,128)(2,1)S(1)}, u32[]{:S(2)}, u32[]{:S(2)}) async-start(bf16[8,32,384]{2,1,0:T(8,128)(2,1)} %shard_map.64), calls=%async_computation | async-start | bytes 393216 | tf_op jit(solution)/shard_map/all_to_all | solution.py:224
  135.4 10.8 %shard_map.65 = bf16[160,384]{1,0:T(8,128)(2,1)} custom-call(bf16[192,7168]{1,0:T(8,128)(2,1)} %bitcast.54, bf16[192,7168]{1,0:T(8,128)(2,1)} %collective-permute-done.pair_a, bf16[192,7168]{1,0:T(8,128)(2,1)} %collective-permute-done.1.gate_b.up_b.own_b, bf16[192,7168]{1,0:T(8,128)(2,1)} %collective-permute-done.5.pair_b, ...), custom_call_target="tpu_custom_call" | custom-call | flops 4697620480 | bytes 16515072 | tf_op jit(solution)/shard_map/pallas_call | solution.py:88
  146.1 33.4 %all-gather.1 = bf16[1280,384]{1,0:T(8,128)(2,1)S(1)} all-gather(bf16[160,384]{1,0:T(8,128)(2,1)} %shard_map.65), channel_id=3, replica_groups=mesh['zh'=4,'k'=2,'p'=2,'x'=4,'y'=4,'c'=2] {'zh','k'}, dimensions={0}, use_global_device_ids=true | all-gather | bytes 1105920 | tf_op jit(solution)/shard_map/all_gather | solution.py:233
  179.5 5.3 %shard_map.66 = bf16[512,896]{1,0:T(8,128)(2,1)} custom-call(s32[1]{0:T(128)} %bitcast.p_ref, bf16[8,160,384]{2,1,0:T(8,128)(2,1)S(1)} %bitcast.46, bf16[8,32,384]{2,1,0:T(8,128)(2,1)S(1)} %all-to-all-done.rest, bf16[448,1536]{1,0:T(8,128)(2,1)S(1)} %bitcast.49, bf16[448,1536]{1,0:T(8,128)(2,1)} %collective-permute-done.3.pair_a, ...), custom_call_target="tpu_custom_call" | custom-call | flops 2113929216 | bytes 5505024 | tf_op jit(solution)/shard_map/pallas_call | solution.py:138
  184.8 5.0 %all-to-all-start.1 = ((bf16[16,32,896]{2,1,0:T(8,128)(2,1)}), bf16[16,32,896]{2,1,0:T(8,128)(2,1)S(1)}, u32[]{:S(2)}, u32[]{:S(2)}) async-start(bf16[16,32,896]{2,1,0:T(8,128)(2,1)} %bitcast.20), calls=%async_computation.1 | async-start | bytes 1835008 | tf_op jit(solution)/shard_map/all_to_all | solution.py:236
  190.0 10.9 %all-to-all-done.1 = bf16[16,32,896]{2,1,0:T(8,128)(2,1)S(1)} async-done(((bf16[16,32,896]{2,1,0:T(8,128)(2,1)}), bf16[16,32,896]{2,1,0:T(8,128)(2,1)S(1)}, u32[]{:S(2)}, u32[]{:S(2)}) %all-to-all-start.1) | async-done | bytes 917536 | tf_op jit(solution)/shard_map/all_to_all | solution.py:236
  201.0 0.8 bitcast_select_fusion
  201.8 12.9 %all-to-all-start.2 = ((bf16[16,4,896]{2,1,0:T(4,128)(2,1)}), bf16[16,4,896]{2,1,0:T(4,128)(2,1)S(1)}, u32[]{:S(2)}, u32[]{:S(2)}) async-start(bf16[16,4,896]{2,1,0:T(4,128)(2,1)} %bitcast_select_fusion), calls=%async_computation.2 | async-start | bytes 229376 | tf_op jit(solution)/shard_map/all_to_all | solution.py:244
  214.6 15.3 %all-to-all-done.2 = bf16[16,4,896]{2,1,0:T(4,128)(2,1)S(1)} async-done(((bf16[16,4,896]{2,1,0:T(4,128)(2,1)}), bf16[16,4,896]{2,1,0:T(4,128)(2,1)S(1)}, u32[]{:S(2)}, u32[]{:S(2)}) %all-to-all-start.2) | async-done | bytes 114720 | tf_op jit(solution)/shard_map/all_to_all | solution.py:244
  (53 shorter events, 5.7 us)
Async XLA Ops:
  6.5 33.7 %copy-start = (bf16[1,1536,448]{1,2,0:T(8,128)(2,1)S(1)}, bf16[1,1536,448]{1,2,0:T(8,128)(2,1)}, u32[]{:S(2)}) copy-start(bf16[1,1536,448]{1,2,0:T(8,128)(2,1)} %param.8) | copy-start | bytes 4128772
  6.5 71.6 %copy-start.1 = (s32[32]{0:T(128)S(1)}, s32[32]{0:T(128)}, u32[]{:S(2)}) copy-start(s32[32]{0:T(128)} %param.11) | copy-start | bytes 388
  6.5 109.9 %all-gather.5.cloned.1.call-start = ((), (), s32[]{:S(2)}) async-start(), calls=%async_computation.3 | async-start | bytes 7798784 | tf_op jit(solution)/shard_map/all_gather | solution.py:179
  40.3 34.8 %collective-permute-start.3 = (bf16[448,1536]{1,0:T(8,128)(2,1)S(1)}, bf16[448,1536]{1,0:T(8,128)(2,1)}, u32[]{:S(2)}, u32[]{:S(2)}) collective-permute-start(bf16[448,1536]{1,0:T(8,128)(2,1)S(1)} %bitcast.47), channel_id=1, source_target_pairs={{0,480},{32,64},{64,32},{96,128},{128,96},{160,192},{192,160},{224... | collective-permute-start | bytes 4128776 | tf_op jit(solution)/shard_map/ppermute | solution.py:204
  42.2 63.1 %collective-permute-start = (bf16[192,7168]{1,0:T(8,128)(2,1)}, bf16[192,7168]{1,0:T(8,128)(2,1)}, u32[]{:S(2)}, u32[]{:S(2)}) collective-permute-start(bf16[192,7168]{1,0:T(8,128)(2,1)} %bitcast.50), channel_id=1, source_target_pairs={{0,32},{32,0},{1,33},{33,1},{2,34},{34,2},{3,35},{35,3},{4,36},{36... | collective-permute-start | bytes 8257544 | tf_op jit(solution)/shard_map/ppermute | solution.py:173
  44.1 61.2 %collective-permute-start.1 = (bf16[192,7168]{1,0:T(8,128)(2,1)}, bf16[192,7168]{1,0:T(8,128)(2,1)}, u32[]{:S(2)}, u32[]{:S(2)}) collective-permute-start(bf16[192,7168]{1,0:T(8,128)(2,1)} %bitcast.51), channel_id=1, source_target_pairs={{0,1},{1,0},{2,3},{3,2},{4,5},{5,4},{6,7},{7,6},{8,9},{9,8},{10,11... | collective-permute-start | bytes 8257544 | tf_op jit(solution)/shard_map/ppermute | solution.py:199
  46.4 36.9 %collective-permute-start.2 = (bf16[448,1536]{1,0:T(8,128)(2,1)S(1)}, bf16[448,1536]{1,0:T(8,128)(2,1)}, u32[]{:S(2)}, u32[]{:S(2)}) collective-permute-start(bf16[448,1536]{1,0:T(8,128)(2,1)S(1)} %bitcast.48), channel_id=1, source_target_pairs={{0,1},{1,0},{2,3},{3,2},{4,5},{5,4},{6,7},{7,6},{8,9},{9,8},{10,11... | collective-permute-start | bytes 4128776 | tf_op jit(solution)/shard_map/ppermute | solution.py:201
  75.1 8.3 %collective-permute-start.4 = (bf16[448,1536]{1,0:T(8,128)(2,1)}, bf16[448,1536]{1,0:T(8,128)(2,1)}, u32[]{:S(2)}, u32[]{:S(2)}) collective-permute-start(bf16[448,1536]{1,0:T(8,128)(2,1)} %collective-permute-done.3.pair_a), channel_id=1, source_target_pairs={{0,1},{1,0},{2,3},{3,2},{4,5},{5,4},{6,7},{7,6},{8,9},{9,8},{10,11... | collective-permute-start | bytes 4128776 | tf_op jit(solution)/shard_map/ppermute | solution.py:205
  105.3 30.1 %collective-permute-start.5 = (bf16[192,7168]{1,0:T(8,128)(2,1)}, bf16[192,7168]{1,0:T(8,128)(2,1)}, u32[]{:S(2)}, u32[]{:S(2)}) collective-permute-start(bf16[192,7168]{1,0:T(8,128)(2,1)} %collective-permute-done.pair_a), channel_id=1, source_target_pairs={{0,1},{1,0},{2,3},{3,2},{4,5},{5,4},{6,7},{7,6},{8,9},{9,8},{10,11... | collective-permute-start | bytes 8257544 | tf_op jit(solution)/shard_map/ppermute | solution.py:209
  123.4 56.0 %all-to-all-start = ((bf16[8,32,384]{2,1,0:T(8,128)(2,1)}), bf16[8,32,384]{2,1,0:T(8,128)(2,1)S(1)}, u32[]{:S(2)}, u32[]{:S(2)}) async-start(bf16[8,32,384]{2,1,0:T(8,128)(2,1)} %shard_map.64), calls=%async_computation | async-start | bytes 393216 | tf_op jit(solution)/shard_map/all_to_all | solution.py:224
  184.8 16.0 %all-to-all-start.1 = ((bf16[16,32,896]{2,1,0:T(8,128)(2,1)}), bf16[16,32,896]{2,1,0:T(8,128)(2,1)S(1)}, u32[]{:S(2)}, u32[]{:S(2)}) async-start(bf16[16,32,896]{2,1,0:T(8,128)(2,1)} %bitcast.20), calls=%async_computation.1 | async-start | bytes 1835008 | tf_op jit(solution)/shard_map/all_to_all | solution.py:236
  201.8 28.1 %all-to-all-start.2 = ((bf16[16,4,896]{2,1,0:T(4,128)(2,1)}), bf16[16,4,896]{2,1,0:T(4,128)(2,1)S(1)}, u32[]{:S(2)}, u32[]{:S(2)}) async-start(bf16[16,4,896]{2,1,0:T(4,128)(2,1)} %bitcast_select_fusion), calls=%async_computation.2 | async-start | bytes 229376 | tf_op jit(solution)/shard_map/all_to_all | solution.py:244
Sparse Core Ops, SparseCore 0:
  40.4 76.0 all-gather.4

commit v13 on v12

--- a/solution.py
+++ b/solution.py
@@ -44,7 +44,7 @@
 def pick(hidden, hits):
     return jnp.dot(
         jnp.concatenate(hidden, axis=1), hits[...], preferred_element_type=jnp.float32
-    ).astype(jnp.bfloat16)
+    )
 
 
 def rest_kernel(gate_a, up_a, gate_b, up_b, tokens, hits, out, total):
@@ -55,7 +55,7 @@
     def _():
         n = gate_a.shape[0]
         hidden = [unit_values(total[i * n : (i + 1) * n], total[(i + 1) * n : (i + 2) * n]) for i in (0, 2)]
-        picked = pick(hidden, hits)
+        picked = pick(hidden, hits)[n - out.shape[1] :].astype(out.dtype)
         for i in range(out.shape[0]):
             out[i] = picked
 
@@ -63,7 +63,7 @@
 def main_kernel(own_a, pair_a, own_b, pair_b, tokens, hits, out, total):
     start_total(total)
     units = pair_a.shape[0] // 2
-    kept = out.shape[0] - units
+    kept = total.shape[0] // 4 - units
     rows = []
     for own, pair in ((own_a, pair_a), (own_b, pair_b)):
         rows += [own[:kept], own[units : units + kept], pair[...]]
@@ -77,8 +77,8 @@
             middle = base + 2 * kept
             near = unit_values(total[base : base + kept], total[base + kept : middle])
             far = unit_values(total[middle : middle + units], total[middle + units : middle + 2 * units])
-            hidden.append(jnp.concatenate([near, far], axis=0))
-        out[...] = pick(hidden, hits)
+            hidden.append(jnp.concatenate([far, near], axis=0))
+        out[...] = pick(hidden, hits)[: out.shape[0]].astype(out.dtype)
 
 
 def slotted_hidden(kernel, weights, tokens, hits, total_rows, out_shape):
@@ -106,13 +106,13 @@
     members, ends = rest.shape[0], rest.shape[1]
     both = main.shape[1] + ends
     units = both // 2
-    kept = units - ends
     for i in range(members):
-        own = pl.multiple_of(i * both + p_ref[0] * units, ends)
-        other = pl.multiple_of(i * both + (1 - p_ref[0]) * units, ends)
-        hidden[pl.ds(own, kept), :] = main[i, :kept]
-        hidden[pl.ds(own + kept, ends), :] = rest[i]
-        hidden[pl.ds(other, units), :] = main[i, kept:]
+        gathered = main[i].astype(jnp.float32)
+        near = jnp.concatenate([gathered[units:], rest[i].astype(jnp.float32)], axis=0)
+        own = pl.multiple_of(i * both + p_ref[0] * units, 32)
+        other = pl.multiple_of(i * both + (1 - p_ref[0]) * units, 32)
+        hidden[pl.ds(own, units), :] = near.astype(hidden.dtype)
+        hidden[pl.ds(other, units), :] = gathered[:units].astype(hidden.dtype)
     cut = hidden.shape[1] // 2
     low, high = cut // 128 * 128, -(-cut // 128) * 128
     outputs = []
@@ -208,16 +208,16 @@
     )
     w_pair_other = lax.ppermute(w_pair, "c", PAIR)
 
-    ends = units // 3
-    kept = units - ends
+    ends = units // 4
+    block = units // 3
     members = far * 2
-    places = (kept // ends, (units + kept) // ends)
+    places = (units // block - 1, 2 * units // block - 1)
     rest = slotted_hidden(
         rest_kernel,
-        [(w, ends, at) for w in (w_own, w_other) for at in places],
+        [(w, block, at) for w in (w_own, w_other) for at in places],
         every,
         hits,
-        4 * ends,
+        4 * block,
         (members, ends, 2 * class_slots),
     )
     every, rest = lax.optimization_barrier((every, rest))
@@ -227,8 +227,8 @@
         [(w, 2 * units, 0) for w in (w_own, w_pair, w_other, w_pair_other)],
         every,
         hits,
-        4 * (units + kept),
-        (units + kept, 2 * class_slots),
+        4 * (2 * units - ends // 16 * 16),
+        (2 * units - ends, 2 * class_slots),
     )
     main = lax.all_gather(main, RING, axis=0, tiled=False)
     summed = token_sums(p, main, rest, d_own, d_pair, d_other, d_pair_other, combine)

time: 239 us -> 239 us (level)
  transfers between devices with their start and end apart: 10 -> 10, of which waited for: 5 -> 5; matrix products, arithmetic and copies ran while one was open for 3% -> 3% of each run, Pallas kernels for 7% -> 8%
where the time goes in v13:
time: 239 us
  waiting for transfers between devices  80.8 us (34%)
  blocking collectives  66.5 us (28%)
  starting transfers between devices  43.9 us (18%)
  Pallas kernels  23.4 us (10%)
  between operations  13.7 us (6%)
  other arithmetic  5.44 us (2%)
  local copies, waits for them, and re-layouts  4.97 us (2%)
    all_gather x1, blocking collectives, local(): main = lax.all_gather(main, RING, axis=0, tiled=False)  33.8 us
    all_gather x1, blocking collectives, local(): chip_rows = lax.all_gather(tokens, RING + ('c',), axis=0, tiled=False)  32.7 us
    ppermute x1, waiting for transfers between devices, local(): d_pair = lax.ppermute(d_own, LINE, swap)  24.8 us
    ppermute x1, waiting for transfers between devices, local(): w_pair = lax.ppermute(w_own, 'p', PAIR)  21.9 us
    pallas_call x2, Pallas kernels, slotted_hidden(): pl.pallas_call(kernel, grid=(width // depth,), in_specs=[pl.BlockSpec((si...  18.1 us
    all_to_all x1, waiting for transfers between devices, local(): lax.all_to_all(send, ('zh', 'k', 'c'), split_axis=0, concat_axis=0, tiled...  15 us
    all_to_all x1, starting transfers between devices, local(): lax.all_to_all(send, ('zh', 'k', 'c'), split_axis=0, concat_axis=0, tiled...  12.9 us
    all_to_all x1, starting transfers between devices, local(): rest = lax.all_to_all(rest, RING, split_axis=0, concat_axis=0, tiled=True)  11.9 us
  transfers between devices with their start and end apart: 10, of which 5 were waited for; matrix products, arithmetic and copies ran while one was open for 3% of the time, Pallas kernels for 8%

profile of v13, /device:TPU:1, one launch (start us, length us, event | category | flops | bytes accessed | tf_op | source)
XLA Modules:
  0.0 238.7 jit_solution(17444083199427961902)
XLA Ops:
  6.5 32.7 %all-gather.2 = bf16[16,4,7168]{2,1,0:T(4,128)(2,1)S(1)} all-gather(bf16[1,4,7168]{2,1,0:T(4,128)(2,1)} %bitcast.66), channel_id=2, replica_groups=mesh['zh'=4,'k'=2,'p'=2,'x'=4,'y'=4,'c'=2] {'zh','k','c'}, dimensions={0}, use_global_device_ids=true | all-gather | bytes 974848 | tf_op jit(solution)/shard_map/all_gather | solution.py:175
  39.4 0.9 reshape.177
  40.3 1.9 collective-permute-start.3
  42.2 1.9 collective-permute-start
  44.1 2.3 collective-permute-start.1
  46.4 2.0 collective-permute-start.2
  48.5 0.8 select_reduce_fusion.1
  50.3 24.8 %collective-permute-done.3.pair_a = bf16[448,1536]{1,0:T(8,128)(2,1)} collective-permute-done((bf16[448,1536]{1,0:T(8,128)(2,1)S(1)}, bf16[448,1536]{1,0:T(8,128)(2,1)}, u32[]{:S(2)}, u32[]{:S(2)}) %collective-permute-start.3) | collective-permute-done | bytes 1376288 | tf_op jit(solution)/shard_map/ppermute | solution.py:204
  75.1 2.9 %collective-permute-start.4 = (bf16[448,1536]{1,0:T(8,128)(2,1)}, bf16[448,1536]{1,0:T(8,128)(2,1)}, u32[]{:S(2)}, u32[]{:S(2)}) collective-permute-start(bf16[448,1536]{1,0:T(8,128)(2,1)} %collective-permute-done.3.pair_a), channel_id=1, source_target_pairs={{0,1},{1,0},{2,3},{3,2},{4,5},{5,4},{6,7},{7,6},{8,9},{9,8},{10,11... | collective-permute-start | bytes 4128776 | tf_op jit(solution)/shard_map/ppermute | solution.py:205
  78.8 1.3 fusion
  82.0 1.0 add_convert_fusion.hits
  83.4 21.9 %collective-permute-done.pair_a = bf16[192,7168]{1,0:T(8,128)(2,1)} collective-permute-done((bf16[192,7168]{1,0:T(8,128)(2,1)}, bf16[192,7168]{1,0:T(8,128)(2,1)}, u32[]{:S(2)}, u32[]{:S(2)}) %collective-permute-start) | collective-permute-done | bytes 2752544 | tf_op jit(solution)/shard_map/ppermute | solution.py:173
  105.3 3.1 %collective-permute-start.5 = (bf16[192,7168]{1,0:T(8,128)(2,1)}, bf16[192,7168]{1,0:T(8,128)(2,1)}, u32[]{:S(2)}, u32[]{:S(2)}) collective-permute-start(bf16[192,7168]{1,0:T(8,128)(2,1)} %collective-permute-done.pair_a), channel_id=1, source_target_pairs={{0,1},{1,0},{2,3},{3,2},{4,5},{5,4},{6,7},{7,6},{8,9},{9,8},{10,11... | collective-permute-start | bytes 8257544 | tf_op jit(solution)/shard_map/ppermute | solution.py:209
  108.4 8.1 %all-gather.5.cloned.1.call-done.tokens = bf16[512,7168]{1,0:T(8,128)(2,1)} async-done(((bf16[32,7168]{1,0:T(8,128)(2,1)}), bf16[512,7168]{1,0:T(8,128)(2,1)}) %all-gather.5.cloned.1.call-update) | async-done | bytes 7340048 | tf_op jit(solution)/shard_map/all_gather | solution.py:179
  116.5 6.9 %shard_map.64 = bf16[8,24,384]{2,1,0:T(8,128)(2,1)} custom-call(bf16[192,7168]{1,0:T(8,128)(2,1)} %bitcast.52, bf16[192,7168]{1,0:T(8,128)(2,1)} %bitcast.53, bf16[192,7168]{1,0:T(8,128)(2,1)} %collective-permute-done.1.gate_b.up_b.own_b, bf16[192,7168]{1,0:T(8,128)(2,1)} %collective-permute-done.1.gate_b.up_b.own_b, ...), custom_call_target="tpu_custom_call" | custom-call | flops 939524096 | bytes 9175040 | tf_op jit(solution)/shard_map/pallas_call | solution.py:88
  123.4 11.9 %all-to-all-start = ((bf16[8,24,384]{2,1,0:T(8,128)(2,1)}), bf16[8,24,384]{2,1,0:T(8,128)(2,1)S(1)}, u32[]{:S(2)}, u32[]{:S(2)}) async-start(bf16[8,24,384]{2,1,0:T(8,128)(2,1)} %shard_map.64), calls=%async_computation | async-start | bytes 294912 | tf_op jit(solution)/shard_map/all_to_all | solution.py:224
  135.3 11.1 %shard_map.65 = bf16[168,384]{1,0:T(8,128)(2,1)} custom-call(bf16[192,7168]{1,0:T(8,128)(2,1)} %bitcast.54, bf16[192,7168]{1,0:T(8,128)(2,1)} %collective-permute-done.pair_a, bf16[192,7168]{1,0:T(8,128)(2,1)} %collective-permute-done.1.gate_b.up_b.own_b, bf16[192,7168]{1,0:T(8,128)(2,1)} %collective-permute-done.5.pair_b, ...), custom_call_target="tpu_custom_call" | custom-call | flops 5167382528 | bytes 17432576 | tf_op jit(solution)/shard_map/pallas_call | solution.py:88
  146.5 33.8 %all-gather.1 = bf16[1344,384]{1,0:T(8,128)(2,1)S(1)} all-gather(bf16[168,384]{1,0:T(8,128)(2,1)} %shard_map.65), channel_id=3, replica_groups=mesh['zh'=4,'k'=2,'p'=2,'x'=4,'y'=4,'c'=2] {'zh','k'}, dimensions={0}, use_global_device_ids=true | all-gather | bytes 1161216 | tf_op jit(solution)/shard_map/all_gather | solution.py:233
  180.3 5.3 %shard_map.66 = bf16[512,896]{1,0:T(8,128)(2,1)} custom-call(s32[1]{0:T(128)} %bitcast.p_ref, bf16[8,168,384]{2,1,0:T(8,128)(2,1)S(1)} %bitcast.46, bf16[8,24,384]{2,1,0:T(8,128)(2,1)S(1)} %all-to-all-done.rest, bf16[448,1536]{1,0:T(8,128)(2,1)S(1)} %bitcast.49, bf16[448,1536]{1,0:T(8,128)(2,1)} %collective-permute-done.3.pair_a, ...), custom_call_target="tpu_custom_call" | custom-call | flops 2113929216 | bytes 5505024 | tf_op jit(solution)/shard_map/pallas_call | solution.py:138
  185.6 5.0 %all-to-all-start.1 = ((bf16[16,32,896]{2,1,0:T(8,128)(2,1)}), bf16[16,32,896]{2,1,0:T(8,128)(2,1)S(1)}, u32[]{:S(2)}, u32[]{:S(2)}) async-start(bf16[16,32,896]{2,1,0:T(8,128)(2,1)} %bitcast.20), calls=%async_computation.1 | async-start | bytes 1835008 | tf_op jit(solution)/shard_map/all_to_all | solution.py:236
  190.8 10.9 %all-to-all-done.1 = bf16[16,32,896]{2,1,0:T(8,128)(2,1)S(1)} async-done(((bf16[16,32,896]{2,1,0:T(8,128)(2,1)}), bf16[16,32,896]{2,1,0:T(8,128)(2,1)S(1)}, u32[]{:S(2)}, u32[]{:S(2)}) %all-to-all-start.1) | async-done | bytes 917536 | tf_op jit(solution)/shard_map/all_to_all | solution.py:236
  201.8 0.8 bitcast_select_fusion
  202.6 12.9 %all-to-all-start.2 = ((bf16[16,4,896]{2,1,0:T(4,128)(2,1)}), bf16[16,4,896]{2,1,0:T(4,128)(2,1)S(1)}, u32[]{:S(2)}, u32[]{:S(2)}) async-start(bf16[16,4,896]{2,1,0:T(4,128)(2,1)} %bitcast_select_fusion), calls=%async_computation.2 | async-start | bytes 229376 | tf_op jit(solution)/shard_map/all_to_all | solution.py:244
  215.5 15.0 %all-to-all-done.2 = bf16[16,4,896]{2,1,0:T(4,128)(2,1)S(1)} async-done(((bf16[16,4,896]{2,1,0:T(4,128)(2,1)}), bf16[16,4,896]{2,1,0:T(4,128)(2,1)S(1)}, u32[]{:S(2)}, u32[]{:S(2)}) %all-to-all-start.2) | async-done | bytes 114720 | tf_op jit(solution)/shard_map/all_to_all | solution.py:244
  (53 shorter events, 5.7 us)
Async XLA Ops:
  6.5 33.7 %copy-start = (bf16[1,1536,448]{1,2,0:T(8,128)(2,1)S(1)}, bf16[1,1536,448]{1,2,0:T(8,128)(2,1)}, u32[]{:S(2)}) copy-start(bf16[1,1536,448]{1,2,0:T(8,128)(2,1)} %param.8) | copy-start | bytes 4128772
  6.5 71.6 %copy-start.1 = (s32[32]{0:T(128)S(1)}, s32[32]{0:T(128)}, u32[]{:S(2)}) copy-start(s32[32]{0:T(128)} %param.11) | copy-start | bytes 388
  6.5 109.9 %all-gather.5.cloned.1.call-start = ((), (), s32[]{:S(2)}) async-start(), calls=%async_computation.3 | async-start | bytes 7798784 | tf_op jit(solution)/shard_map/all_gather | solution.py:179
  40.3 34.8 %collective-permute-start.3 = (bf16[448,1536]{1,0:T(8,128)(2,1)S(1)}, bf16[448,1536]{1,0:T(8,128)(2,1)}, u32[]{:S(2)}, u32[]{:S(2)}) collective-permute-start(bf16[448,1536]{1,0:T(8,128)(2,1)S(1)} %bitcast.47), channel_id=1, source_target_pairs={{0,480},{32,64},{64,32},{96,128},{128,96},{160,192},{192,160},{224... | collective-permute-start | bytes 4128776 | tf_op jit(solution)/shard_map/ppermute | solution.py:204
  42.2 63.1 %collective-permute-start = (bf16[192,7168]{1,0:T(8,128)(2,1)}, bf16[192,7168]{1,0:T(8,128)(2,1)}, u32[]{:S(2)}, u32[]{:S(2)}) collective-permute-start(bf16[192,7168]{1,0:T(8,128)(2,1)} %bitcast.50), channel_id=1, source_target_pairs={{0,32},{32,0},{1,33},{33,1},{2,34},{34,2},{3,35},{35,3},{4,36},{36... | collective-permute-start | bytes 8257544 | tf_op jit(solution)/shard_map/ppermute | solution.py:173
  44.1 61.2 %collective-permute-start.1 = (bf16[192,7168]{1,0:T(8,128)(2,1)}, bf16[192,7168]{1,0:T(8,128)(2,1)}, u32[]{:S(2)}, u32[]{:S(2)}) collective-permute-start(bf16[192,7168]{1,0:T(8,128)(2,1)} %bitcast.51), channel_id=1, source_target_pairs={{0,1},{1,0},{2,3},{3,2},{4,5},{5,4},{6,7},{7,6},{8,9},{9,8},{10,11... | collective-permute-start | bytes 8257544 | tf_op jit(solution)/shard_map/ppermute | solution.py:199
  46.4 36.9 %collective-permute-start.2 = (bf16[448,1536]{1,0:T(8,128)(2,1)S(1)}, bf16[448,1536]{1,0:T(8,128)(2,1)}, u32[]{:S(2)}, u32[]{:S(2)}) collective-permute-start(bf16[448,1536]{1,0:T(8,128)(2,1)S(1)} %bitcast.48), channel_id=1, source_target_pairs={{0,1},{1,0},{2,3},{3,2},{4,5},{5,4},{6,7},{7,6},{8,9},{9,8},{10,11... | collective-permute-start | bytes 4128776 | tf_op jit(solution)/shard_map/ppermute | solution.py:201
  75.1 8.3 %collective-permute-start.4 = (bf16[448,1536]{1,0:T(8,128)(2,1)}, bf16[448,1536]{1,0:T(8,128)(2,1)}, u32[]{:S(2)}, u32[]{:S(2)}) collective-permute-start(bf16[448,1536]{1,0:T(8,128)(2,1)} %collective-permute-done.3.pair_a), channel_id=1, source_target_pairs={{0,1},{1,0},{2,3},{3,2},{4,5},{5,4},{6,7},{7,6},{8,9},{9,8},{10,11... | collective-permute-start | bytes 4128776 | tf_op jit(solution)/shard_map/ppermute | solution.py:205
  105.3 30.0 %collective-permute-start.5 = (bf16[192,7168]{1,0:T(8,128)(2,1)}, bf16[192,7168]{1,0:T(8,128)(2,1)}, u32[]{:S(2)}, u32[]{:S(2)}) collective-permute-start(bf16[192,7168]{1,0:T(8,128)(2,1)} %collective-permute-done.pair_a), channel_id=1, source_target_pairs={{0,1},{1,0},{2,3},{3,2},{4,5},{5,4},{6,7},{7,6},{8,9},{9,8},{10,11... | collective-permute-start | bytes 8257544 | tf_op jit(solution)/shard_map/ppermute | solution.py:209
  123.4 56.9 %all-to-all-start = ((bf16[8,24,384]{2,1,0:T(8,128)(2,1)}), bf16[8,24,384]{2,1,0:T(8,128)(2,1)S(1)}, u32[]{:S(2)}, u32[]{:S(2)}) async-start(bf16[8,24,384]{2,1,0:T(8,128)(2,1)} %shard_map.64), calls=%async_computation | async-start | bytes 294912 | tf_op jit(solution)/shard_map/all_to_all | solution.py:224
  185.6 16.0 %all-to-all-start.1 = ((bf16[16,32,896]{2,1,0:T(8,128)(2,1)}), bf16[16,32,896]{2,1,0:T(8,128)(2,1)S(1)}, u32[]{:S(2)}, u32[]{:S(2)}) async-start(bf16[16,32,896]{2,1,0:T(8,128)(2,1)} %bitcast.20), calls=%async_computation.1 | async-start | bytes 1835008 | tf_op jit(solution)/shard_map/all_to_all | solution.py:236
  202.6 28.0 %all-to-all-start.2 = ((bf16[16,4,896]{2,1,0:T(4,128)(2,1)}), bf16[16,4,896]{2,1,0:T(4,128)(2,1)S(1)}, u32[]{:S(2)}, u32[]{:S(2)}) async-start(bf16[16,4,896]{2,1,0:T(4,128)(2,1)} %bitcast_select_fusion), calls=%async_computation.2 | async-start | bytes 229376 | tf_op jit(solution)/shard_map/all_to_all | solution.py:244
Sparse Core Ops, SparseCore 0:
  40.4 76.0 all-gather.4

commit v14 on v12

--- a/solution.py
+++ b/solution.py
@@ -93,7 +93,7 @@
         out_specs=whole(out_shape),
         scratch_shapes=[pltpu.VMEM((total_rows, count), jnp.float32)],
         out_shape=jax.ShapeDtypeStruct(out_shape, jnp.bfloat16),
-        compiler_params=pltpu.CompilerParams(vmem_limit_bytes=60 * 2**20),
+        compiler_params=pltpu.CompilerParams(vmem_limit_bytes=40 * 2**20),
         cost_estimate=pl.CostEstimate(
             flops=2 * total_rows * width * count,
             bytes_accessed=2 * width * (total_rows + count),

time: 239 us -> 243 us (1.017)
  local copies, waits for them, and re-layouts: 4.97 us -> 12.1 us
  Pallas kernels: 23.1 us -> 19.2 us
    unnamed x5 -> x13, local copies, waits for them, and re-layouts: 0.17 us -> 7.27 us
    pallas_call x2, Pallas kernels: 17.7 us -> 13.8 us  [slotted_hidden(): pl.pallas_call(kernel, grid=(width // depth,), in_specs=[pl.BlockSpec((si...]
  transfers between devices with their start and end apart: 10 -> 10, of which waited for: 5 -> 5; matrix products, arithmetic and copies ran while one was open for 3% -> 3% of each run, Pallas kernels for 7% -> 6%
where the time goes in v14:
time: 243 us; the launch traced here: 242 us
  waiting for transfers between devices  81.4 us (33%)
  blocking collectives  67 us (28%)
  starting transfers between devices  43.7 us (18%)
  Pallas kernels  19.2 us (8%)
  between operations  13.7 us (6%)
  local copies, waits for them, and re-layouts  12.1 us (5%)
  other arithmetic  5.32 us (2%)
    all_gather x1, blocking collectives, local(): chip_rows = lax.all_gather(tokens, RING + ('c',), axis=0, tiled=False)  34 us
    all_gather x1, blocking collectives, local(): main = lax.all_gather(main, RING, axis=0, tiled=False)  33 us
    ppermute x1, waiting for transfers between devices, local(): d_pair = lax.ppermute(d_own, LINE, swap)  25 us
    ppermute x1, waiting for transfers between devices, local(): w_pair = lax.ppermute(w_own, 'p', PAIR)  21.8 us
    all_to_all x1, waiting for transfers between devices, local(): lax.all_to_all(send, ('zh', 'k', 'c'), split_axis=0, concat_axis=0, tiled...  15.1 us
    pallas_call x2, Pallas kernels, slotted_hidden(): pl.pallas_call(kernel, grid=(width // depth,), in_specs=[pl.BlockSpec((si...  13.8 us
    all_to_all x1, starting transfers between devices, local(): lax.all_to_all(send, ('zh', 'k', 'c'), split_axis=0, concat_axis=0, tiled...  12.3 us
    all_to_all x1, starting transfers between devices, local(): rest = lax.all_to_all(rest, RING, split_axis=0, concat_axis=0, tiled=True)  11.9 us
  transfers between devices with their start and end apart: 10, of which 5 were waited for; matrix products, arithmetic and copies ran while one was open for 3% of the time, Pallas kernels for 6%

profile of v14, /device:TPU:1, one launch (start us, length us, event | category | flops | bytes accessed | tf_op | source)
XLA Modules:
  0.0 242.4 jit_solution(16127443267253345827)
XLA Ops:
  6.5 34.0 %all-gather.2 = bf16[16,4,7168]{2,1,0:T(4,128)(2,1)} all-gather(bf16[1,4,7168]{2,1,0:T(4,128)(2,1)} %bitcast.66), channel_id=2, replica_groups=mesh['zh'=4,'k'=2,'p'=2,'x'=4,'y'=4,'c'=2] {'zh','k','c'}, dimensions={0}, use_global_device_ids=true | all-gather | bytes 974848 | tf_op jit(solution)/shard_map/all_gather | solution.py:175
  40.6 1.2 dynamic-slice_bitcast_fusion
  42.6 1.9 collective-permute-start.3
  44.6 1.9 collective-permute-start
  46.5 2.1 collective-permute-start.1
  48.7 2.2 collective-permute-start.2
  52.7 25.0 %collective-permute-done.3.pair_a = bf16[448,1536]{1,0:T(8,128)(2,1)} collective-permute-done((bf16[448,1536]{1,0:T(8,128)(2,1)}, bf16[448,1536]{1,0:T(8,128)(2,1)}, u32[]{:S(2)}, u32[]{:S(2)}) %collective-permute-start.3) | collective-permute-done | bytes 1376288 | tf_op jit(solution)/shard_map/ppermute | solution.py:204
  77.7 2.9 %collective-permute-start.4 = (bf16[448,1536]{1,0:T(8,128)(2,1)}, bf16[448,1536]{1,0:T(8,128)(2,1)}, u32[]{:S(2)}, u32[]{:S(2)}) collective-permute-start(bf16[448,1536]{1,0:T(8,128)(2,1)} %collective-permute-done.3.pair_a), channel_id=1, source_target_pairs={{0,1},{1,0},{2,3},{3,2},{4,5},{5,4},{6,7},{7,6},{8,9},{9,8},{10,11... | collective-permute-start | bytes 4128776 | tf_op jit(solution)/shard_map/ppermute | solution.py:205
  81.4 1.4 fusion
  84.8 1.1 add_convert_fusion.1.combine
  85.9 21.8 %collective-permute-done.pair_a = bf16[192,7168]{1,0:T(8,128)(2,1)} collective-permute-done((bf16[192,7168]{1,0:T(8,128)(2,1)S(1)}, bf16[192,7168]{1,0:T(8,128)(2,1)}, u32[]{:S(2)}, u32[]{:S(2)}) %collective-permute-start) | collective-permute-done | bytes 2752544 | tf_op jit(solution)/shard_map/ppermute | solution.py:173
  107.6 2.9 %collective-permute-start.5 = (bf16[192,7168]{1,0:T(8,128)(2,1)}, bf16[192,7168]{1,0:T(8,128)(2,1)}, u32[]{:S(2)}, u32[]{:S(2)}) collective-permute-start(bf16[192,7168]{1,0:T(8,128)(2,1)} %collective-permute-done.pair_a), channel_id=1, source_target_pairs={{0,1},{1,0},{2,3},{3,2},{4,5},{5,4},{6,7},{7,6},{8,9},{9,8},{10,11... | collective-permute-start | bytes 8257544 | tf_op jit(solution)/shard_map/ppermute | solution.py:209
  110.6 8.6 %all-gather.5.cloned.1.call-done.tokens = bf16[512,7168]{1,0:T(8,128)(2,1)} async-done(((bf16[32,7168]{1,0:T(8,128)(2,1)}), bf16[512,7168]{1,0:T(8,128)(2,1)}) %all-gather.5.cloned.1.call-update) | async-done | bytes 7340048 | tf_op jit(solution)/shard_map/all_gather | solution.py:179
  119.2 3.1 %copy-done = bf16[512,7168]{1,0:T(8,128)(2,1)S(1)} copy-done((bf16[512,7168]{1,0:T(8,128)(2,1)S(1)}, bf16[512,7168]{1,0:T(8,128)(2,1)}, u32[]{:S(2)}) %copy-start) | copy-done | bytes 7340056
  122.2 4.6 %shard_map.64 = bf16[8,32,384]{2,1,0:T(8,128)(2,1)S(1)} custom-call(bf16[192,7168]{1,0:T(8,128)(2,1)S(1)} %bitcast.48, bf16[192,7168]{1,0:T(8,128)(2,1)S(1)} %bitcast.49, bf16[192,7168]{1,0:T(8,128)(2,1)} %collective-permute-done.1.gate_b.up_b.own_b, bf16[192,7168]{1,0:T(8,128)(2,1)} %collective-permute-done.1.gate_b.up_b.own_b, ...), custom_call_target="tpu_custom_call" | custom-call | flops 939524096 | bytes 9175040 | tf_op jit(solution)/shard_map/pallas_call | solution.py:88
  127.5 11.9 %all-to-all-start = ((bf16[8,32,384]{2,1,0:T(8,128)(2,1)}), bf16[8,32,384]{2,1,0:T(8,128)(2,1)}, u32[]{:S(2)}, u32[]{:S(2)}) async-start(bf16[8,32,384]{2,1,0:T(8,128)(2,1)} %copy-done.4), calls=%async_computation | async-start | bytes 393216 | tf_op jit(solution)/shard_map/all_to_all | solution.py:224
  139.4 9.2 %shard_map.65 = bf16[160,384]{1,0:T(8,128)(2,1)S(1)} custom-call(bf16[192,7168]{1,0:T(8,128)(2,1)S(1)} %bitcast.50, bf16[192,7168]{1,0:T(8,128)(2,1)} %collective-permute-done.pair_a, bf16[192,7168]{1,0:T(8,128)(2,1)} %collective-permute-done.1.gate_b.up_b.own_b, bf16[192,7168]{1,0:T(8,128)(2,1)} %collective-permute-done.5.pair_b, ...), custom_call_target="tpu_custom_call" | custom-call | flops 4697620480 | bytes 16515072 | tf_op jit(solution)/shard_map/pallas_call | solution.py:88
  148.6 33.0 %all-gather.1 = bf16[1280,384]{1,0:T(8,128)(2,1)S(1)} all-gather(bf16[160,384]{1,0:T(8,128)(2,1)S(1)} %shard_map.65), channel_id=3, replica_groups=mesh['zh'=4,'k'=2,'p'=2,'x'=4,'y'=4,'c'=2] {'zh','k'}, dimensions={0}, use_global_device_ids=true | all-gather | bytes 1105920 | tf_op jit(solution)/shard_map/all_gather | solution.py:233
  182.6 1.3 copy-done.3
  184.0 5.4 %shard_map.66 = bf16[512,896]{1,0:T(8,128)(2,1)} custom-call(s32[1]{0:T(128)} %bitcast.p_ref, bf16[8,160,384]{2,1,0:T(8,128)(2,1)S(1)} %bitcast.51, bf16[8,32,384]{2,1,0:T(8,128)(2,1)} %all-to-all-done.rest, bf16[448,1536]{1,0:T(8,128)(2,1)S(1)} %bitcast.54, bf16[448,1536]{1,0:T(8,128)(2,1)} %collective-permute-done.3.pair_a, ...), custom_call_target="tpu_custom_call" | custom-call | flops 2113929216 | bytes 5505024 | tf_op jit(solution)/shard_map/pallas_call | solution.py:138
  189.4 5.5 %all-to-all-start.1 = ((bf16[16,32,896]{2,1,0:T(8,128)(2,1)}), bf16[16,32,896]{2,1,0:T(8,128)(2,1)S(1)}, u32[]{:S(2)}, u32[]{:S(2)}) async-start(bf16[16,32,896]{2,1,0:T(8,128)(2,1)} %bitcast.20), calls=%async_computation.1 | async-start | bytes 1835008 | tf_op jit(solution)/shard_map/all_to_all | solution.py:236
  195.0 11.0 %all-to-all-done.1 = bf16[16,32,896]{2,1,0:T(8,128)(2,1)S(1)} async-done(((bf16[16,32,896]{2,1,0:T(8,128)(2,1)}), bf16[16,32,896]{2,1,0:T(8,128)(2,1)S(1)}, u32[]{:S(2)}, u32[]{:S(2)}) %all-to-all-start.1) | async-done | bytes 917536 | tf_op jit(solution)/shard_map/all_to_all | solution.py:236
  206.9 12.3 %all-to-all-start.2 = ((bf16[16,4,896]{2,1,0:T(4,128)(2,1)}), bf16[16,4,896]{2,1,0:T(4,128)(2,1)S(1)}, u32[]{:S(2)}, u32[]{:S(2)}) async-start(bf16[16,4,896]{2,1,0:T(4,128)(2,1)} %bitcast_select_fusion), calls=%async_computation.2 | async-start | bytes 229376 | tf_op jit(solution)/shard_map/all_to_all | solution.py:244
  219.2 15.1 %all-to-all-done.2 = bf16[16,4,896]{2,1,0:T(4,128)(2,1)S(1)} async-done(((bf16[16,4,896]{2,1,0:T(4,128)(2,1)}), bf16[16,4,896]{2,1,0:T(4,128)(2,1)S(1)}, u32[]{:S(2)}, u32[]{:S(2)}) %all-to-all-start.2) | async-done | bytes 114720 | tf_op jit(solution)/shard_map/all_to_all | solution.py:244
  (61 shorter events, 9.4 us)
Async XLA Ops:
  6.5 38.0 %copy-start.1 = (bf16[1,2,96,7168]{3,2,1,0:T(8,128)(2,1)S(1)}, bf16[1,2,96,7168]{3,2,1,0:T(8,128)(2,1)}, u32[]{:S(2)}) copy-start(bf16[1,2,96,7168]{3,2,1,0:T(8,128)(2,1)} %param.7) | copy-start | bytes 8257540
  6.5 74.2 %copy-start.5 = (s32[32]{0:T(128)S(1)}, s32[32]{0:T(128)}, u32[]{:S(2)}) copy-start(s32[32]{0:T(128)} %param.11) | copy-start | bytes 388
  6.5 112.6 %all-gather.5.cloned.1.call-start = ((), (), s32[]{:S(2)}) async-start(), calls=%async_computation.3 | async-start | bytes 7798784 | tf_op jit(solution)/shard_map/all_gather | solution.py:179
  42.6 35.1 %collective-permute-start.3 = (bf16[448,1536]{1,0:T(8,128)(2,1)}, bf16[448,1536]{1,0:T(8,128)(2,1)}, u32[]{:S(2)}, u32[]{:S(2)}) collective-permute-start(bf16[448,1536]{1,0:T(8,128)(2,1)} %bitcast.52), channel_id=1, source_target_pairs={{0,480},{32,64},{64,32},{96,128},{128,96},{160,192},{192,160},{224... | collective-permute-start | bytes 4128776 | tf_op jit(solution)/shard_map/ppermute | solution.py:204
  44.6 63.0 %collective-permute-start = (bf16[192,7168]{1,0:T(8,128)(2,1)S(1)}, bf16[192,7168]{1,0:T(8,128)(2,1)}, u32[]{:S(2)}, u32[]{:S(2)}) collective-permute-start(bf16[192,7168]{1,0:T(8,128)(2,1)S(1)} %bitcast.46), channel_id=1, source_target_pairs={{0,32},{32,0},{1,33},{33,1},{2,34},{34,2},{3,35},{35,3},{4,36},{36... | collective-permute-start | bytes 8257544 | tf_op jit(solution)/shard_map/ppermute | solution.py:173
  46.5 61.1 %collective-permute-start.1 = (bf16[192,7168]{1,0:T(8,128)(2,1)S(1)}, bf16[192,7168]{1,0:T(8,128)(2,1)}, u32[]{:S(2)}, u32[]{:S(2)}) collective-permute-start(bf16[192,7168]{1,0:T(8,128)(2,1)S(1)} %bitcast.47), channel_id=1, source_target_pairs={{0,1},{1,0},{2,3},{3,2},{4,5},{5,4},{6,7},{7,6},{8,9},{9,8},{10,11... | collective-permute-start | bytes 8257544 | tf_op jit(solution)/shard_map/ppermute | solution.py:199
  48.7 37.2 %collective-permute-start.2 = (bf16[448,1536]{1,0:T(8,128)(2,1)}, bf16[448,1536]{1,0:T(8,128)(2,1)}, u32[]{:S(2)}, u32[]{:S(2)}) collective-permute-start(bf16[448,1536]{1,0:T(8,128)(2,1)} %bitcast.53), channel_id=1, source_target_pairs={{0,1},{1,0},{2,3},{3,2},{4,5},{5,4},{6,7},{7,6},{8,9},{9,8},{10,11... | collective-permute-start | bytes 4128776 | tf_op jit(solution)/shard_map/ppermute | solution.py:201
  77.7 8.2 %collective-permute-start.4 = (bf16[448,1536]{1,0:T(8,128)(2,1)}, bf16[448,1536]{1,0:T(8,128)(2,1)}, u32[]{:S(2)}, u32[]{:S(2)}) collective-permute-start(bf16[448,1536]{1,0:T(8,128)(2,1)} %collective-permute-done.3.pair_a), channel_id=1, source_target_pairs={{0,1},{1,0},{2,3},{3,2},{4,5},{5,4},{6,7},{7,6},{8,9},{9,8},{10,11... | collective-permute-start | bytes 4128776 | tf_op jit(solution)/shard_map/ppermute | solution.py:205
  107.6 31.8 %collective-permute-start.5 = (bf16[192,7168]{1,0:T(8,128)(2,1)}, bf16[192,7168]{1,0:T(8,128)(2,1)}, u32[]{:S(2)}, u32[]{:S(2)}) collective-permute-start(bf16[192,7168]{1,0:T(8,128)(2,1)} %collective-permute-done.pair_a), channel_id=1, source_target_pairs={{0,1},{1,0},{2,3},{3,2},{4,5},{5,4},{6,7},{7,6},{8,9},{9,8},{10,11... | collective-permute-start | bytes 8257544 | tf_op jit(solution)/shard_map/ppermute | solution.py:209
  119.2 3.1 %copy-start = (bf16[512,7168]{1,0:T(8,128)(2,1)S(1)}, bf16[512,7168]{1,0:T(8,128)(2,1)}, u32[]{:S(2)}) copy-start(bf16[512,7168]{1,0:T(8,128)(2,1)} %all-gather.5.cloned.1.call-done.tokens) | copy-start | bytes 22020100
  126.8 0.7 copy-start.4
  127.5 54.1 %all-to-all-start = ((bf16[8,32,384]{2,1,0:T(8,128)(2,1)}), bf16[8,32,384]{2,1,0:T(8,128)(2,1)}, u32[]{:S(2)}, u32[]{:S(2)}) async-start(bf16[8,32,384]{2,1,0:T(8,128)(2,1)} %copy-done.4), calls=%async_computation | async-start | bytes 393216 | tf_op jit(solution)/shard_map/all_to_all | solution.py:224
  181.6 1.0 copy-start.2
  182.6 1.3 copy-start.3
  189.4 16.6 %all-to-all-start.1 = ((bf16[16,32,896]{2,1,0:T(8,128)(2,1)}), bf16[16,32,896]{2,1,0:T(8,128)(2,1)S(1)}, u32[]{:S(2)}, u32[]{:S(2)}) async-start(bf16[16,32,896]{2,1,0:T(8,128)(2,1)} %bitcast.20), calls=%async_computation.1 | async-start | bytes 1835008 | tf_op jit(solution)/shard_map/all_to_all | solution.py:236
  206.9 27.4 %all-to-all-start.2 = ((bf16[16,4,896]{2,1,0:T(4,128)(2,1)}), bf16[16,4,896]{2,1,0:T(4,128)(2,1)S(1)}, u32[]{:S(2)}, u32[]{:S(2)}) async-start(bf16[16,4,896]{2,1,0:T(4,128)(2,1)} %bitcast_select_fusion), calls=%async_computation.2 | async-start | bytes 229376 | tf_op jit(solution)/shard_map/all_to_all | solution.py:244
Sparse Core Ops, SparseCore 0:
  42.8 76.3 all-gather.4
